TPU v7x, 1024 devices: a whole 8x8x8 slice. The times are simulated.
1024 devices in a mesh: grp: 16 (over x, core), mem: 64 (over y, z).
Axes of the slice: x: 8, y: 8, z: 8, core: 2. Of those that a mesh axis runs over, the one named last changes fastest.
Arguments:
- embeddings: bfloat16 [524288, 1024], P(('grp', 'mem')), may hold values from -6 to 6
- assignment: int32 [524288], P(('grp', 'mem')), may hold values from 0 to 131071, as said below
- second_choice: int32 [524288], P(('grp', 'mem')), may hold values from 0 to 131071, as said below
- list_slot: int32 [131072], replicated, may hold values from 0 to 131071, as said below
- old_centroids: bfloat16 [131072, 1024], P(('grp', 'mem')), may hold values from -6 to 6
Outputs:
- new_centroids: bfloat16 [131072, 1024], P(('grp', 'mem'))
- margins: float32 [524288], P(('grp', 'mem'))
Inputs may be any that keep to these rules, and one draw needn't show every extreme that they name: Each list is stored at slot list_slot[list]; the slots are a permutation of all lists. Slot s lies on device s // 128 in the order grp then mem. `assignment`: of the 512 vectors of one device, at most 10 have a list whose slot lies on one index of mem (any grp); every device has one index of mem that receives exactly 10. `second_choice`: A vector's second-choice list differs from its list, and its slot lies on the same index of mem as the slot of its list.
All inputs are finite; a program needn't handle non-finite values.
Results may differ from a plain program's by a relative error of at most 0.015.
Values may be sent and summed in bfloat16 or wider, within the bound.
No kernel may reach another device: no remote copies, remote signals or barrier semaphores. Data moves between devices by JAX's collectives and lax.ppermute only.
A program may use at most 32 MiB of HBM per device.

v0:
```python
import jax
import jax.numpy as jnp
from jax import lax
from jax.sharding import PartitionSpec as P


def on_device(embeddings, assignment, second_choice, list_slot, old_centroids):
    rows_dev, width = embeddings.shape
    lists_dev = old_centroids.shape[0]
    members = lax.axis_size("mem")
    groups = lax.axis_size("grp")
    capacity = rows_dev // members + 2
    span = groups * lists_dev
    slot_first = list_slot[assignment]
    slot_second = list_slot[second_choice]
    owner = slot_first // lists_dev % members

    def range_index(slot):
        return slot // (lists_dev * members) * lists_dev + slot % lists_dev

    owner_table = (owner[:, None] == jnp.arange(members, dtype=jnp.int32)[None, :]).astype(
        jnp.int32
    )
    earlier = jnp.cumsum(owner_table, axis=0) - owner_table
    rank = jnp.sum(earlier * owner_table, axis=1)
    place = owner * capacity + rank
    outgoing = jnp.zeros((members * capacity, width), jnp.bfloat16).at[place].set(embeddings)
    first_ids = (
        jnp.full((members * capacity,), -1, jnp.int32).at[place].set(range_index(slot_first))
    )
    second_ids = (
        jnp.full((members * capacity,), -1, jnp.int32).at[place].set(range_index(slot_second))
    )
    arrived, arrived_first, arrived_second = (
        lax.all_to_all(
            outgoing.reshape(members, capacity, width),
            "mem",
            split_axis=0,
            concat_axis=0,
            tiled=True,
        ),
        lax.all_to_all(
            first_ids.reshape(members, capacity), "mem", split_axis=0, concat_axis=0, tiled=True
        ),
        lax.all_to_all(
            second_ids.reshape(members, capacity), "mem", split_axis=0, concat_axis=0, tiled=True
        ),
    )
    received = arrived.reshape(members * capacity, width)
    flat_first = arrived_first.reshape(-1)
    flat_second = arrived_second.reshape(-1)
    targets = jnp.arange(lists_dev * lax.axis_size("grp"), dtype=jnp.int32)
    table = (targets[:, None] == flat_first[None, :]).astype(jnp.bfloat16)
    summed = lax.psum_scatter(
        jnp.dot(table, received, preferred_element_type=jnp.float32).astype(jnp.bfloat16),
        "grp",
        scatter_dimension=0,
        tiled=True,
    ).astype(jnp.float32)
    hits = jnp.sum(
        (jnp.arange(span, dtype=jnp.int32)[:, None] == flat_first[None, :]).astype(jnp.float32),
        axis=1,
    )
    counts = lax.psum_scatter(hits, "grp", scatter_dimension=0, tiled=True)
    fresh = ((summed + old_centroids.astype(jnp.float32)) / (counts + 1.0)[:, None]).astype(
        jnp.bfloat16
    )

    def take_rows(piece, start, labels):
        offset = labels - start
        inside = (offset >= 0) & (offset < piece.shape[0])
        safe = jnp.clip(offset, 0, piece.shape[0] - 1)
        rows = jnp.take(piece, safe, axis=0).astype(jnp.float32)
        return jnp.where(inside[:, None], rows, 0.0)

    piece = lax.all_gather(fresh, "grp", axis=0, tiled=True)
    start = jnp.int32(0)
    near = take_rows(piece, start, flat_first)
    other = take_rows(piece, start, flat_second)
    values = received.astype(jnp.float32)
    scored = (
        jnp.sum((values - other) ** 2, axis=1) - jnp.sum((values - near) ** 2, axis=1)
    ) / width
    returned = lax.all_to_all(
        scored.reshape(members, capacity), "mem", split_axis=0, concat_axis=0, tiled=True
    )
    margins = returned.reshape(-1)[place]
    return (fresh, margins)


def solution(mesh):
    placed = (
        P(("grp", "mem"), None),
        P(("grp", "mem")),
        P(("grp", "mem")),
        P(),
        P(("grp", "mem"), None),
    )
    return jax.shard_map(
        on_device,
        mesh=mesh,
        in_specs=placed,
        out_specs=(P(("grp", "mem"), None), P(("grp", "mem"))),
        check_vma=False,
    )
```

profile of v0, /device:TPU:1, one launch (start us, length us, event | category | flops | bytes accessed | tf_op | source)
XLA Modules:
  0.0 289.5 jit_solution(424778015720114780)
XLA Ops:
  8.2 3.1 %gather_fusion = s32[512]{0:T(512)S(1)} fusion(s32[131072]{0:T(1024)S(1)} %copy-done, s32[1024]{0:T(1024)S(1)} %pad_clamp_fusion.4), kind=kCustom, calls=%fused_computation.2 | custom fusion | bytes 6144 | tf_op jit(solution)/shard_map/gather | solution.py:14
  13.1 2.4 scatter_custom_fusion
  16.3 24.0 %all-to-all-start = ((s32[64,1,10]{2,1,0:T(1,128)}), s32[64,1,10]{2,1,0:T(1,128)S(1)}, u32[]{:S(2)}, u32[]{:S(2)}) async-start(s32[64,1,10]{2,1,0:T(1,128)} %bitcast.5), calls=%async_computation | async-start | bytes 65536 | tf_op jit(solution)/shard_map/all_to_all | solution.py:42
  40.2 3.6 %scatter_custom_fusion.1 = bf16[640,1024]{1,0:T(8,128)(2,1)S(1)} fusion(s32[512]{0:T(512)S(1)} %bitcast.52, bf16[512,1024]{1,0:T(8,128)(2,1)} %param.7, bf16[]{:T(256)} %constant.94.clone.1), kind=kCustom, calls=%fused_computation.19 | custom fusion | bytes 1311232 | tf_op jit(solution)/shard_map/scatter | solution.py:27
  43.8 1.6 reshape.213
  45.4 5.6 %all-to-all-done = s32[64,1,10]{2,1,0:T(1,128)S(1)} async-done(((s32[64,1,10]{2,1,0:T(1,128)}), s32[64,1,10]{2,1,0:T(1,128)S(1)}, u32[]{:S(2)}, u32[]{:S(2)}) %all-to-all-start) | async-done | bytes 2592 | tf_op jit(solution)/shard_map/all_to_all | solution.py:42
  51.0 6.5 %all-to-all-start.1 = ((bf16[64,10,1024]{2,1,0:T(8,128)(2,1)}), bf16[64,10,1024]{2,1,0:T(8,128)(2,1)S(1)}, u32[]{:S(2)}, u32[]{:S(2)}) async-start(bf16[64,10,1024]{2,1,0:T(8,128)(2,1)} %reshape.213), calls=%async_computation.1 | async-start | bytes 4194304 | tf_op jit(solution)/shard_map/all_to_all | solution.py:35
  59.0 47.0 %all-to-all-done.1 = bf16[64,10,1024]{2,1,0:T(8,128)(2,1)S(1)} async-done(((bf16[64,10,1024]{2,1,0:T(8,128)(2,1)}), bf16[64,10,1024]{2,1,0:T(8,128)(2,1)S(1)}, u32[]{:S(2)}, u32[]{:S(2)}) %all-to-all-start.1) | async-done | bytes 1310752 | tf_op jit(solution)/shard_map/all_to_all | solution.py:35
  106.0 1.3 reshape.214
  107.3 6.2 %fusion.1 = bf16[2048,1024]{1,0:T(8,128)(2,1)} fusion(bf16[640,1024]{1,0:T(8,128)(2,1)} %reshape.214, s32[640]{0:T(1024)S(1)} %eq.54), kind=kOutput, calls=%fused_computation.11 | convolution fusion | flops 2687762432 | bytes 5507584 | tf_op jit(solution)/shard_map/dot_general | solution.py:55
  113.6 1.3 dynamic-slice
  116.1 27.1 %all-reduce = f32[2048]{0:T(1024)S(1)} all-reduce(f32[2048]{0:T(1024)S(1)} %convert_reduce_fusion), channel_id=3, replica_groups=mesh['grp'=16,'mem'=64] {'grp'}, use_global_device_ids=true, to_apply=%region_7.8.clone | all-reduce | flops 2048 | bytes 16384
  143.3 41.1 %reduce-scatter.2.cloned.1.call-done = bf16[128,1024]{1,0:T(8,128)(2,1)} async-done(((bf16[2048,1024]{1,0:T(8,128)(2,1)}), bf16[128,1024]{1,0:T(8,128)(2,1)}) %reduce-scatter.2.cloned.1.call-update) | async-done | bytes 262160 | tf_op jit(solution)/shard_map/reduce_scatter | solution.py:54
  184.4 1.8 divide_convert_fusion
  186.2 3.1 %gather_fusion.1 = s32[512]{0:T(512)S(1)} fusion(s32[131072]{0:T(1024)S(1)} %copy-done, s32[1024]{0:T(1024)S(1)} %pad_clamp_fusion.3), kind=kCustom, calls=%fused_computation.3 | custom fusion | bytes 6144 | tf_op jit(solution)/shard_map/gather | solution.py:15
  189.4 2.4 scatter_custom_fusion.2
  192.0 22.0 %all_to_all.29 = s32[64,1,10]{2,1,0:T(1,128)S(1)} all-to-all(s32[64,1,10]{2,1,0:T(1,128)S(1)} %bitcast.48), channel_id=1, replica_groups=mesh['grp'=16,'mem'=64] {'mem'}, dimensions={0} | all-to-all | bytes 5120 | tf_op jit(solution)/shard_map/all_to_all | solution.py:45
  214.5 21.2 %all-gather.2.cloned.1.call-done = bf16[2048,1024]{1,0:T(8,128)(2,1)} async-done(((bf16[128,1024]{1,0:T(8,128)(2,1)}), bf16[2048,1024]{1,0:T(8,128)(2,1)}) %all-gather.2.cloned.1.call-update) | async-done | bytes 4194320 | tf_op jit(solution)/shard_map/all_gather | solution.py:76
  235.7 6.6 %gather_fusion.4 = bf16[640,1024]{1,0:T(8,128)(2,1)S(1)} fusion(bf16[2048,1024]{1,0:T(8,128)(2,1)} %all-gather.2.cloned.1.call-done, s32[1024]{0:T(1024)S(1)} %pad_clamp_fusion.1), kind=kCustom, calls=%fused_computation.1.clone | custom fusion | bytes 2624000 | tf_op jit(solution)/shard_map/jit(_take)/gather | solution.py:73
  242.3 7.3 %gather_fusion.3 = bf16[640,1024]{1,0:T(8,128)(2,1)} fusion(bf16[2048,1024]{1,0:T(8,128)(2,1)} %all-gather.2.cloned.1.call-done, s32[1024]{0:T(1024)S(1)} %pad_clamp_fusion.2), kind=kCustom, calls=%fused_computation.clone | custom fusion | bytes 2624000 | tf_op jit(solution)/shard_map/jit(_take)/gather | solution.py:73
  249.6 3.1 %fusion.5 = (f32[640]{0:T(1024)S(1)}, f32[640]{0:T(1024)S(1)}) fusion(bf16[640,1024]{1,0:T(8,128)(2,1)S(1)} %copy-done.1, bf16[640,1024]{1,0:T(8,128)(2,1)S(1)} %gather_fusion.4, pred[640]{0:T(1024)(128)(4,1)S(1)} %get-tuple-element.6, pred[640]{0:T(1024)(128)(4,1)S(1)} %get-tuple-element.5, bf16[640,1024]{1,0:T(8,128)(2,1)} %gather_fusion.3, ...), kind=kLoop, calls=%fused_computation.17 | loop fusion | flops 8518400 | bytes 3939840 | tf_op jit(solution)/shard_map/reduce_sum | solution.py:82
  253.4 13.6 %all-to-all-start.3 = ((f32[64,1,10]{2,1,0:T(1,128)}), f32[64,1,10]{2,1,0:T(1,128)S(1)}, u32[]{:S(2)}, u32[]{:S(2)}) async-start(f32[64,1,10]{2,1,0:T(1,128)} %bitcast.7), calls=%async_computation.4 | async-start | bytes 65536 | tf_op jit(solution)/shard_map/all_to_all | solution.py:84
  267.0 10.8 %all-to-all-done.3 = f32[64,1,10]{2,1,0:T(1,128)S(1)} async-done(((f32[64,1,10]{2,1,0:T(1,128)}), f32[64,1,10]{2,1,0:T(1,128)S(1)}, u32[]{:S(2)}, u32[]{:S(2)}) %all-to-all-start.3) | async-done | bytes 2592 | tf_op jit(solution)/shard_map/all_to_all | solution.py:84
  279.3 3.4 %gather_fusion.2 = f32[512]{0:T(512)} fusion(f32[640]{0:T(1024)S(1)} %reshape.215, s32[1024]{0:T(1024)S(1)} %pad_clamp_fusion), kind=kCustom, calls=%fused_computation.4 | custom fusion | bytes 6144 | tf_op jit(solution)/shard_map/gather | solution.py:87
  (49 shorter events, 8.5 us)
Async XLA Ops:
  7.2 1.1 copy-start
  16.3 34.7 %all-to-all-start = ((s32[64,1,10]{2,1,0:T(1,128)}), s32[64,1,10]{2,1,0:T(1,128)S(1)}, u32[]{:S(2)}, u32[]{:S(2)}) async-start(s32[64,1,10]{2,1,0:T(1,128)} %bitcast.5), calls=%async_computation | async-start | bytes 65536 | tf_op jit(solution)/shard_map/all_to_all | solution.py:42
  51.0 55.0 %all-to-all-start.1 = ((bf16[64,10,1024]{2,1,0:T(8,128)(2,1)}), bf16[64,10,1024]{2,1,0:T(8,128)(2,1)S(1)}, u32[]{:S(2)}, u32[]{:S(2)}) async-start(bf16[64,10,1024]{2,1,0:T(8,128)(2,1)} %reshape.213), calls=%async_computation.1 | async-start | bytes 4194304 | tf_op jit(solution)/shard_map/all_to_all | solution.py:35
  57.6 126.8 %reduce-scatter.2.cloned.1.call-start = ((), (), s32[]{:S(2)}) async-start(), calls=%async_computation.5 | async-start | bytes 4456448 | tf_op jit(solution)/shard_map/reduce_scatter | solution.py:54
  113.5 70.9 %copy-start.2 = (bf16[128,1024]{1,0:T(8,128)(2,1)S(1)}, bf16[128,1024]{1,0:T(8,128)(2,1)}, u32[]{:S(2)}) copy-start(bf16[128,1024]{1,0:T(8,128)(2,1)} %param.11) | copy-start | bytes 786436
  113.5 72.7 %copy-start.3 = (s32[512]{0:T(512)S(1)}, s32[512]{0:T(512)}, u32[]{:S(2)}) copy-start(s32[512]{0:T(512)} %param.9) | copy-start | bytes 6148
  113.5 122.2 %all-gather.2.cloned.1.call-start = ((), (), s32[]{:S(2)}) async-start(), calls=%async_computation.6 | async-start | bytes 4456448 | tf_op jit(solution)/shard_map/all_gather | solution.py:76
  242.3 7.3 %copy-start.1 = (bf16[640,1024]{1,0:T(8,128)(2,1)S(1)}, bf16[640,1024]{1,0:T(8,128)(2,1)}, u32[]{:S(2)}) copy-start(bf16[640,1024]{1,0:T(8,128)(2,1)} %reshape.214) | copy-start | bytes 3932164
  253.4 24.4 %all-to-all-start.3 = ((f32[64,1,10]{2,1,0:T(1,128)}), f32[64,1,10]{2,1,0:T(1,128)S(1)}, u32[]{:S(2)}, u32[]{:S(2)}) async-start(f32[64,1,10]{2,1,0:T(1,128)} %bitcast.7), calls=%async_computation.4 | async-start | bytes 65536 | tf_op jit(solution)/shard_map/all_to_all | solution.py:84
Sparse Core Ops, SparseCore 0:
  113.6 70.7 reduce-scatter.1
  187.7 47.9 all-gather.1
where the time goes:
time: 290 us
  waiting for transfers between devices  126 us (43%)
  blocking collectives  49.1 us (17%)
  starting transfers between devices  44.2 us (15%)
  local copies, waits for them, and re-layouts  40 us (14%)
  between operations  15 us (5%)
  other arithmetic  9.47 us (3%)
  matrix products  6.21 us (2%)
    all_to_all x1, waiting for transfers between devices, on_device(): lax.all_to_all(outgoing.reshape(members, capacity, width), 'mem', split_a...  47 us
    reduce_scatter x1, waiting for transfers between devices, on_device(): lax.psum_scatter(jnp.dot(table, received, preferred_element_type=jnp.floa...  41.1 us
    unnamed x1, blocking collectives  27.1 us
    all_to_all x1, starting transfers between devices, on_device(): lax.all_to_all(first_ids.reshape(members, capacity), 'mem', split_axis=0,...  24 us
    all_to_all x1, blocking collectives, on_device(): lax.all_to_all(second_ids.reshape(members, capacity), 'mem', split_axis=0...  22 us
    all_gather x1, waiting for transfers between devices, on_device(): piece = lax.all_gather(fresh, 'grp', axis=0, tiled=True)  21.2 us
    gather x2, local copies, waits for them, and re-layouts, take_rows(): rows = jnp.take(piece, safe, axis=0).astype(jnp.float32)  13.9 us
    all_to_all x1, starting transfers between devices, on_device(): lax.all_to_all(scored.reshape(members, capacity), 'mem', split_axis=0, co...  13.6 us
  transfers between devices with their start and end apart: 5, of which 5 were waited for; matrix products, arithmetic and copies ran while one was open for 5% of the time, Pallas kernels for 0%

commit v1 on v0

v1 whole, which is shorter than its diff:
```python
import functools

import jax
import jax.numpy as jnp
from jax import lax
from jax.experimental import pallas as pl
from jax.experimental.pallas import tpu as pltpu
from jax.sharding import Mesh
from jax.sharding import PartitionSpec as P

F32 = jnp.float32
BF16 = jnp.bfloat16
LANES = 128
ID_ROWS = 8
PARAMS = pltpu.CompilerParams(vmem_limit_bytes=56 * 2**20)


def rows_of(shape):
    return lax.broadcasted_iota(jnp.int32, shape, 0).astype(F32)


def lanes_of(shape):
    return lax.broadcasted_iota(jnp.int32, shape, 1).astype(F32)


def hot(condition):
    return jnp.where(condition, 1.0, 0.0).astype(BF16)


def dot(a, b, contract):
    return lax.dot_general(a, b, (contract, ((), ())), preferred_element_type=F32)


def prepare(members, capacity, first, second, table, embeddings, packed, labels, place):
    vectors = first.shape[1]
    slots = table[...]
    local = slots & (LANES - 1)
    owner = (slots // LANES) & (members - 1)
    group = slots // (LANES * members)
    planes = jnp.concatenate([local, owner, group], axis=1).astype(F32).astype(BF16)

    def look_up(ids):
        row = (ids // LANES).astype(F32)
        lane = (ids & (LANES - 1)).astype(F32)
        found = dot(planes, hot(rows_of((table.shape[0], vectors)) == row), ((0,), (0,)))
        mask = rows_of((LANES, vectors)) == lane

        def pick(k):
            return jnp.sum(
                jnp.where(mask, found[k * LANES : (k + 1) * LANES], 0.0), axis=0, keepdims=True
            )

        return pick(0), pick(1), pick(2)

    first_local, first_owner, first_group = look_up(first[...])
    second_local, _, second_group = look_up(second[...])
    is_owner = rows_of((members, vectors)) == first_owner
    before = hot(rows_of((vectors, vectors)) < lanes_of((vectors, vectors)))
    earlier = dot(hot(is_owner), before, ((1,), (0,)))
    rank = jnp.sum(jnp.where(is_owner, earlier, 0.0), axis=0, keepdims=True)
    spot = first_owner * capacity + rank
    order = hot(rows_of((members * capacity, vectors)) == spot)
    packed[...] = dot(order, embeddings[...], ((1,), (0,))).astype(BF16)
    ranked = rows_of((16, vectors)) == rank
    digits = [first_group + 1.0, first_local, second_group + 1.0, second_local]
    spread = [jnp.where(ranked, digit, 0.0) for digit in digits]
    spread.append(jnp.zeros((LANES - 16 * len(digits), vectors), F32))
    table_of = jnp.concatenate(spread, axis=0).astype(BF16)
    labels[...] = dot(hot(is_owner), table_of, ((1,), (1,))).astype(BF16)
    place[...] = spot.astype(jnp.int32)


def partial_sums(
    chips, capacity, where, own, other, own_labels, other_labels, ids, *blocks
):
    chip = where[0].astype(F32)
    core = where[1].astype(F32)
    members = own_labels.shape[0]
    count = own.shape[0]
    width = own.shape[1]
    from_member = jnp.floor((lanes_of((members, count)) + 0.5) * (1.0 / capacity))
    spread = hot(rows_of((members, count)) == from_member)
    position = lanes_of((16, count))
    position = position - capacity * jnp.floor((position + 0.5) * (1.0 / capacity))
    ranked = rows_of((16, count)) == position

    def decode(labels):
        found = dot(labels[...], spread, ((0,), (0,)))

        def pick(k):
            return jnp.sum(
                jnp.where(ranked, found[k * 16 : (k + 1) * 16], 0.0), axis=0, keepdims=True
            )

        def index(group, local):
            group = group - 1.0
            at_chip = jnp.floor((group + 0.5) * 0.5)
            at_core = group - 2.0 * at_chip
            ahead = at_chip - chip
            ahead = jnp.where(ahead < 0.0, ahead + chips, ahead)
            mine = (group >= 0.0) & (at_core == core)
            return jnp.where(mine, ahead * LANES + local, -1.0)

        return index(pick(0), pick(1)), index(pick(2), pick(3))

    own_first, own_second = decode(own_labels)
    other_first, other_second = decode(other_labels)
    first = jnp.concatenate([own_first, other_first], axis=1)
    second = jnp.concatenate([own_second, other_second], axis=1)
    ids[0:1, :] = first
    ids[1:2, :] = second
    ones = jnp.ones((16, 2 * count), BF16)
    for ahead in range(chips):
        table = hot(rows_of((LANES, 2 * count)) + ahead * LANES == first)
        total = dot(table[:, :count], own[...], ((1,), (0,))) + dot(
            table[:, count:], other[...], ((1,), (0,))
        )
        hits = dot(ones, table, ((1,), (1,)))
        high = jnp.floor(hits * (1.0 / 256.0))
        rest = hits - 256.0 * high
        middle = jnp.floor(rest * (1.0 / 16.0))
        low = rest - 16.0 * middle
        block = blocks[ahead]
        block[0:LANES, :] = total.astype(BF16)
        block[LANES : LANES + 16, :] = jnp.concatenate(
            [low, middle, high, jnp.zeros((16, width - 3 * LANES), F32)], axis=1
        ).astype(BF16)


def refit(mine, above, below, old, fresh):
    total = mine[...].astype(F32) + above[...].astype(F32) + below[...].astype(F32)
    digits = total[LANES : LANES + 16].astype(BF16)
    identity = hot(rows_of((LANES, LANES)) == lanes_of((LANES, LANES)))

    def column(k):
        return dot(identity, digits[:, k * LANES : (k + 1) * LANES], ((1,), (1,)))[:, 0:1]

    counts = column(0) + 16.0 * column(1) + 256.0 * column(2)
    fresh[...] = ((total[0:LANES] + old[...].astype(F32)) / (counts + 1.0)).astype(BF16)


def score(chips, own, other, ids, *refs):
    blocks, out = refs[:-1], refs[-1]
    width = own.shape[1]
    count = own.shape[0]
    first = ids[0:1, :]
    second = ids[1:2, :]
    total = jnp.zeros((1, 2 * count), F32)
    for ahead in range(chips):
        block = blocks[ahead][...]
        products = [dot(block, v[...], ((1,), (1,))) for v in (own, other)]
        product = jnp.concatenate(products, axis=1)
        size = jnp.sum(block.astype(F32) ** 2, axis=1, keepdims=True)
        distance = size - 2.0 * product
        at = rows_of((LANES, 2 * count)) + ahead * LANES
        total += jnp.sum(
            jnp.where(at == second, distance, 0.0) - jnp.where(at == first, distance, 0.0),
            axis=0,
            keepdims=True,
        )
    out[...] = total * (1.0 / width)


def shifted(axis, size, step):
    pairs = [(i, (i + step) % size) for i in range(size)]
    return lambda a: lax.ppermute(a, axis, pairs)


def add(a, b):
    return (a.astype(F32) + b.astype(F32)).astype(BF16)


def ring_sum(up, down, blocks):
    half = blocks[0].shape[1] // 2
    above = up(blocks[4][:, :half])
    below = down(blocks[4][:, half:])
    above = up(jnp.concatenate([add(blocks[3][:, :half], above), blocks[3][:, half:]], axis=1))
    below = down(jnp.concatenate([blocks[5][:, :half], add(blocks[5][:, half:], below)], axis=1))
    above = up(add(blocks[2], above))
    below = down(add(blocks[6], below))
    above = up(add(blocks[1], above))
    below = down(add(blocks[7], below))
    return blocks[0], above, below


def ring_gather(up, down, block):
    half = block.shape[1] // 2
    above, below = [block], [block]
    for _ in range(3):
        above.append(up(above[-1]))
        below.append(down(below[-1]))
    far = jnp.concatenate([up(above[3][:, :half]), down(below[3][:, half:])], axis=1)
    return [block, below[1], below[2], below[3], far, above[3], above[2], above[1]]


def on_device(embeddings, assignment, second_choice, list_slot, old_centroids):
    vectors, width = embeddings.shape
    lists = old_centroids.shape[0]
    members = lax.axis_size("mem")
    chips = lax.axis_size("x")
    capacity = vectors // members + 2
    count = members * capacity
    tiles = capacity * width // LANES
    up = shifted("x", chips, 1)
    down = shifted("x", chips, -1)
    across = shifted("core", 2, 1)

    packed, labels, place = pl.pallas_call(
        functools.partial(prepare, members, capacity),
        out_shape=(
            jax.ShapeDtypeStruct((count, width), BF16),
            jax.ShapeDtypeStruct((members, LANES), BF16),
            jax.ShapeDtypeStruct((1, vectors), jnp.int32),
        ),
        compiler_params=PARAMS,
        name="prepare",
    )(
        assignment.reshape(1, vectors),
        second_choice.reshape(1, vectors),
        list_slot.reshape(-1, LANES),
        embeddings,
    )
    outgoing = jnp.concatenate(
        [
            packed.reshape(members, tiles, LANES),
            jnp.pad(labels[:, None, :], ((0, 0), (0, ID_ROWS - 1), (0, 0))),
        ],
        axis=1,
    )
    arrived = lax.all_to_all(outgoing, "mem", split_axis=0, concat_axis=0, tiled=True)
    beside = across(arrived)

    def unpack(a):
        return a[:, :tiles].reshape(count, width), a[:, tiles]

    own, own_labels = unpack(arrived)
    other, other_labels = unpack(beside)
    where = jnp.stack([lax.axis_index("x"), lax.axis_index("core")]).astype(jnp.int32)
    vmem = pl.BlockSpec(memory_space=pltpu.VMEM)
    ids, *blocks = pl.pallas_call(
        functools.partial(partial_sums, chips, capacity),
        in_specs=[pl.BlockSpec(memory_space=pltpu.SMEM)] + [vmem] * 4,
        out_shape=[jax.ShapeDtypeStruct((2, 2 * count), F32)]
        + [jax.ShapeDtypeStruct((lists + 16, width), BF16)] * chips,
        compiler_params=PARAMS,
        name="partial_sums",
    )(where, own, other, own_labels, other_labels)
    fresh = pl.pallas_call(
        refit,
        out_shape=jax.ShapeDtypeStruct((lists, width), BF16),
        compiler_params=PARAMS,
        name="refit",
    )(*ring_sum(up, down, blocks), old_centroids)
    scored = pl.pallas_call(
        functools.partial(score, chips),
        out_shape=jax.ShapeDtypeStruct((1, 2 * count), F32),
        compiler_params=PARAMS,
        name="score",
    )(own, other, ids, *ring_gather(up, down, fresh))
    scored = scored.reshape(2, members, 1, capacity)
    margin = scored[0] + across(scored[1])
    returned = lax.all_to_all(margin, "mem", split_axis=0, concat_axis=0, tiled=True)
    spots = jnp.arange(count, dtype=jnp.int32)
    margins = jnp.sum(
        jnp.where(place.reshape(vectors, 1) == spots[None, :], returned.reshape(1, count), 0.0),
        axis=1,
    )
    return fresh, margins


def solution(mesh):
    groups, members = mesh.devices.shape
    chip_mesh = Mesh(mesh.devices.reshape(groups // 2, 2, members), ("x", "core", "mem"))
    everywhere = ("x", "core", "mem")
    placed = (
        P(everywhere, None),
        P(everywhere),
        P(everywhere),
        P(),
        P(everywhere, None),
    )
    return jax.shard_map(
        on_device,
        mesh=chip_mesh,
        in_specs=placed,
        out_specs=(P(everywhere, None), P(everywhere)),
        check_vma=False,
    )
```

time: 290 us -> 218 us (0.75); the launches traced: 290 us -> 214 us
  waiting for transfers between devices: 126 us -> 23.3 us
  blocking collectives: 49.1 us -> 76.9 us
  Pallas kernels: 0 us -> 24.3 us
  local copies, waits for them, and re-layouts: 40 us -> 17.1 us
  starting transfers between devices: 44.2 us -> 67.1 us
  between operations: 15 us -> 1.03 us
  matrix products: 6.21 us -> 0 us
  other arithmetic: 9.47 us -> 4.48 us
    ppermute x0 -> x18, starting transfers between devices: none -> 67.1 us  [shifted(): return lambda a: lax.ppermute(a, axis, pairs)]
    all_to_all x3 -> x0, waiting for transfers between devices: 63.4 us -> none  [the longest x1 47 us: on_device(): lax.all_to_all(outgoing.reshape(members, capacity, width), 'mem', split_a...]
    all_to_all x1 -> x2, blocking collectives: 22 us -> 76.9 us  [the longest x1 58.5 us: on_device(): lax.all_to_all(outgoing, 'mem', split_axis=0, concat_axis=0, tiled=True)]
    all_to_all x3 -> x0, starting transfers between devices: 44.1 us -> none  [the longest x1 24 us: on_device(): lax.all_to_all(first_ids.reshape(members, capacity), 'mem', split_axis=0,...]
    reduce_scatter x1 -> x0, waiting for transfers between devices: 41.1 us -> none  [on_device(): lax.psum_scatter(jnp.dot(table, received, preferred_element_type=jnp.floa...]
    unnamed x1 -> x0, blocking collectives: 27.1 us -> none
    pallas_call x0 -> x4, Pallas kernels: none -> 24.3 us  [the longest x1 9.83 us: on_device(): pl.pallas_call(functools.partial(score, chips), out_shape=jax.ShapeDtypeS...]
    gather x5 -> x0, local copies, waits for them, and re-layouts: 23.6 us -> none  [the longest x2 13.9 us: take_rows(): rows = jnp.take(piece, safe, axis=0).astype(jnp.float32)]
  transfers between devices with their start and end apart: 5 -> 18, of which waited for: 5 -> 14; matrix products, arithmetic and copies ran while one was open for 5% -> 3% of each run, Pallas kernels for 0% -> 0%
where the time goes in v1:
time: 218 us; the launch traced here: 214 us
  blocking collectives  76.9 us (35%)
  starting transfers between devices  67.1 us (31%)
  Pallas kernels  24.3 us (11%)
  waiting for transfers between devices  23.3 us (11%)
  local copies, waits for them, and re-layouts  17.1 us (8%)
  other arithmetic  4.48 us (2%)
    ppermute x18, starting transfers between devices, shifted(): return lambda a: lax.ppermute(a, axis, pairs)  67.1 us
    all_to_all x1, blocking collectives, on_device(): lax.all_to_all(outgoing, 'mem', split_axis=0, concat_axis=0, tiled=True)  58.5 us
    ppermute x18, waiting for transfers between devices, shifted(): return lambda a: lax.ppermute(a, axis, pairs)  23.3 us
    all_to_all x1, blocking collectives, on_device(): lax.all_to_all(margin, 'mem', split_axis=0, concat_axis=0, tiled=True)  18.3 us
    pallas_call x1, Pallas kernels, on_device(): pl.pallas_call(functools.partial(score, chips), out_shape=jax.ShapeDtypeS...  9.83 us
    pallas_call x1, Pallas kernels, on_device(): pl.pallas_call(functools.partial(partial_sums, chips, capacity), in_specs...  7.33 us
    pallas_call x1, Pallas kernels, on_device(): pl.pallas_call(functools.partial(prepare, members, capacity), out_shape=(...  4.94 us
  transfers between devices with their start and end apart: 18, of which 14 were waited for; matrix products, arithmetic and copies ran while one was open for 3% of the time, Pallas kernels for 0%

profile of v1, /device:TPU:1, one launch (start us, length us, event | category | flops | bytes accessed | tf_op | source)
XLA Modules:
  0.0 214.1 jit_solution(9968386384866637797)
XLA Ops:
  0.6 4.9 %prepare.1 = (bf16[640,1024]{1,0:T(8,128)(2,1)}, bf16[64,128]{1,0:T(8,128)(2,1)}, s32[1,512]{1,0:T(1,128)}) custom-call(s32[1,512]{1,0:T(1,128)} %bitcast.15, s32[1,512]{1,0:T(1,128)} %bitcast.16, s32[1024,128]{1,0:T(8,128)} %bitcast.12, bf16[512,1024]{1,0:T(8,128)(2,1)} %embeddings.1), custom_call_target="tpu_custom_call" | custom-call | tf_op jit(solution)/shard_map/prepare/pallas_call | solution.py:208
  5.6 2.4 %reshape.34 = bf16[64,80,128]{2,1,0:T(8,128)(2,1)S(1)} reshape(bf16[640,1024]{1,0:T(8,128)(2,1)} %get-tuple-element.14) | data formatting | bytes 2621440 | tf_op jit(solution)/shard_map/reshape | solution.py:225
  8.1 58.5 %all_to_all.10 = bf16[64,88,128]{2,1,0:T(8,128)(2,1)S(1)} all-to-all(bf16[64,88,128]{2,1,0:T(8,128)(2,1)S(1)} %fusion.1), channel_id=1, replica_groups=mesh['x'=8,'core'=2,'mem'=64] {'mem'}, dimensions={0} | all-to-all | bytes 2883584 | tf_op jit(solution)/shard_map/all_to_all | solution.py:230
  68.1 6.1 %collective-permute-start = (bf16[64,88,128]{2,0,1:T(8,128)(2,1)}, bf16[64,88,128]{2,0,1:T(8,128)(2,1)}, u32[]{:S(2)}, u32[]{:S(2)}) collective-permute-start(bf16[64,88,128]{2,0,1:T(8,128)(2,1)} %copy.18), channel_id=1, source_target_pairs={{0,64},{64,0},{1,65},{65,1},{2,66},{66,2},{3,67},{67,3},{4,68},{68... | collective-permute-start | bytes 4325384 | tf_op jit(solution)/shard_map/ppermute | solution.py:166
  82.8 7.3 %partial_sums.1 = (f32[2,1280]{1,0:T(2,128)}, bf16[144,1024]{1,0:T(8,128)(2,1)}, bf16[144,1024]{1,0:T(8,128)(2,1)}, bf16[144,1024]{1,0:T(8,128)(2,1)}, bf16[144,...) custom-call(s32[2]{0:T(128)} %pad_add_fusion.where, ...), custom_call_target="tpu_custom_call" | custom-call | tf_op jit(solution)/shard_map/partial_sums/pallas_call | solution.py:240
  91.2 3.3 %collective-permute-start.1 = (bf16[144,512]{1,0:T(8,128)(2,1)S(1)}, bf16[144,512]{1,0:T(8,128)(2,1)S(1)}, u32[]{:S(2)}, u32[]{:S(2)}) collective-permute-start(bf16[144,512]{1,0:T(8,128)(2,1)S(1)} %get-tuple-element.29), channel_id=1, source_target_pairs={{0,128},{128,256},{256,384},{384,512},{512,640},{640,768},{768,896... | collective-permute-start | bytes 442376 | tf_op jit(solution)/shard_map/ppermute | solution.py:166
  96.3 3.5 %collective-permute-start.5 = (bf16[144,512]{1,0:T(8,128)(2,1)S(1)}, bf16[144,512]{1,0:T(8,128)(2,1)S(1)}, u32[]{:S(2)}, u32[]{:S(2)}) collective-permute-start(bf16[144,512]{1,0:T(8,128)(2,1)S(1)} %get-tuple-element.28), channel_id=1, source_target_pairs={{0,896},{128,0},{256,128},{384,256},{512,384},{640,512},{768,640},... | collective-permute-start | bytes 442376 | tf_op jit(solution)/shard_map/ppermute | solution.py:166
  103.5 4.7 %collective-permute-start.6 = (bf16[144,1024]{1,0:T(8,128)(2,1)S(1)}, bf16[144,1024]{1,0:T(8,128)(2,1)S(1)}, u32[]{:S(2)}, u32[]{:S(2)}) collective-permute-start(bf16[144,1024]{1,0:T(8,128)(2,1)S(1)} %pad_maximum_fusion.1), channel_id=1, source_target_pairs={{0,896},{128,0},{256,128},{384,256},{512,384},{640,512},{768,640},... | collective-permute-start | bytes 884744 | tf_op jit(solution)/shard_map/ppermute | solution.py:166
  108.2 3.5 %collective-permute-done.2 = bf16[144,1024]{1,0:T(8,128)(2,1)S(1)} collective-permute-done((bf16[144,1024]{1,0:T(8,128)(2,1)S(1)}, bf16[144,1024]{1,0:T(8,128)(2,1)S(1)}, u32[]{:S(2)}, u32[]{:S(2)}) %collective-permute-start.2) | collective-permute-done | bytes 294944 | tf_op jit(solution)/shard_map/ppermute | solution.py:166
  113.8 4.9 %collective-permute-start.7 = (bf16[144,1024]{1,0:T(8,128)(2,1)S(1)}, bf16[144,1024]{1,0:T(8,128)(2,1)S(1)}, u32[]{:S(2)}, u32[]{:S(2)}) collective-permute-start(bf16[144,1024]{1,0:T(8,128)(2,1)S(1)} %add_convert_fusion.1), channel_id=1, source_target_pairs={{0,896},{128,0},{256,128},{384,256},{512,384},{640,512},{768,640},... | collective-permute-start | bytes 884744 | tf_op jit(solution)/shard_map/ppermute | solution.py:166
  118.7 2.9 %collective-permute-done.3 = bf16[144,1024]{1,0:T(8,128)(2,1)S(1)} collective-permute-done((bf16[144,1024]{1,0:T(8,128)(2,1)S(1)}, bf16[144,1024]{1,0:T(8,128)(2,1)S(1)}, u32[]{:S(2)}, u32[]{:S(2)}) %collective-permute-start.3) | collective-permute-done | bytes 294944 | tf_op jit(solution)/shard_map/ppermute | solution.py:166
  123.8 4.6 %collective-permute-start.8 = (bf16[144,1024]{1,0:T(8,128)(2,1)S(1)}, bf16[144,1024]{1,0:T(8,128)(2,1)S(1)}, u32[]{:S(2)}, u32[]{:S(2)}) collective-permute-start(bf16[144,1024]{1,0:T(8,128)(2,1)S(1)} %add_convert_fusion), channel_id=1, source_target_pairs={{0,896},{128,0},{256,128},{384,256},{512,384},{640,512},{768,640},... | collective-permute-start | bytes 884744 | tf_op jit(solution)/shard_map/ppermute | solution.py:166
  132.8 2.2 %refit.1.refs_0_ = bf16[128,1024]{1,0:T(8,128)(2,1)} custom-call(bf16[144,1024]{1,0:T(8,128)(2,1)} %get-tuple-element.16.mine, bf16[144,1024]{1,0:T(8,128)(2,1)} %copy-done.7, bf16[144,1024]{1,0:T(8,128)(2,1)} %copy-done.8, bf16[128,1024]{1,0:T(8,128)(2,1)} %old.1), custom_call_target="tpu_custom_call" | custom-call | tf_op jit(solution)/shard_map/refit/pallas_call | solution.py:248
  135.0 3.8 %collective-permute-start.12 = (bf16[128,1024]{1,0:T(8,128)(2,1)}, bf16[128,1024]{1,0:T(8,128)(2,1)S(1)}, u32[]{:S(2)}, u32[]{:S(2)}) collective-permute-start(bf16[128,1024]{1,0:T(8,128)(2,1)} %refit.1.refs_0_), channel_id=1, source_target_pairs={{0,128},{128,256},{256,384},{384,512},{512,640},{640,768},{768,896... | collective-permute-start | bytes 786440 | tf_op jit(solution)/shard_map/ppermute | solution.py:166
  138.8 3.1 %collective-permute-start.9 = (bf16[128,1024]{1,0:T(8,128)(2,1)}, bf16[128,1024]{1,0:T(8,128)(2,1)S(1)}, u32[]{:S(2)}, u32[]{:S(2)}) collective-permute-start(bf16[128,1024]{1,0:T(8,128)(2,1)} %refit.1.refs_0_), channel_id=1, source_target_pairs={{0,896},{128,0},{256,128},{384,256},{512,384},{640,512},{768,640},... | collective-permute-start | bytes 786440 | tf_op jit(solution)/shard_map/ppermute | solution.py:166
  144.0 2.3 %collective-permute-start.13 = (bf16[128,1024]{1,0:T(8,128)(2,1)S(1)}, bf16[128,1024]{1,0:T(8,128)(2,1)S(1)}, u32[]{:S(2)}, u32[]{:S(2)}) collective-permute-start(bf16[128,1024]{1,0:T(8,128)(2,1)S(1)} %collective-permute-done.12.refs_7_), channel_id=1, source_target_pairs={{0,128},{128,256},{256,384},{384,512},{512,640},{640,768},{768,896... | collective-permute-start | bytes 786440 | tf_op jit(solution)/shard_map/ppermute | solution.py:166
  146.9 3.6 %collective-permute-start.10 = (bf16[128,1024]{1,0:T(8,128)(2,1)S(1)}, bf16[128,1024]{1,0:T(8,128)(2,1)S(1)}, u32[]{:S(2)}, u32[]{:S(2)}) collective-permute-start(bf16[128,1024]{1,0:T(8,128)(2,1)S(1)} %collective-permute-done.9.refs_1_), channel_id=1, source_target_pairs={{0,896},{128,0},{256,128},{384,256},{512,384},{640,512},{768,640},... | collective-permute-start | bytes 786440 | tf_op jit(solution)/shard_map/ppermute | solution.py:166
  154.9 3.9 %collective-permute-start.11 = (bf16[128,1024]{1,0:T(8,128)(2,1)S(1)}, bf16[128,1024]{1,0:T(8,128)(2,1)S(1)}, u32[]{:S(2)}, u32[]{:S(2)}) collective-permute-start(bf16[128,1024]{1,0:T(8,128)(2,1)S(1)} %collective-permute-done.10.refs_2_), channel_id=1, source_target_pairs={{0,896},{128,0},{256,128},{384,256},{512,384},{640,512},{768,640},... | collective-permute-start | bytes 786440 | tf_op jit(solution)/shard_map/ppermute | solution.py:166
  160.6 2.2 %collective-permute-start.15 = (bf16[128,512]{1,0:T(8,128)(2,1)S(1)}, bf16[128,512]{1,0:T(8,128)(2,1)S(1)}, u32[]{:S(2)}, u32[]{:S(2)}) collective-permute-start(bf16[128,512]{1,0:T(8,128)(2,1)S(1)} %slice.62), channel_id=1, source_target_pairs={{0,128},{128,256},{256,384},{384,512},{512,640},{640,768},{768,896... | collective-permute-start | bytes 393224 | tf_op jit(solution)/shard_map/ppermute | solution.py:166
  163.4 4.0 %collective-permute-start.16 = (bf16[128,512]{1,0:T(8,128)(2,1)S(1)}, bf16[128,512]{1,0:T(8,128)(2,1)S(1)}, u32[]{:S(2)}, u32[]{:S(2)}) collective-permute-start(bf16[128,512]{1,0:T(8,128)(2,1)S(1)} %slice.63), channel_id=1, source_target_pairs={{0,896},{128,0},{256,128},{384,256},{512,384},{640,512},{768,640},... | collective-permute-start | bytes 393224 | tf_op jit(solution)/shard_map/ppermute | solution.py:166
  168.6 3.1 %collective-permute-done.16 = bf16[128,512]{1,0:T(8,128)(2,1)S(1)} collective-permute-done((bf16[128,512]{1,0:T(8,128)(2,1)S(1)}, bf16[128,512]{1,0:T(8,128)(2,1)S(1)}, u32[]{:S(2)}, u32[]{:S(2)}) %collective-permute-start.16) | collective-permute-done | bytes 131104 | tf_op jit(solution)/shard_map/ppermute | solution.py:166
  172.5 9.8 %score.1 = f32[1,1280]{1,0:T(1,128)} custom-call(bf16[640,1024]{1,0:T(8,128)(2,1)} %reshape.35.own, bf16[640,1024]{1,0:T(8,128)(2,1)} %reshape.36.other, f32[2,1280]{1,0:T(2,128)} %get-tuple-element.25.ids, bf16[128,1024]{1,0:T(8,128)(2,1)} %refit.1.refs_0_, bf16[128,1024]{1,0:T(8,128)(2,1)} %copy-done.10, bf16[128,1024]{1,0:T(8,128)(2,1)} %copy-done.12, ...), custom_call_target="tpu_custom_call" | custom-call | tf_op jit(solution)/shard_map/score/pallas_call | solution.py:254
  183.1 9.4 %collective-permute-start.17 = (f32[64,1,10]{2,0,1:T(8,128)S(1)}, f32[64,1,10]{2,0,1:T(8,128)S(1)}, u32[]{:S(2)}, u32[]{:S(2)}) collective-permute-start(f32[64,1,10]{2,0,1:T(8,128)S(1)} %squeeze.15), channel_id=1, source_target_pairs={{0,64},{64,0},{1,65},{65,1},{2,66},{66,2},{3,67},{67,3},{4,68},{68... | collective-permute-start | bytes 7688 | tf_op jit(solution)/shard_map/ppermute | solution.py:166
  193.4 18.3 %all_to_all.11 = f32[64,1,10]{2,1,0:T(1,128)S(1)} all-to-all(f32[64,1,10]{2,1,0:T(1,128)S(1)} %bitcast.13), channel_id=1, replica_groups=mesh['x'=8,'core'=2,'mem'=64] {'mem'}, dimensions={0} | all-to-all | bytes 5120 | tf_op jit(solution)/shard_map/all_to_all | solution.py:262
  (82 shorter events, 40.7 us)
Async XLA Ops:
  68.1 9.6 %collective-permute-start = (bf16[64,88,128]{2,0,1:T(8,128)(2,1)}, bf16[64,88,128]{2,0,1:T(8,128)(2,1)}, u32[]{:S(2)}, u32[]{:S(2)}) collective-permute-start(bf16[64,88,128]{2,0,1:T(8,128)(2,1)} %copy.18), channel_id=1, source_target_pairs={{0,64},{64,0},{1,65},{65,1},{2,66},{66,2},{3,67},{67,3},{4,68},{68... | collective-permute-start | bytes 4325384 | tf_op jit(solution)/shard_map/ppermute | solution.py:166
  91.2 20.6 %copy-start.5 = (bf16[144,1024]{1,0:T(8,128)(2,1)S(1)}, bf16[144,1024]{1,0:T(8,128)(2,1)}, u32[]{:S(2)}) copy-start(bf16[144,1024]{1,0:T(8,128)(2,1)} %get-tuple-element.18) | copy-start | bytes 884740
  91.2 8.7 %collective-permute-start.1 = (bf16[144,512]{1,0:T(8,128)(2,1)S(1)}, bf16[144,512]{1,0:T(8,128)(2,1)S(1)}, u32[]{:S(2)}, u32[]{:S(2)}) collective-permute-start(bf16[144,512]{1,0:T(8,128)(2,1)S(1)} %get-tuple-element.29), channel_id=1, source_target_pairs={{0,128},{128,256},{256,384},{384,512},{512,640},{640,768},{768,896... | collective-permute-start | bytes 442376 | tf_op jit(solution)/shard_map/ppermute | solution.py:166
  96.3 7.1 %collective-permute-start.5 = (bf16[144,512]{1,0:T(8,128)(2,1)S(1)}, bf16[144,512]{1,0:T(8,128)(2,1)S(1)}, u32[]{:S(2)}, u32[]{:S(2)}) collective-permute-start(bf16[144,512]{1,0:T(8,128)(2,1)S(1)} %get-tuple-element.28), channel_id=1, source_target_pairs={{0,896},{128,0},{256,128},{384,256},{512,384},{640,512},{768,640},... | collective-permute-start | bytes 442376 | tf_op jit(solution)/shard_map/ppermute | solution.py:166
  100.8 20.9 %copy-start.3 = (bf16[144,1024]{1,0:T(8,128)(2,1)S(1)}, bf16[144,1024]{1,0:T(8,128)(2,1)}, u32[]{:S(2)}) copy-start(bf16[144,1024]{1,0:T(8,128)(2,1)} %get-tuple-element.17) | copy-start | bytes 884740
  100.8 10.9 %collective-permute-start.2 = (bf16[144,1024]{1,0:T(8,128)(2,1)S(1)}, bf16[144,1024]{1,0:T(8,128)(2,1)S(1)}, u32[]{:S(2)}, u32[]{:S(2)}) collective-permute-start(bf16[144,1024]{1,0:T(8,128)(2,1)S(1)} %pad_maximum_fusion), channel_id=1, source_target_pairs={{0,128},{128,256},{256,384},{384,512},{512,640},{640,768},{768,896... | collective-permute-start | bytes 884744 | tf_op jit(solution)/shard_map/ppermute | solution.py:166
  103.5 20.2 %copy-start.2 = (bf16[144,1024]{1,0:T(8,128)(2,1)S(1)}, bf16[144,1024]{1,0:T(8,128)(2,1)}, u32[]{:S(2)}) copy-start(bf16[144,1024]{1,0:T(8,128)(2,1)} %get-tuple-element.21) | copy-start | bytes 884740
  103.5 10.3 %collective-permute-start.6 = (bf16[144,1024]{1,0:T(8,128)(2,1)S(1)}, bf16[144,1024]{1,0:T(8,128)(2,1)S(1)}, u32[]{:S(2)}, u32[]{:S(2)}) collective-permute-start(bf16[144,1024]{1,0:T(8,128)(2,1)S(1)} %pad_maximum_fusion.1), channel_id=1, source_target_pairs={{0,896},{128,0},{256,128},{384,256},{512,384},{640,512},{768,640},... | collective-permute-start | bytes 884744 | tf_op jit(solution)/shard_map/ppermute | solution.py:166
  111.8 9.9 %collective-permute-start.3 = (bf16[144,1024]{1,0:T(8,128)(2,1)S(1)}, bf16[144,1024]{1,0:T(8,128)(2,1)S(1)}, u32[]{:S(2)}, u32[]{:S(2)}) collective-permute-start(bf16[144,1024]{1,0:T(8,128)(2,1)S(1)} %add_convert_fusion.3), channel_id=1, source_target_pairs={{0,128},{128,256},{256,384},{384,512},{512,640},{640,768},{768,896... | collective-permute-start | bytes 884744 | tf_op jit(solution)/shard_map/ppermute | solution.py:166
  113.8 9.8 %collective-permute-start.7 = (bf16[144,1024]{1,0:T(8,128)(2,1)S(1)}, bf16[144,1024]{1,0:T(8,128)(2,1)S(1)}, u32[]{:S(2)}, u32[]{:S(2)}) collective-permute-start(bf16[144,1024]{1,0:T(8,128)(2,1)S(1)} %add_convert_fusion.1), channel_id=1, source_target_pairs={{0,896},{128,0},{256,128},{384,256},{512,384},{640,512},{768,640},... | collective-permute-start | bytes 884744 | tf_op jit(solution)/shard_map/ppermute | solution.py:166
  121.8 8.7 %collective-permute-start.4 = (bf16[144,1024]{1,0:T(8,128)(2,1)S(1)}, bf16[144,1024]{1,0:T(8,128)(2,1)S(1)}, u32[]{:S(2)}, u32[]{:S(2)}) collective-permute-start(bf16[144,1024]{1,0:T(8,128)(2,1)S(1)} %add_convert_fusion.2), channel_id=1, source_target_pairs={{0,128},{128,256},{256,384},{384,512},{512,640},{640,768},{768,896... | collective-permute-start | bytes 884744 | tf_op jit(solution)/shard_map/ppermute | solution.py:166
  123.8 8.2 %collective-permute-start.8 = (bf16[144,1024]{1,0:T(8,128)(2,1)S(1)}, bf16[144,1024]{1,0:T(8,128)(2,1)S(1)}, u32[]{:S(2)}, u32[]{:S(2)}) collective-permute-start(bf16[144,1024]{1,0:T(8,128)(2,1)S(1)} %add_convert_fusion), channel_id=1, source_target_pairs={{0,896},{128,0},{256,128},{384,256},{512,384},{640,512},{768,640},... | collective-permute-start | bytes 884744 | tf_op jit(solution)/shard_map/ppermute | solution.py:166
  135.0 9.0 %collective-permute-start.12 = (bf16[128,1024]{1,0:T(8,128)(2,1)}, bf16[128,1024]{1,0:T(8,128)(2,1)S(1)}, u32[]{:S(2)}, u32[]{:S(2)}) collective-permute-start(bf16[128,1024]{1,0:T(8,128)(2,1)} %refit.1.refs_0_), channel_id=1, source_target_pairs={{0,128},{128,256},{256,384},{384,512},{512,640},{640,768},{768,896... | collective-permute-start | bytes 786440 | tf_op jit(solution)/shard_map/ppermute | solution.py:166
  138.8 8.1 %collective-permute-start.9 = (bf16[128,1024]{1,0:T(8,128)(2,1)}, bf16[128,1024]{1,0:T(8,128)(2,1)S(1)}, u32[]{:S(2)}, u32[]{:S(2)}) collective-permute-start(bf16[128,1024]{1,0:T(8,128)(2,1)} %refit.1.refs_0_), channel_id=1, source_target_pairs={{0,896},{128,0},{256,128},{384,256},{512,384},{640,512},{768,640},... | collective-permute-start | bytes 786440 | tf_op jit(solution)/shard_map/ppermute | solution.py:166
  144.0 28.5 %copy-start.9 = (bf16[128,1024]{1,0:T(8,128)(2,1)}, bf16[128,1024]{1,0:T(8,128)(2,1)S(1)}, u32[]{:S(2)}) copy-start(bf16[128,1024]{1,0:T(8,128)(2,1)S(1)} %collective-permute-done.12.refs_7_) | copy-start | bytes 786436
  144.0 8.3 %collective-permute-start.13 = (bf16[128,1024]{1,0:T(8,128)(2,1)S(1)}, bf16[128,1024]{1,0:T(8,128)(2,1)S(1)}, u32[]{:S(2)}, u32[]{:S(2)}) collective-permute-start(bf16[128,1024]{1,0:T(8,128)(2,1)S(1)} %collective-permute-done.12.refs_7_), channel_id=1, source_target_pairs={{0,128},{128,256},{256,384},{384,512},{512,640},{640,768},{768,896... | collective-permute-start | bytes 786440 | tf_op jit(solution)/shard_map/ppermute | solution.py:166
  146.9 25.5 %copy-start.10 = (bf16[128,1024]{1,0:T(8,128)(2,1)}, bf16[128,1024]{1,0:T(8,128)(2,1)S(1)}, u32[]{:S(2)}) copy-start(bf16[128,1024]{1,0:T(8,128)(2,1)S(1)} %collective-permute-done.9.refs_1_) | copy-start | bytes 786436
  146.9 8.0 %collective-permute-start.10 = (bf16[128,1024]{1,0:T(8,128)(2,1)S(1)}, bf16[128,1024]{1,0:T(8,128)(2,1)S(1)}, u32[]{:S(2)}, u32[]{:S(2)}) collective-permute-start(bf16[128,1024]{1,0:T(8,128)(2,1)S(1)} %collective-permute-done.9.refs_1_), channel_id=1, source_target_pairs={{0,896},{128,0},{256,128},{384,256},{512,384},{640,512},{768,640},... | collective-permute-start | bytes 786440 | tf_op jit(solution)/shard_map/ppermute | solution.py:166
  152.3 8.3 %collective-permute-start.14 = (bf16[128,1024]{1,0:T(8,128)(2,1)S(1)}, bf16[128,1024]{1,0:T(8,128)(2,1)S(1)}, u32[]{:S(2)}, u32[]{:S(2)}) collective-permute-start(bf16[128,1024]{1,0:T(8,128)(2,1)S(1)} %collective-permute-done.13.refs_6_), channel_id=1, source_target_pairs={{0,128},{128,256},{256,384},{384,512},{512,640},{640,768},{768,896... | collective-permute-start | bytes 786440 | tf_op jit(solution)/shard_map/ppermute | solution.py:166
  154.9 8.5 %collective-permute-start.11 = (bf16[128,1024]{1,0:T(8,128)(2,1)S(1)}, bf16[128,1024]{1,0:T(8,128)(2,1)S(1)}, u32[]{:S(2)}, u32[]{:S(2)}) collective-permute-start(bf16[128,1024]{1,0:T(8,128)(2,1)S(1)} %collective-permute-done.10.refs_2_), channel_id=1, source_target_pairs={{0,896},{128,0},{256,128},{384,256},{512,384},{640,512},{768,640},... | collective-permute-start | bytes 786440 | tf_op jit(solution)/shard_map/ppermute | solution.py:166
  160.6 8.0 %collective-permute-start.15 = (bf16[128,512]{1,0:T(8,128)(2,1)S(1)}, bf16[128,512]{1,0:T(8,128)(2,1)S(1)}, u32[]{:S(2)}, u32[]{:S(2)}) collective-permute-start(bf16[128,512]{1,0:T(8,128)(2,1)S(1)} %slice.62), channel_id=1, source_target_pairs={{0,128},{128,256},{256,384},{384,512},{512,640},{640,768},{768,896... | collective-permute-start | bytes 393224 | tf_op jit(solution)/shard_map/ppermute | solution.py:166
  163.4 8.3 %collective-permute-start.16 = (bf16[128,512]{1,0:T(8,128)(2,1)S(1)}, bf16[128,512]{1,0:T(8,128)(2,1)S(1)}, u32[]{:S(2)}, u32[]{:S(2)}) collective-permute-start(bf16[128,512]{1,0:T(8,128)(2,1)S(1)} %slice.63), channel_id=1, source_target_pairs={{0,896},{128,0},{256,128},{384,256},{512,384},{640,512},{768,640},... | collective-permute-start | bytes 393224 | tf_op jit(solution)/shard_map/ppermute | solution.py:166
  172.5 40.8 %copy-start.14 = (s32[1,512]{1,0:T(1,128)S(1)}, s32[1,512]{1,0:T(1,128)}, u32[]{:S(2)}) copy-start(s32[1,512]{1,0:T(1,128)} %get-tuple-element.24) | copy-start | bytes 6148
  183.1 10.3 %collective-permute-start.17 = (f32[64,1,10]{2,0,1:T(8,128)S(1)}, f32[64,1,10]{2,0,1:T(8,128)S(1)}, u32[]{:S(2)}, u32[]{:S(2)}) collective-permute-start(f32[64,1,10]{2,0,1:T(8,128)S(1)} %squeeze.15), channel_id=1, source_target_pairs={{0,64},{64,0},{1,65},{65,1},{2,66},{66,2},{3,67},{67,3},{4,68},{68... | collective-permute-start | bytes 7688 | tf_op jit(solution)/shard_map/ppermute | solution.py:166
  (9 other events, 94.1 us)

commit v2 on v0

v2 whole, which is shorter than its diff:
```python
import functools

import jax
import jax.numpy as jnp
from jax import lax
from jax.experimental import pallas as pl
from jax.experimental.pallas import tpu as pltpu
from jax.sharding import Mesh
from jax.sharding import PartitionSpec as P

F32 = jnp.float32
BF16 = jnp.bfloat16
LANES = 128
TILE = 8
NOTES = 16
SMEM = pl.BlockSpec(memory_space=pltpu.SMEM)
VMEM = pl.BlockSpec(memory_space=pltpu.VMEM)


def rows_of(shape):
    return lax.broadcasted_iota(jnp.int32, shape, 0).astype(F32)


def lanes_of(shape):
    return lax.broadcasted_iota(jnp.int32, shape, 1).astype(F32)


def hot(condition):
    return jnp.where(condition, 1.0, 0.0).astype(BF16)


def dot(a, b, contract):
    return lax.dot_general(a, b, (contract, ((), ())), preferred_element_type=F32)


def whole(a, size):
    return jnp.floor((a + 0.5) * (1.0 / size))


def call(kernel, name, out_shape, flops, *args, scalars=None):
    specs = [VMEM] * len(args)
    if scalars is not None:
        specs = [SMEM] + specs
        args = (scalars,) + args
    return pl.pallas_call(
        kernel,
        in_specs=specs,
        out_shape=out_shape,
        compiler_params=pltpu.CompilerParams(vmem_limit_bytes=56 * 2**20),
        cost_estimate=pl.CostEstimate(flops=flops, bytes_accessed=2**21, transcendentals=0),
        name=name,
    )(*args)


def prepare(members, capacity, first, second, table, embeddings, payload, place):
    vectors = first.shape[1]
    parts = embeddings.shape[1] // LANES
    slots = table[...]
    local = slots & (LANES - 1)
    owner = (slots // LANES) & (members - 1)
    group = slots // (LANES * members)
    planes = jnp.concatenate([local, owner, group], axis=1).astype(F32).astype(BF16)

    def look_up(ids):
        row = (ids // LANES).astype(F32)
        lane = (ids & (LANES - 1)).astype(F32)
        found = dot(planes, hot(rows_of((table.shape[0], vectors)) == row), ((0,), (0,)))
        mask = rows_of((LANES, vectors)) == lane

        def pick(k):
            return jnp.sum(
                jnp.where(mask, found[k * LANES : (k + 1) * LANES], 0.0), axis=0, keepdims=True
            )

        return pick(0), pick(1), pick(2)

    first_local, first_owner, first_group = look_up(first[...])
    second_local, _, second_group = look_up(second[...])
    is_owner = rows_of((members, vectors)) == first_owner
    before = hot(rows_of((vectors, vectors)) < lanes_of((vectors, vectors)))
    earlier = dot(hot(is_owner), before, ((1,), (0,)))
    rank = jnp.sum(jnp.where(is_owner, earlier, 0.0), axis=0, keepdims=True)
    place[...] = (first_owner * capacity + rank).astype(jnp.int32)
    spot = jnp.where(
        rank < TILE, first_owner * TILE + rank, rank * members + first_owner
    )
    order = hot(rows_of((members * capacity, vectors)) == spot)
    packed = dot(order, embeddings[...], ((1,), (0,)))
    pieces = [
        packed[: TILE * members, j * LANES : (j + 1) * LANES].reshape(members, TILE, LANES)
        for j in range(parts)
    ]
    for p in range(TILE, capacity):
        vector = packed[p * members : (p + 1) * members]
        pieces.append(
            jnp.stack([vector[:, j * LANES : (j + 1) * LANES] for j in range(parts)], axis=1)
        )
    ranked = rows_of((16, vectors)) == rank
    digits = [first_group + 1.0, first_local, second_group + 1.0, second_local]
    spread = [jnp.where(ranked, digit, 0.0) for digit in digits]
    spread.append(jnp.zeros((LANES - 16 * len(digits), vectors), F32))
    labels = dot(
        hot(is_owner), jnp.concatenate(spread, axis=0).astype(BF16), ((1,), (1,))
    )
    pieces.append(jnp.broadcast_to(labels[:, None, :], (members, TILE, LANES)))
    payload[...] = jnp.concatenate(pieces, axis=1).astype(BF16)


def unpack(capacity, arrived, box):
    members = arrived.shape[0]
    count = members * capacity
    width = box.shape[1]
    parts = width // LANES
    values = arrived[...].astype(F32)
    for j in range(parts):
        at = slice(j * LANES, (j + 1) * LANES)
        box[: TILE * members, at] = (
            values[:, j * TILE : (j + 1) * TILE].reshape(TILE * members, LANES).astype(BF16)
        )
        for p in range(TILE, capacity):
            box[p * members : (p + 1) * members, at] = values[:, p * parts + j].astype(BF16)
    labels = values[:, capacity * parts].astype(BF16)
    vector = lanes_of((members, count))
    from_member = jnp.where(
        vector < TILE * members, whole(vector, TILE), vector - members * whole(vector, members)
    )
    found = dot(labels, hot(rows_of((members, count)) == from_member), ((0,), (0,)))
    vector = lanes_of((16, count))
    rank = jnp.where(
        vector < TILE * members, vector - TILE * whole(vector, TILE), whole(vector, members)
    )
    ranked = rows_of((16, count)) == rank
    rows = [
        jnp.sum(jnp.where(ranked, found[k * 16 : (k + 1) * 16], 0.0), axis=0, keepdims=True)
        for k in range(4)
    ]
    notes = jnp.concatenate(rows + [jnp.zeros((NOTES - 4, count), F32)], axis=0)
    notes = jnp.concatenate([notes, jnp.zeros((NOTES, width - count), F32)], axis=1)
    box[count : count + NOTES] = notes.astype(BF16)


def index(chips, where, notes, k, towards):
    chip = where[0].astype(F32)
    core = where[1].astype(F32)
    group = notes[2 * k : 2 * k + 1] - 1.0
    local = notes[2 * k + 1 : 2 * k + 2]
    at_chip = whole(group, 2)
    at_core = group - 2.0 * at_chip
    way = 1.0 - 2.0 * core
    away = (at_chip - chip) * (way if towards else -way)
    away = away - chips * jnp.floor((away + 0.5) * (1.0 / chips))
    return jnp.where(group >= 0.0, away * (2 * LANES) + at_core * LANES + local, -1.0)


def halves(where, width):
    half = width // 2
    core = where[1]
    return (
        pl.ds(pl.multiple_of(core * half, half), half),
        pl.ds(pl.multiple_of((1 - core) * half, half), half),
    )


def sums(chips, count, added, where, box, *refs):
    earlier, outs = refs[: len(refs) - 5], refs[-5:]
    width = box.shape[1]
    half = width // 2
    lists = 2 * LANES
    notes = box[count : count + NOTES, :count].astype(F32)
    at = index(chips, where, notes, 0, True)
    mine, rest = halves(where, width)
    ones = jnp.ones((NOTES, count), BF16)
    for k in range(5):
        table = hot(rows_of((lists, count)) + k * lists == at)
        hits = dot(ones, table, ((1,), (1,)))
        high = whole(hits, 256)
        left = hits - 256.0 * high
        middle = whole(left, 16)
        low = left - 16.0 * middle
        one = jnp.concatenate([low, middle], axis=1)
        two = jnp.concatenate([high, jnp.zeros((NOTES, half - lists), F32)], axis=1)
        digits = [jnp.where(where[1] == 0, one, two), jnp.where(where[1] == 0, two, one)]
        for n, columns in enumerate([mine] if k in (0, 4) else [mine, rest]):
            total = jnp.concatenate(
                [dot(table, box[0:count, columns], ((1,), (0,))), digits[n]], axis=0
            )
            to = slice(n * half, (n + 1) * half)
            if added:
                total = total + earlier[k][:, to].astype(F32)
            outs[k][:, to] = total.astype(BF16)


def refit(where, here, there, old, other_old, turned, fresh):
    width = here.shape[1]
    half = width // 2
    lists = 2 * LANES
    first = where[1] == 0
    left = here[:, :half].astype(F32) + there[:, half:].astype(F32)
    right = here[:, half:].astype(F32) + there[:, :half].astype(F32)

    def order(a, b):
        return jnp.where(first, a, b), jnp.where(first, b, a)

    one, two = order(left[lists:], right[lists:])
    identity = hot(rows_of((lists, lists)) == lanes_of((lists, lists)))

    def column(digits):
        return dot(identity, digits.astype(BF16), ((1,), (1,)))[:, 0:1]

    counts = column(one[:, :lists]) + 16.0 * column(one[:, lists : 2 * lists])
    counts = counts + 256.0 * column(two[:, :lists]) + 1.0
    both = jnp.concatenate(order(old[...].astype(F32), other_old[...].astype(F32)), axis=0)
    old_left, old_right = order(both[:, :half], both[:, half:])
    left = (left[:lists] + old_left) / counts
    right = (right[:lists] + old_right) / counts
    turned[:, :half] = left.astype(BF16)
    turned[:, half:] = right.astype(BF16)
    one, two = order(left, right)
    fresh[:, :half] = order(one[:LANES], one[LANES:])[0].astype(BF16)
    fresh[:, half:] = order(two[:LANES], two[LANES:])[0].astype(BF16)


def score(chips, count, k, where, own, other, block, *refs):
    before, out = refs[:-1], refs[-1]
    lists = block.shape[0]
    half = own.shape[1] // 2
    mine, rest = halves(where, own.shape[1])
    values = block[...]
    size = jnp.sum(values.astype(F32) ** 2, axis=1, keepdims=True)
    for n, box in enumerate((own, other)):
        notes = box[count : count + NOTES, :count].astype(F32)
        product = dot(values[:, :half], box[0:count, mine], ((1,), (1,)))
        if block.shape[1] > half:
            product = product + dot(values[:, half:], box[0:count, rest], ((1,), (1,)))
        distance = size - 2.0 * product
        at = rows_of((lists, count)) + k * lists
        is_first = at == index(chips, where, notes, 0, False)
        is_second = at == index(chips, where, notes, 1, False)
        total = jnp.sum(
            jnp.where(is_second, distance, 0.0) - jnp.where(is_first, distance, 0.0),
            axis=0,
            keepdims=True,
        )
        if before:
            total = total + before[0][n : n + 1]
        out[n : n + 1] = total


def add(a, b):
    return (a.astype(F32) + b.astype(F32)).astype(BF16)


def on_device(embeddings, assignment, second_choice, list_slot, old_centroids):
    vectors, width = embeddings.shape
    lists = old_centroids.shape[0]
    members = lax.axis_size("mem")
    chips = lax.axis_size("x")
    capacity = vectors // members + 2
    count = members * capacity
    half = width // 2
    tiles = (capacity + 1) * TILE
    around = [(2 * i, 2 * ((i + 1) % chips)) for i in range(chips)]
    around += [(2 * i + 1, 2 * ((i - 1) % chips) + 1) for i in range(chips)]

    def onward(a):
        return lax.ppermute(a, ("x", "core"), around)

    def across(a):
        return lax.ppermute(a, "core", [(0, 1), (1, 0)])

    def shape(*dims, kind=BF16):
        return jax.ShapeDtypeStruct(dims, kind)

    where = jnp.stack([lax.axis_index("x"), lax.axis_index("core")]).astype(jnp.int32)
    payload, place = call(
        functools.partial(prepare, members, capacity),
        "prepare",
        (shape(members, tiles, LANES), shape(1, vectors, kind=jnp.int32)),
        2**31,
        assignment.reshape(1, vectors),
        second_choice.reshape(1, vectors),
        list_slot.reshape(-1, LANES),
        embeddings,
    )
    arrived = lax.all_to_all(payload, "mem", split_axis=0, concat_axis=0, tiled=True)
    own = call(
        functools.partial(unpack, capacity), "unpack", shape(count + NOTES, width), 2**24, arrived
    )
    other = across(own)
    other_old = across(old_centroids)
    rows = 2 * lists + NOTES
    widths = (half, width, width, width, half)
    sums_shape = [shape(rows, w) for w in widths]
    flops = 2**31
    blocks = call(
        functools.partial(sums, chips, count, False), "sums", sums_shape, flops, own, scalars=where
    )
    near, one, two, three, far = call(
        functools.partial(sums, chips, count, True),
        "sums",
        sums_shape,
        flops,
        other,
        *blocks,
        scalars=where,
    )
    moving = onward(far)
    moving = onward(jnp.concatenate([add(three[:, :half], moving), three[:, half:]], axis=1))
    moving = onward(add(two, moving))
    moving = onward(add(one, moving))
    here = jnp.concatenate([add(near, moving[:, :half]), moving[:, half:]], axis=1)
    turned, fresh = call(
        refit,
        "refit",
        (shape(2 * lists, width), shape(lists, width)),
        2**24,
        here,
        across(here),
        old_centroids,
        other_old,
        scalars=where,
    )

    def scored(k, block, *before):
        return call(
            functools.partial(score, chips, count, k),
            "score",
            shape(2, count, kind=F32),
            2**31,
            own,
            other,
            block,
            *before,
            scalars=where,
        )

    first = onward(turned)
    total = scored(0, turned[:, :half])
    second = onward(first)
    total = scored(1, first, total)
    third = onward(second)
    total = scored(2, second, total)
    fourth = onward(third[:, :half])
    total = scored(3, third, total)
    total = scored(4, fourth, total)
    margin = (total[0] + across(total[1])) * (1.0 / width)
    margin = jnp.concatenate(
        [
            margin[: TILE * members].reshape(members, TILE),
            margin[TILE * members :].reshape(capacity - TILE, members).T,
        ],
        axis=1,
    )
    returned = lax.all_to_all(
        margin.reshape(members, 1, capacity), "mem", split_axis=0, concat_axis=0, tiled=True
    )
    spots = jnp.arange(count, dtype=jnp.int32)
    margins = jnp.sum(
        jnp.where(place.reshape(vectors, 1) == spots[None, :], returned.reshape(1, count), 0.0),
        axis=1,
    )
    return fresh, margins


def solution(mesh):
    groups, members = mesh.devices.shape
    chip_mesh = Mesh(mesh.devices.reshape(groups // 2, 2, members), ("x", "core", "mem"))
    everywhere = ("x", "core", "mem")
    placed = (
        P(everywhere, None),
        P(everywhere),
        P(everywhere),
        P(),
        P(everywhere, None),
    )
    return jax.shard_map(
        on_device,
        mesh=chip_mesh,
        in_specs=placed,
        out_specs=(P(everywhere, None), P(everywhere)),
        check_vma=False,
    )
```

time: 290 us -> 223 us (0.77)
  waiting for transfers between devices: 126 us -> 40.4 us
  Pallas kernels: 0 us -> 37.8 us
  local copies, waits for them, and re-layouts: 40 us -> 7.79 us
  blocking collectives: 49.1 us -> 77.2 us
  between operations: 15 us -> 0.89 us
  starting transfers between devices: 44.2 us -> 51.6 us
  matrix products: 6.21 us -> 0 us
  other arithmetic: 9.47 us -> 4.02 us
    all_to_all x3 -> x0, waiting for transfers between devices: 63.4 us -> none  [the longest x1 47 us: on_device(): lax.all_to_all(outgoing.reshape(members, capacity, width), 'mem', split_a...]
    all_to_all x1 -> x2, blocking collectives: 22 us -> 77.2 us  [the longest x1 58.8 us: on_device(): lax.all_to_all(payload, 'mem', split_axis=0, concat_axis=0, tiled=True)]
    ppermute x0 -> x12, starting transfers between devices: none -> 51.6 us  [the longest x8 30.8 us: onward(): return lax.ppermute(a, ('x', 'core'), around)]
    all_to_all x3 -> x0, starting transfers between devices: 44.1 us -> none  [the longest x1 24 us: on_device(): lax.all_to_all(first_ids.reshape(members, capacity), 'mem', split_axis=0,...]
    reduce_scatter x1 -> x0, waiting for transfers between devices: 41.1 us -> none  [on_device(): lax.psum_scatter(jnp.dot(table, received, preferred_element_type=jnp.floa...]
    ppermute x0 -> x12, waiting for transfers between devices: none -> 40.4 us  [the longest x8 38 us: onward(): return lax.ppermute(a, ('x', 'core'), around)]
    pallas_call x0 -> x10, Pallas kernels: none -> 37.8 us  [call(): pl.pallas_call(kernel, in_specs=specs, out_shape=out_shape, compiler_para...]
    unnamed x1 -> x0, blocking collectives: 27.1 us -> none
  transfers between devices with their start and end apart: 5 -> 12, of which waited for: 5 -> 8; matrix products, arithmetic and copies ran while one was open for 5% -> 2% of each run, Pallas kernels for 0% -> 8%
where the time goes in v2:
time: 223 us; the launch traced here: 220 us
  blocking collectives  77.2 us (35%)
  starting transfers between devices  51.6 us (23%)
  waiting for transfers between devices  40.4 us (18%)
  Pallas kernels  37.8 us (17%)
  local copies, waits for them, and re-layouts  7.79 us (3%)
  other arithmetic  4.02 us (2%)
    all_to_all x1, blocking collectives, on_device(): lax.all_to_all(payload, 'mem', split_axis=0, concat_axis=0, tiled=True)  58.8 us
    ppermute x8, waiting for transfers between devices, onward(): return lax.ppermute(a, ('x', 'core'), around)  38 us
    pallas_call x10, Pallas kernels, call(): pl.pallas_call(kernel, in_specs=specs, out_shape=out_shape, compiler_para...  37.8 us
    ppermute x8, starting transfers between devices, onward(): return lax.ppermute(a, ('x', 'core'), around)  30.8 us
    ppermute x4, starting transfers between devices, across(): return lax.ppermute(a, 'core', [(0, 1), (1, 0)])  20.8 us
    all_to_all x1, blocking collectives, on_device(): lax.all_to_all(margin.reshape(members, 1, capacity), 'mem', split_axis=0,...  18.4 us
  transfers between devices with their start and end apart: 12, of which 8 were waited for; matrix products, arithmetic and copies ran while one was open for 2% of the time, Pallas kernels for 8%

profile of v2, /device:TPU:1, one launch (start us, length us, event | category | flops | bytes accessed | tf_op | source)
XLA Modules:
  0.0 219.7 jit_solution(9343636256027214785)
XLA Ops:
  0.6 5.3 %prepare.1 = (bf16[64,88,128]{2,1,0:T(8,128)(2,1)}, s32[1,512]{1,0:T(1,128)}) custom-call(s32[1,512]{1,0:T(1,128)} %bitcast.14, s32[1,512]{1,0:T(1,128)} %bitcast.15, s32[1024,128]{1,0:T(8,128)} %bitcast.13, bf16[512,1024]{1,0:T(8,128)(2,1)} %embeddings.1), custom_call_target="tpu_custom_call" | custom-call | flops 2147483648 | bytes 2097152 | tf_op jit(solution)/shard_map/prepare/pallas_call | solution.py:45
  5.9 58.8 %all_to_all.10.arrived = bf16[64,88,128]{2,1,0:T(8,128)(2,1)} all-to-all(bf16[64,88,128]{2,1,0:T(8,128)(2,1)} %get-tuple-element.16), channel_id=1, replica_groups=mesh['x'=8,'core'=2,'mem'=64] {'mem'}, dimensions={0} | all-to-all | bytes 2883584 | tf_op jit(solution)/shard_map/all_to_all | solution.py:285
  64.7 3.2 %unpack.1.box.own = bf16[656,1024]{1,0:T(8,128)(2,1)} custom-call(bf16[64,88,128]{2,1,0:T(8,128)(2,1)} %all_to_all.10.arrived), custom_call_target="tpu_custom_call" | custom-call | flops 16777216 | bytes 2097152 | tf_op jit(solution)/shard_map/unpack/pallas_call | solution.py:45
  67.9 6.1 %collective-permute-start = (bf16[656,1024]{1,0:T(8,128)(2,1)}, bf16[656,1024]{1,0:T(8,128)(2,1)S(1)}, u32[]{:S(2)}, u32[]{:S(2)}) collective-permute-start(bf16[656,1024]{1,0:T(8,128)(2,1)} %unpack.1.box.own), channel_id=1, source_target_pairs={{0,64},{64,0},{1,65},{65,1},{2,66},{66,2},{3,67},{67,3},{4,68},{68... | collective-permute-start | bytes 4030472 | tf_op jit(solution)/shard_map/ppermute | solution.py:269
  74.7 4.5 %sums.2 = (bf16[272,512]{1,0:T(8,128)(2,1)}, bf16[272,1024]{1,0:T(8,128)(2,1)}, bf16[272,1024]{1,0:T(8,128)(2,1)}, bf16[272,1024]{1,0:T(8,128)(2,1)}, bf16[272,512]{1,0:T(8,128)(2,1)}) custom-call(s32[2]{0:T(128)} %pad_add_fusion.where, bf16[656,1024]{1,0:T(8,128)(2,1)} %unpack.1.box.own), custom_call_target="tpu_custom_call" | custom-call | flops 2147483648 | bytes 2097152 | tf_op jit(solution)/shard_map/sums/pallas_call | solution.py:45
  80.3 4.9 %sums.3 = (bf16[272,512]{1,0:T(8,128)(2,1)}, bf16[272,1024]{1,0:T(8,128)(2,1)}, bf16[272,1024]{1,0:T(8,128)(2,1)}, bf16[272,1024]{1,0:T(8,128)(2,1)}, bf16[272,512]{1,0:T(8,128)(2,1)}) custom-call(s32[2]{0:T(128)} %pad_add_fusion.where, bf16[656,1024]{1,0:T(8,128)(2,1)} %copy-done.9, bf16[272,512]{1,0:T(8,128)(2,1)} %get-tuple-element.17.refs_0_, ...), custom_call_target="tpu_custom_call" | custom-call | flops 2147483648 | bytes 2097152 | tf_op jit(solution)/shard_map/sums/pallas_call | solution.py:45
  85.2 4.5 %collective-permute-start.1 = (bf16[272,512]{1,0:T(8,128)(2,1)}, bf16[272,512]{1,0:T(8,128)(2,1)S(1)}, u32[]{:S(2)}, u32[]{:S(2)}) collective-permute-start(bf16[272,512]{1,0:T(8,128)(2,1)} %get-tuple-element.26), channel_id=1, source_target_pairs={{0,128},{128,256},{256,384},{384,512},{512,640},{640,768},{768,896... | collective-permute-start | bytes 835592 | tf_op jit(solution)/shard_map/ppermute | solution.py:266
  94.6 5.1 %collective-permute-start.2 = (bf16[272,1024]{1,0:T(8,128)(2,1)S(1)}, bf16[272,1024]{1,0:T(8,128)(2,1)S(1)}, u32[]{:S(2)}, u32[]{:S(2)}) collective-permute-start(bf16[272,1024]{1,0:T(8,128)(2,1)S(1)} %pad_maximum_fusion), channel_id=1, source_target_pairs={{0,128},{128,256},{256,384},{384,512},{512,640},{640,768},{768,896... | collective-permute-start | bytes 1671176 | tf_op jit(solution)/shard_map/ppermute | solution.py:266
  99.6 6.5 %collective-permute-done.2 = bf16[272,1024]{1,0:T(8,128)(2,1)S(1)} collective-permute-done((bf16[272,1024]{1,0:T(8,128)(2,1)S(1)}, bf16[272,1024]{1,0:T(8,128)(2,1)S(1)}, u32[]{:S(2)}, u32[]{:S(2)}) %collective-permute-start.2) | collective-permute-done | bytes 557088 | tf_op jit(solution)/shard_map/ppermute | solution.py:266
  106.3 5.0 %collective-permute-start.3 = (bf16[272,1024]{1,0:T(8,128)(2,1)S(1)}, bf16[272,1024]{1,0:T(8,128)(2,1)S(1)}, u32[]{:S(2)}, u32[]{:S(2)}) collective-permute-start(bf16[272,1024]{1,0:T(8,128)(2,1)S(1)} %add_convert_fusion.1), channel_id=1, source_target_pairs={{0,128},{128,256},{256,384},{384,512},{512,640},{640,768},{768,896... | collective-permute-start | bytes 1671176 | tf_op jit(solution)/shard_map/ppermute | solution.py:266
  111.3 6.5 %collective-permute-done.3 = bf16[272,1024]{1,0:T(8,128)(2,1)S(1)} collective-permute-done((bf16[272,1024]{1,0:T(8,128)(2,1)S(1)}, bf16[272,1024]{1,0:T(8,128)(2,1)S(1)}, u32[]{:S(2)}, u32[]{:S(2)}) %collective-permute-start.3) | collective-permute-done | bytes 557088 | tf_op jit(solution)/shard_map/ppermute | solution.py:266
  118.0 5.0 %collective-permute-start.4 = (bf16[272,1024]{1,0:T(8,128)(2,1)S(1)}, bf16[272,1024]{1,0:T(8,128)(2,1)S(1)}, u32[]{:S(2)}, u32[]{:S(2)}) collective-permute-start(bf16[272,1024]{1,0:T(8,128)(2,1)S(1)} %add_convert_fusion), channel_id=1, source_target_pairs={{0,128},{128,256},{256,384},{384,512},{512,640},{640,768},{768,896... | collective-permute-start | bytes 1671176 | tf_op jit(solution)/shard_map/ppermute | solution.py:266
  123.0 6.5 %collective-permute-done.4 = bf16[272,1024]{1,0:T(8,128)(2,1)S(1)} collective-permute-done((bf16[272,1024]{1,0:T(8,128)(2,1)S(1)}, bf16[272,1024]{1,0:T(8,128)(2,1)S(1)}, u32[]{:S(2)}, u32[]{:S(2)}) %collective-permute-start.4) | collective-permute-done | bytes 557088 | tf_op jit(solution)/shard_map/ppermute | solution.py:266
  129.7 7.0 %collective-permute-start.5 = (bf16[272,1024]{1,0:T(8,128)(2,1)S(1)}, bf16[272,1024]{1,0:T(8,128)(2,1)S(1)}, u32[]{:S(2)}, u32[]{:S(2)}) collective-permute-start(bf16[272,1024]{1,0:T(8,128)(2,1)S(1)} %pad_maximum_fusion.1.here), channel_id=1, source_target_pairs={{0,64},{64,0},{1,65},{65,1},{2,66},{66,2},{3,67},{67,3},{4,68},{68... | collective-permute-start | bytes 1671176 | tf_op jit(solution)/shard_map/ppermute | solution.py:269
  146.5 8.5 %collective-permute-done.7.block = bf16[256,1024]{1,0:T(8,128)(2,1)S(1)} collective-permute-done((bf16[256,1024]{1,0:T(8,128)(2,1)}, bf16[256,1024]{1,0:T(8,128)(2,1)S(1)}, u32[]{:S(2)}, u32[]{:S(2)}) %collective-permute-start.7) | collective-permute-done | bytes 524320 | tf_op jit(solution)/shard_map/ppermute | solution.py:266
  157.8 7.4 %collective-permute-done.8.block = bf16[256,1024]{1,0:T(8,128)(2,1)S(1)} collective-permute-done((bf16[256,1024]{1,0:T(8,128)(2,1)S(1)}, bf16[256,1024]{1,0:T(8,128)(2,1)S(1)}, u32[]{:S(2)}, u32[]{:S(2)}) %collective-permute-start.8) | collective-permute-done | bytes 524320 | tf_op jit(solution)/shard_map/ppermute | solution.py:266
  165.2 3.9 %collective-permute-start.9 = (bf16[256,1024]{1,0:T(8,128)(2,1)S(1)}, bf16[256,1024]{1,0:T(8,128)(2,1)S(1)}, u32[]{:S(2)}, u32[]{:S(2)}) collective-permute-start(bf16[256,1024]{1,0:T(8,128)(2,1)S(1)} %collective-permute-done.8.block), channel_id=1, source_target_pairs={{0,128},{128,256},{256,384},{384,512},{512,640},{640,768},{768,896... | collective-permute-start | bytes 1572872 | tf_op jit(solution)/shard_map/ppermute | solution.py:266
  170.8 3.1 %score.5.refs_0_ = f32[2,640]{1,0:T(2,128)} custom-call(s32[2]{0:T(128)} %pad_add_fusion.where, bf16[656,1024]{1,0:T(8,128)(2,1)} %unpack.1.box.own, bf16[656,1024]{1,0:T(8,128)(2,1)} %copy-done.9, bf16[256,512]{1,0:T(8,128)(2,1)} %slice.55.block), custom_call_target="tpu_custom_call" | custom-call | flops 2147483648 | bytes 2097152 | tf_op jit(solution)/shard_map/score/pallas_call | solution.py:45
  173.9 3.6 %score.6.refs_0_ = f32[2,640]{1,0:T(2,128)} custom-call(s32[2]{0:T(128)} %pad_add_fusion.where, bf16[656,1024]{1,0:T(8,128)(2,1)} %unpack.1.box.own, bf16[656,1024]{1,0:T(8,128)(2,1)} %copy-done.9, bf16[256,1024]{1,0:T(8,128)(2,1)} %copy-done.11, f32[2,640]{1,0:T(2,128)} %score.5.refs_0_), custom_call_target="tpu_custom_call" | custom-call | flops 2147483648 | bytes 2097152 | tf_op jit(solution)/shard_map/score/pallas_call | solution.py:45
  180.1 3.6 %score.7.refs_0_ = f32[2,640]{1,0:T(2,128)} custom-call(s32[2]{0:T(128)} %pad_add_fusion.where, bf16[656,1024]{1,0:T(8,128)(2,1)} %unpack.1.box.own, bf16[656,1024]{1,0:T(8,128)(2,1)} %copy-done.9, bf16[256,1024]{1,0:T(8,128)(2,1)} %copy-done.10, f32[2,640]{1,0:T(2,128)} %score.6.refs_0_), custom_call_target="tpu_custom_call" | custom-call | flops 2147483648 | bytes 2097152 | tf_op jit(solution)/shard_map/score/pallas_call | solution.py:45
  183.7 3.6 %score.8.refs_0_ = f32[2,640]{1,0:T(2,128)} custom-call(s32[2]{0:T(128)} %pad_add_fusion.where, bf16[656,1024]{1,0:T(8,128)(2,1)} %unpack.1.box.own, bf16[656,1024]{1,0:T(8,128)(2,1)} %copy-done.9, bf16[256,1024]{1,0:T(8,128)(2,1)} %copy-done.7, f32[2,640]{1,0:T(2,128)} %score.7.refs_0_), custom_call_target="tpu_custom_call" | custom-call | flops 2147483648 | bytes 2097152 | tf_op jit(solution)/shard_map/score/pallas_call | solution.py:45
  188.1 3.2 %score.9 = f32[2,640]{1,0:T(2,128)} custom-call(s32[2]{0:T(128)} %pad_add_fusion.where, bf16[656,1024]{1,0:T(8,128)(2,1)} %unpack.1.box.own, bf16[656,1024]{1,0:T(8,128)(2,1)} %copy-done.9, bf16[256,512]{1,0:T(8,128)(2,1)} %copy-done.12, f32[2,640]{1,0:T(2,128)} %score.8.refs_0_), custom_call_target="tpu_custom_call" | custom-call | flops 2147483648 | bytes 2097152 | tf_op jit(solution)/shard_map/score/pallas_call | solution.py:45
  192.0 5.8 %collective-permute-start.11 = (f32[640]{0:T(1024)S(1)}, f32[640]{0:T(1024)S(1)}, u32[]{:S(2)}, u32[]{:S(2)}) collective-permute-start(f32[640]{0:T(1024)S(1)} %get-tuple-element.30), channel_id=1, source_target_pairs={{0,64},{64,0},{1,65},{65,1},{2,66},{66,2},{3,67},{67,3},{4,68},{68... | collective-permute-start | bytes 7688 | tf_op jit(solution)/shard_map/ppermute | solution.py:269
  199.0 18.4 %all_to_all.11 = f32[64,1,10]{2,1,0:T(1,128)S(1)} all-to-all(f32[64,1,10]{2,1,0:T(1,128)S(1)} %bitcast.11), channel_id=1, replica_groups=mesh['x'=8,'core'=2,'mem'=64] {'mem'}, dimensions={0} | all-to-all | bytes 5120 | tf_op jit(solution)/shard_map/all_to_all | solution.py:354
  (61 shorter events, 29.0 us)
Async XLA Ops:
  67.9 11.3 %collective-permute-start = (bf16[656,1024]{1,0:T(8,128)(2,1)}, bf16[656,1024]{1,0:T(8,128)(2,1)S(1)}, u32[]{:S(2)}, u32[]{:S(2)}) collective-permute-start(bf16[656,1024]{1,0:T(8,128)(2,1)} %unpack.1.box.own), channel_id=1, source_target_pairs={{0,64},{64,0},{1,65},{65,1},{2,66},{66,2},{3,67},{67,3},{4,68},{68... | collective-permute-start | bytes 4030472 | tf_op jit(solution)/shard_map/ppermute | solution.py:269
  79.2 1.1 copy-start.9
  85.2 8.3 %collective-permute-start.1 = (bf16[272,512]{1,0:T(8,128)(2,1)}, bf16[272,512]{1,0:T(8,128)(2,1)S(1)}, u32[]{:S(2)}, u32[]{:S(2)}) collective-permute-start(bf16[272,512]{1,0:T(8,128)(2,1)} %get-tuple-element.26), channel_id=1, source_target_pairs={{0,128},{128,256},{256,384},{384,512},{512,640},{640,768},{768,896... | collective-permute-start | bytes 835592 | tf_op jit(solution)/shard_map/ppermute | solution.py:266
  90.7 15.4 %copy-start.3 = (bf16[272,1024]{1,0:T(8,128)(2,1)S(1)}, bf16[272,1024]{1,0:T(8,128)(2,1)}, u32[]{:S(2)}) copy-start(bf16[272,1024]{1,0:T(8,128)(2,1)} %get-tuple-element.24) | copy-start | bytes 1671172
  94.6 23.2 %copy-start.2 = (bf16[272,1024]{1,0:T(8,128)(2,1)S(1)}, bf16[272,1024]{1,0:T(8,128)(2,1)}, u32[]{:S(2)}) copy-start(bf16[272,1024]{1,0:T(8,128)(2,1)} %get-tuple-element.23) | copy-start | bytes 1671172
  94.6 11.5 %collective-permute-start.2 = (bf16[272,1024]{1,0:T(8,128)(2,1)S(1)}, bf16[272,1024]{1,0:T(8,128)(2,1)S(1)}, u32[]{:S(2)}, u32[]{:S(2)}) collective-permute-start(bf16[272,1024]{1,0:T(8,128)(2,1)S(1)} %pad_maximum_fusion), channel_id=1, source_target_pairs={{0,128},{128,256},{256,384},{384,512},{512,640},{640,768},{768,896... | collective-permute-start | bytes 1671176 | tf_op jit(solution)/shard_map/ppermute | solution.py:266
  106.3 11.5 %collective-permute-start.3 = (bf16[272,1024]{1,0:T(8,128)(2,1)S(1)}, bf16[272,1024]{1,0:T(8,128)(2,1)S(1)}, u32[]{:S(2)}, u32[]{:S(2)}) collective-permute-start(bf16[272,1024]{1,0:T(8,128)(2,1)S(1)} %add_convert_fusion.1), channel_id=1, source_target_pairs={{0,128},{128,256},{256,384},{384,512},{512,640},{640,768},{768,896... | collective-permute-start | bytes 1671176 | tf_op jit(solution)/shard_map/ppermute | solution.py:266
  117.8 11.7 %copy-start.4 = (bf16[272,512]{1,0:T(8,128)(2,1)S(1)}, bf16[272,512]{1,0:T(8,128)(2,1)}, u32[]{:S(2)}) copy-start(bf16[272,512]{1,0:T(8,128)(2,1)} %get-tuple-element.22) | copy-start | bytes 835588
  118.0 11.5 %collective-permute-start.4 = (bf16[272,1024]{1,0:T(8,128)(2,1)S(1)}, bf16[272,1024]{1,0:T(8,128)(2,1)S(1)}, u32[]{:S(2)}, u32[]{:S(2)}) collective-permute-start(bf16[272,1024]{1,0:T(8,128)(2,1)S(1)} %add_convert_fusion), channel_id=1, source_target_pairs={{0,128},{128,256},{256,384},{384,512},{512,640},{640,768},{768,896... | collective-permute-start | bytes 1671176 | tf_op jit(solution)/shard_map/ppermute | solution.py:266
  129.5 7.2 %copy-start.5 = (bf16[128,1024]{1,0:T(8,128)(2,1)S(1)}, bf16[128,1024]{1,0:T(8,128)(2,1)}, u32[]{:S(2)}) copy-start(bf16[128,1024]{1,0:T(8,128)(2,1)} %old.1) | copy-start | bytes 786436
  129.7 10.5 %copy-start = (bf16[272,1024]{1,0:T(8,128)(2,1)}, bf16[272,1024]{1,0:T(8,128)(2,1)S(1)}, u32[]{:S(2)}) copy-start(bf16[272,1024]{1,0:T(8,128)(2,1)S(1)} %pad_maximum_fusion.1.here) | copy-start | bytes 1671172
  129.7 10.5 %collective-permute-start.5 = (bf16[272,1024]{1,0:T(8,128)(2,1)S(1)}, bf16[272,1024]{1,0:T(8,128)(2,1)S(1)}, u32[]{:S(2)}, u32[]{:S(2)}) collective-permute-start(bf16[272,1024]{1,0:T(8,128)(2,1)S(1)} %pad_maximum_fusion.1.here), channel_id=1, source_target_pairs={{0,64},{64,0},{1,65},{65,1},{2,66},{66,2},{3,67},{67,3},{4,68},{68... | collective-permute-start | bytes 1671176 | tf_op jit(solution)/shard_map/ppermute | solution.py:269
  136.7 3.4 %collective-permute-start.6 = (bf16[128,1024]{1,0:T(8,128)(2,1)S(1)}, bf16[128,1024]{1,0:T(8,128)(2,1)S(1)}, u32[]{:S(2)}, u32[]{:S(2)}) collective-permute-start(bf16[128,1024]{1,0:T(8,128)(2,1)S(1)} %copy-done.5), channel_id=1, source_target_pairs={{0,64},{64,0},{1,65},{65,1},{2,66},{66,2},{3,67},{67,3},{4,68},{68... | collective-permute-start | bytes 786440 | tf_op jit(solution)/shard_map/ppermute | solution.py:269
  140.2 0.7 copy-start.6
  140.9 0.8 copy-start.1
  144.6 10.4 %collective-permute-start.7 = (bf16[256,1024]{1,0:T(8,128)(2,1)}, bf16[256,1024]{1,0:T(8,128)(2,1)S(1)}, u32[]{:S(2)}, u32[]{:S(2)}) collective-permute-start(bf16[256,1024]{1,0:T(8,128)(2,1)} %get-tuple-element.29), channel_id=1, source_target_pairs={{0,128},{128,256},{256,384},{384,512},{512,640},{640,768},{768,896... | collective-permute-start | bytes 1572872 | tf_op jit(solution)/shard_map/ppermute | solution.py:266
  155.0 18.9 %copy-start.11 = (bf16[256,1024]{1,0:T(8,128)(2,1)}, bf16[256,1024]{1,0:T(8,128)(2,1)S(1)}, u32[]{:S(2)}) copy-start(bf16[256,1024]{1,0:T(8,128)(2,1)S(1)} %collective-permute-done.7.block) | copy-start | bytes 1572868
  155.0 10.2 %collective-permute-start.8 = (bf16[256,1024]{1,0:T(8,128)(2,1)S(1)}, bf16[256,1024]{1,0:T(8,128)(2,1)S(1)}, u32[]{:S(2)}, u32[]{:S(2)}) collective-permute-start(bf16[256,1024]{1,0:T(8,128)(2,1)S(1)} %collective-permute-done.7.block), channel_id=1, source_target_pairs={{0,128},{128,256},{256,384},{384,512},{512,640},{640,768},{768,896... | collective-permute-start | bytes 1572872 | tf_op jit(solution)/shard_map/ppermute | solution.py:266
  165.2 8.7 %copy-start.10 = (bf16[256,1024]{1,0:T(8,128)(2,1)}, bf16[256,1024]{1,0:T(8,128)(2,1)S(1)}, u32[]{:S(2)}) copy-start(bf16[256,1024]{1,0:T(8,128)(2,1)S(1)} %collective-permute-done.8.block) | copy-start | bytes 1572868
  165.2 12.3 %collective-permute-start.9 = (bf16[256,1024]{1,0:T(8,128)(2,1)S(1)}, bf16[256,1024]{1,0:T(8,128)(2,1)S(1)}, u32[]{:S(2)}, u32[]{:S(2)}) collective-permute-start(bf16[256,1024]{1,0:T(8,128)(2,1)S(1)} %collective-permute-done.8.block), channel_id=1, source_target_pairs={{0,128},{128,256},{256,384},{384,512},{512,640},{640,768},{768,896... | collective-permute-start | bytes 1572872 | tf_op jit(solution)/shard_map/ppermute | solution.py:266
  177.5 6.2 %copy-start.7 = (bf16[256,1024]{1,0:T(8,128)(2,1)}, bf16[256,1024]{1,0:T(8,128)(2,1)S(1)}, u32[]{:S(2)}) copy-start(bf16[256,1024]{1,0:T(8,128)(2,1)S(1)} %collective-permute-done.9.block) | copy-start | bytes 1572868
  177.6 9.8 %collective-permute-start.10 = (bf16[256,512]{1,0:T(8,128)(2,1)S(1)}, bf16[256,512]{1,0:T(8,128)(2,1)S(1)}, u32[]{:S(2)}, u32[]{:S(2)}) collective-permute-start(bf16[256,512]{1,0:T(8,128)(2,1)S(1)} %slice.64), channel_id=1, source_target_pairs={{0,128},{128,256},{256,384},{384,512},{512,640},{640,768},{768,896... | collective-permute-start | bytes 786440 | tf_op jit(solution)/shard_map/ppermute | solution.py:266
  187.3 31.5 %copy-start.8 = (s32[1,512]{1,0:T(1,128)S(1)}, s32[1,512]{1,0:T(1,128)}, u32[]{:S(2)}) copy-start(s32[1,512]{1,0:T(1,128)} %get-tuple-element.28) | copy-start | bytes 6148
  192.0 6.6 %collective-permute-start.11 = (f32[640]{0:T(1024)S(1)}, f32[640]{0:T(1024)S(1)}, u32[]{:S(2)}, u32[]{:S(2)}) collective-permute-start(f32[640]{0:T(1024)S(1)} %get-tuple-element.30), channel_id=1, source_target_pairs={{0,64},{64,0},{1,65},{65,1},{2,66},{66,2},{3,67},{67,3},{4,68},{68... | collective-permute-start | bytes 7688 | tf_op jit(solution)/shard_map/ppermute | solution.py:269
  (1 other events, 0.7 us)

commit v3 on v2

v3 whole, which is shorter than its diff:
```python
import functools

import jax
import jax.numpy as jnp
from jax import lax
from jax.experimental import pallas as pl
from jax.experimental.pallas import tpu as pltpu
from jax.sharding import Mesh
from jax.sharding import PartitionSpec as P

F32 = jnp.float32
BF16 = jnp.bfloat16
LANES = 128
TILE = 8
NOTES = 16
CUT = 5
SMEM = pl.BlockSpec(memory_space=pltpu.SMEM)
VMEM = pl.BlockSpec(memory_space=pltpu.VMEM)


def rows_of(shape):
    return lax.broadcasted_iota(jnp.int32, shape, 0).astype(F32)


def lanes_of(shape):
    return lax.broadcasted_iota(jnp.int32, shape, 1).astype(F32)


def hot(condition):
    return jnp.where(condition, 1.0, 0.0).astype(BF16)


def dot(a, b, contract):
    return lax.dot_general(a, b, (contract, ((), ())), preferred_element_type=F32)


def whole(a, size):
    return jnp.floor((a + 0.5) * (1.0 / size))


def call(kernel, name, out_shape, flops, *args, scalars=None):
    specs = [VMEM] * len(args)
    if scalars is not None:
        specs = [SMEM] + specs
        args = (scalars,) + args
    return pl.pallas_call(
        kernel,
        in_specs=specs,
        out_shape=out_shape,
        compiler_params=pltpu.CompilerParams(vmem_limit_bytes=56 * 2**20),
        cost_estimate=pl.CostEstimate(flops=flops, bytes_accessed=2**21, transcendentals=0),
        name=name,
    )(*args)


def prepare(members, capacity, cut, first, second, table, embeddings, one, two, place):
    vectors = first.shape[1]
    slots = table[...]
    local = slots & (LANES - 1)
    owner = (slots // LANES) & (members - 1)
    group = slots // (LANES * members)
    planes = jnp.concatenate([local, owner, group], axis=1).astype(F32).astype(BF16)

    def look_up(ids):
        row = (ids // LANES).astype(F32)
        lane = (ids & (LANES - 1)).astype(F32)
        found = dot(planes, hot(rows_of((table.shape[0], vectors)) == row), ((0,), (0,)))
        mask = rows_of((LANES, vectors)) == lane

        def pick(k):
            return jnp.sum(
                jnp.where(mask, found[k * LANES : (k + 1) * LANES], 0.0), axis=0, keepdims=True
            )

        return pick(0), pick(1), pick(2)

    first_local, first_owner, first_group = look_up(first[...])
    second_local, _, second_group = look_up(second[...])
    is_owner = rows_of((members, vectors)) == first_owner
    before = hot(rows_of((vectors, vectors)) < lanes_of((vectors, vectors)))
    earlier = dot(hot(is_owner), before, ((1,), (0,)))
    rank = jnp.sum(jnp.where(is_owner, earlier, 0.0), axis=0, keepdims=True)
    place[...] = (first_owner * capacity + rank).astype(jnp.int32)
    spot = jnp.where(rank < TILE, first_owner * TILE + rank, rank * members + first_owner)
    order = hot(rows_of((members * capacity, vectors)) == spot)
    packed = dot(order, embeddings[...], ((1,), (0,)))
    ranked = rows_of((16, vectors)) == rank
    digits = [first_group + 1.0, first_local, second_group + 1.0, second_local]
    spread = [jnp.where(ranked, digit, 0.0) for digit in digits]
    spread.append(jnp.zeros((LANES - 16 * len(digits), vectors), F32))
    labels = dot(hot(is_owner), jnp.concatenate(spread, axis=0).astype(BF16), ((1,), (1,)))
    for out, start, stop, tail in (
        (one, 0, cut, [labels]),
        (two, cut, embeddings.shape[1] // LANES, []),
    ):
        pieces = [
            packed[: TILE * members, j * LANES : (j + 1) * LANES].reshape(members, TILE, LANES)
            for j in range(start, stop)
        ]
        rest = [
            packed[p * members : (p + 1) * members, j * LANES : (j + 1) * LANES]
            for p in range(TILE, capacity)
            for j in range(start, stop)
        ] + tail
        rest += [jnp.zeros((members, LANES), F32)] * (-len(rest) % TILE)
        for k in range(0, len(rest), TILE):
            pieces.append(jnp.stack(rest[k : k + TILE], axis=1))
        out[...] = jnp.concatenate(pieces, axis=1).astype(BF16)


def payload_rows(capacity, parts, labels):
    rows = capacity * parts + labels
    return rows + -rows % TILE


def unpack(capacity, labelled, arrived, box):
    members = arrived.shape[0]
    count = members * capacity
    parts = box.shape[1] // LANES
    values = arrived[...].astype(F32)
    for j in range(parts):
        at = slice(j * LANES, (j + 1) * LANES)
        box[: TILE * members, at] = (
            values[:, j * TILE : (j + 1) * TILE].reshape(TILE * members, LANES).astype(BF16)
        )
        for p in range(TILE, capacity):
            box[p * members : (p + 1) * members, at] = values[:, p * parts + j].astype(BF16)
    if not labelled:
        return
    labels = values[:, capacity * parts].astype(BF16)
    vector = lanes_of((members, count))
    from_member = jnp.where(
        vector < TILE * members, whole(vector, TILE), vector - members * whole(vector, members)
    )
    found = dot(labels, hot(rows_of((members, count)) == from_member), ((0,), (0,)))
    vector = lanes_of((16, count))
    rank = jnp.where(
        vector < TILE * members, vector - TILE * whole(vector, TILE), whole(vector, members)
    )
    ranked = rows_of((16, count)) == rank
    rows = [
        jnp.sum(jnp.where(ranked, found[k * 16 : (k + 1) * 16], 0.0), axis=0, keepdims=True)
        for k in range(4)
    ]
    notes = jnp.concatenate(rows + [jnp.zeros((NOTES - 4, count), F32)], axis=0)
    if count < box.shape[1]:
        notes = jnp.concatenate(
            [notes, jnp.zeros((NOTES, box.shape[1] - count), F32)], axis=1
        )
    box[count : count + NOTES] = notes.astype(BF16)


def index(chips, where, notes, k, ahead):
    group = notes[2 * k : 2 * k + 1] - 1.0
    local = notes[2 * k + 1 : 2 * k + 2]
    chip = whole(group, 2)
    core = group - 2.0 * chip
    if ahead:
        chip = chip - where[0].astype(F32)
        chip = jnp.where(chip < 0.0, chip + chips, chip)
    mine = (group >= 0.0) & (core == where[1].astype(F32))
    return jnp.where(mine, chip * LANES + local, -1.0)


def sums_one(chips, count, where, box, *refs):
    earlier, out = refs[:-1], refs[-1]
    width = box.shape[1]
    notes = box[count : count + NOTES, :count].astype(F32)
    at = index(chips, where, notes, 0, False)
    ones = jnp.ones((NOTES, count), BF16)
    for pair in range(0, chips, 2):
        table = hot(rows_of((2 * LANES, count)) + pair * LANES == at)
        total = dot(table, box[0:count, :], ((1,), (0,)))
        hits = dot(ones, table, ((1,), (1,)))
        high = whole(hits, 256)
        left = hits - 256.0 * high
        middle = whole(left, 16)
        low = left - 16.0 * middle
        for n in range(2):
            half = slice(n * LANES, (n + 1) * LANES)
            digits = [low[:, half], middle[:, half], high[:, half]]
            digits.append(jnp.zeros((NOTES, width - 3 * LANES), F32))
            block = jnp.concatenate([total[half], jnp.concatenate(digits, axis=1)], axis=0)
            to = slice((pair + n) * (LANES + NOTES), (pair + n + 1) * (LANES + NOTES))
            if earlier:
                block = block + earlier[0][to].astype(F32)
            out[to] = block.astype(BF16)


def sums_two(chips, count, where, box, notes_box, *refs):
    earlier, outs = refs[: len(refs) - chips - 1], refs[len(refs) - chips - 1 :]
    notes = notes_box[count : count + NOTES, :count].astype(F32)
    at = index(chips, where, notes, 0, True)
    cut = outs[chips // 2].shape[1]
    for pair in range(0, chips, 2):
        table = hot(rows_of((2 * LANES, count)) + pair * LANES == at)
        total = dot(table, box[...], ((1,), (0,)))
        for n in range(2):
            block = total[n * LANES : (n + 1) * LANES]
            places = [(pair + n, block)]
            if pair + n == chips // 2:
                places = [(pair + n, block[:, :cut]), (chips, block[:, cut:])]
            for place, value in places:
                if earlier:
                    value = value + earlier[place][...].astype(F32)
                outs[place][...] = value.astype(BF16)


def counts_of(digits):
    identity = hot(rows_of((LANES, LANES)) == lanes_of((LANES, LANES)))

    def column(k):
        return dot(identity, digits[:, k * LANES : (k + 1) * LANES], ((1,), (1,)))[:, 0:1]

    return column(0) + 16.0 * column(1) + 256.0 * column(2)


def refit_one(summed, old, fresh):
    width = summed.shape[1]
    counts = counts_of(summed[LANES : LANES + NOTES])
    total = summed[0:LANES].astype(F32) + old[:, :width].astype(F32)
    fresh[...] = (total / (counts + 1.0)).astype(BF16)


def refit_two(summed, fresh_one, mine, above, below, old, fresh_two, fresh):
    width = summed.shape[1]
    counts = counts_of(summed[LANES : LANES + NOTES])
    total = mine[...].astype(F32) + above[...].astype(F32) + below[...].astype(F32)
    total = total + old[:, width:].astype(F32)
    part = (total / (counts + 1.0)).astype(BF16)
    fresh_two[...] = part
    fresh[:, :width] = fresh_one[...]
    fresh[:, width:] = part


def score(chips, count, ahead, places, where, notes_own, notes_other, own, other, *refs):
    blocks, out = refs[: len(places)], refs[-1]
    before = refs[len(places) : -1]
    lists = 2 * LANES
    items = []
    for start, block in zip(places, blocks):
        rows = block.shape[0]
        items += [(start + r, block, r) for r in range(0, rows, LANES)]
    totals = [jnp.zeros((1, count), F32)] * 2
    for k in range(0, len(items), 2):
        pair = items[k : k + 2]
        values = jnp.concatenate([block[r : r + LANES] for _, block, r in pair], axis=0)
        size = jnp.sum(values.astype(F32) ** 2, axis=1, keepdims=True)
        lists = LANES * len(pair)
        row = rows_of((lists, count))
        if len(pair) == 2:
            row = jnp.where(row < LANES, row + pair[0][0], row + (pair[1][0] - LANES))
        else:
            row = row + pair[0][0]
        for n, (notes_box, box) in enumerate(((notes_own, own), (notes_other, other))):
            notes = notes_box[count : count + NOTES, :count].astype(F32)
            distance = size - 2.0 * dot(values, box[0:count, :], ((1,), (1,)))
            is_first = row == index(chips, where, notes, 0, ahead)
            is_second = row == index(chips, where, notes, 1, ahead)
            totals[n] = totals[n] + jnp.sum(
                jnp.where(is_second, distance, 0.0) - jnp.where(is_first, distance, 0.0),
                axis=0,
                keepdims=True,
            )
    total = jnp.concatenate(totals, axis=0)
    for earlier in before:
        total = total + earlier[...]
    out[...] = total


def shifted(axis, size, step):
    pairs = [(i, (i + step) % size) for i in range(size)]
    return lambda a: lax.ppermute(a, axis, pairs)


def add(a, b):
    return (a.astype(F32) + b.astype(F32)).astype(BF16)


def ring_sum(up, down, blocks):
    cut = blocks[4].shape[1]
    above = up(blocks[4])
    below = down(blocks[8])
    above = up(jnp.concatenate([add(blocks[3][:, :cut], above), blocks[3][:, cut:]], axis=1))
    below = down(jnp.concatenate([blocks[5][:, :cut], add(blocks[5][:, cut:], below)], axis=1))
    above = up(add(blocks[2], above))
    below = down(add(blocks[6], below))
    above = up(add(blocks[1], above))
    below = down(add(blocks[7], below))
    return blocks[0], above, below


def ring_gather(up, down, cut, block):
    above, below = [block], [block]
    for _ in range(3):
        above.append(up(above[-1]))
        below.append(down(below[-1]))
    far = jnp.concatenate([up(above[3][:, :cut]), down(below[3][:, cut:])], axis=1)
    return [block, below[1], below[2], below[3], far, above[3], above[2], above[1]]


def on_device(embeddings, assignment, second_choice, list_slot, old_centroids):
    vectors, width = embeddings.shape
    lists = old_centroids.shape[0]
    members = lax.axis_size("mem")
    chips = lax.axis_size("x")
    capacity = vectors // members + 2
    count = members * capacity
    parts = width // LANES
    cut = CUT
    wide, narrow = cut * LANES, width - cut * LANES
    up = shifted("x", chips, 1)
    down = shifted("x", chips, -1)
    across = shifted("core", 2, 1)

    def shape(*dims, kind=BF16):
        return jax.ShapeDtypeStruct(dims, kind)

    def exchange(a):
        return lax.all_to_all(a, "mem", split_axis=0, concat_axis=0, tiled=True)

    where = jnp.stack([lax.axis_index("x"), lax.axis_index("core")]).astype(jnp.int32)
    sent_one, sent_two, place = call(
        functools.partial(prepare, members, capacity, cut),
        "prepare",
        (
            shape(members, payload_rows(capacity, cut, 1), LANES),
            shape(members, payload_rows(capacity, parts - cut, 0), LANES),
            shape(1, vectors, kind=jnp.int32),
        ),
        2**31,
        assignment.reshape(1, vectors),
        second_choice.reshape(1, vectors),
        list_slot.reshape(-1, LANES),
        embeddings,
    )
    arrived_one = exchange(sent_one)
    arrived_two = exchange(sent_two)

    own = call(
        functools.partial(unpack, capacity, True),
        "unpack",
        shape(count + NOTES, wide),
        2**24,
        arrived_one,
    )
    other = across(own)
    kernel = functools.partial(sums_one, chips, count)
    block = shape(chips * (lists + NOTES), wide)
    sums = call(kernel, "sums_one", block, 2**31, own, scalars=where)
    sums = call(kernel, "sums_one", block, 2**31, other, sums, scalars=where)
    summed = lax.psum_scatter(sums, "x", scatter_dimension=0, tiled=True)

    own_two = call(
        functools.partial(unpack, capacity, False), "unpack", shape(count, narrow), 2**24, arrived_two
    )
    other_two = across(own_two)
    kernel = functools.partial(sums_two, chips, count)
    far = (narrow // LANES + 1) // 2 * LANES
    outs = [shape(lists, far if k == chips // 2 else narrow) for k in range(chips)]
    outs.append(shape(lists, narrow - far))
    blocks = call(kernel, "sums_two", outs, 2**31, own_two, own, scalars=where)
    blocks = call(kernel, "sums_two", outs, 2**31, other_two, other, *blocks, scalars=where)
    mine, above, below = ring_sum(up, down, blocks)

    fresh_one = call(refit_one, "refit", shape(lists, wide), 2**24, summed, old_centroids)
    all_one = lax.all_gather(fresh_one, "x", axis=0, tiled=True)
    fresh_two, fresh = call(
        refit_two,
        "refit",
        (shape(lists, narrow), shape(lists, width)),
        2**24,
        summed,
        fresh_one,
        mine,
        above,
        below,
        old_centroids,
    )
    gathered = ring_gather(up, down, far, fresh_two)

    def scored(ahead, places, a, b, *rest):
        return call(
            functools.partial(score, chips, count, ahead, places),
            "score",
            shape(2, count, kind=F32),
            2**31,
            own,
            other,
            a,
            b,
            *rest,
            scalars=where,
        )

    near = [0, 1, 7, 2, 6]
    last = [3, 5, 4]
    total = scored(
        True, [k * LANES for k in near], own_two, other_two, *[gathered[k] for k in near]
    )
    total = scored(False, [0], own, other, all_one, total)
    total = scored(
        True, [k * LANES for k in last], own_two, other_two, *[gathered[k] for k in last], total
    )
    margin = (total[0] + across(total[1])) * (1.0 / width)
    margin = jnp.concatenate(
        [
            margin[: TILE * members].reshape(members, TILE),
            margin[TILE * members :].reshape(capacity - TILE, members).T,
        ],
        axis=1,
    )
    returned = exchange(margin.reshape(members, 1, capacity))
    spots = jnp.arange(count, dtype=jnp.int32)
    margins = jnp.sum(
        jnp.where(place.reshape(vectors, 1) == spots[None, :], returned.reshape(1, count), 0.0),
        axis=1,
    )
    return fresh, margins


def solution(mesh):
    groups, members = mesh.devices.shape
    chip_mesh = Mesh(mesh.devices.reshape(groups // 2, 2, members), ("x", "core", "mem"))
    everywhere = ("x", "core", "mem")
    placed = (
        P(everywhere, None),
        P(everywhere),
        P(everywhere),
        P(),
        P(everywhere, None),
    )
    return jax.shard_map(
        on_device,
        mesh=chip_mesh,
        in_specs=placed,
        out_specs=(P(everywhere, None), P(everywhere)),
        check_vma=False,
    )
```

time: 223 us -> 237 us (1.063)
  waiting for transfers between devices: 40.4 us -> 10.1 us
  starting transfers between devices: 51.6 us -> 68.4 us
  between operations: 0.89 us -> 14.5 us
  blocking collectives: 77.2 us -> 90.3 us
  Pallas kernels: 37.8 us -> 41.6 us
    ppermute x12 -> x19, waiting for transfers between devices: 40.4 us -> 10.1 us  [shifted(): return lambda a: lax.ppermute(a, axis, pairs)]
    ppermute x12 -> x19, starting transfers between devices: 51.6 us -> 68.3 us  [shifted(): return lambda a: lax.ppermute(a, axis, pairs)]
    all_to_all x2 -> x3, blocking collectives: 77.2 us -> 90.3 us  [exchange(): return lax.all_to_all(a, 'mem', split_axis=0, concat_axis=0, tiled=True)]
    pallas_call x10 -> x12, Pallas kernels: 37.8 us -> 41.6 us  [call(): pl.pallas_call(kernel, in_specs=specs, out_shape=out_shape, compiler_para...]
  transfers between devices with their start and end apart: 12 -> 21, of which waited for: 8 -> 6; matrix products, arithmetic and copies ran while one was open for 2% -> 2% of each run, Pallas kernels for 8% -> 8%
where the time goes in v3:
time: 237 us; the launch traced here: 235 us
  blocking collectives  90.3 us (38%)
  starting transfers between devices  68.4 us (29%)
  Pallas kernels  41.6 us (18%)
  between operations  14.5 us (6%)
  waiting for transfers between devices  10.1 us (4%)
  local copies, waits for them, and re-layouts  6.64 us (3%)
  other arithmetic  3.84 us (2%)
    all_to_all x3, blocking collectives, exchange(): return lax.all_to_all(a, 'mem', split_axis=0, concat_axis=0, tiled=True)  90.3 us
    ppermute x19, starting transfers between devices, shifted(): return lambda a: lax.ppermute(a, axis, pairs)  68.3 us
    pallas_call x12, Pallas kernels, call(): pl.pallas_call(kernel, in_specs=specs, out_shape=out_shape, compiler_para...  41.6 us
    ppermute x19, waiting for transfers between devices, shifted(): return lambda a: lax.ppermute(a, axis, pairs)  10.1 us
  transfers between devices with their start and end apart: 21, of which 6 were waited for; matrix products, arithmetic and copies ran while one was open for 2% of the time, Pallas kernels for 8%

profile of v3, /device:TPU:1, one launch (start us, length us, event | category | flops | bytes accessed | tf_op | source)
XLA Modules:
  0.0 235.4 jit_solution(15451681524383883119)
XLA Ops:
  7.2 5.3 %prepare.1 = (bf16[64,56,128]{2,1,0:T(8,128)(2,1)}, bf16[64,32,128]{2,1,0:T(8,128)(2,1)}, s32[1,512]{1,0:T(1,128)}) custom-call(s32[1,512]{1,0:T(1,128)} %bitcast.14, s32[1,512]{1,0:T(1,128)} %bitcast.15, s32[1024,128]{1,0:T(8,128)} %bitcast.13, bf16[512,1024]{1,0:T(8,128)(2,1)} %embeddings.1), custom_call_target="tpu_custom_call" | custom-call | flops 2147483648 | bytes 2097152 | tf_op jit(solution)/shard_map/prepare/pallas_call | solution.py:46
  12.5 48.1 %all_to_all.15.arrived = bf16[64,56,128]{2,1,0:T(8,128)(2,1)} all-to-all(bf16[64,56,128]{2,1,0:T(8,128)(2,1)} %get-tuple-element.25), channel_id=1, replica_groups=mesh['x'=8,'core'=2,'mem'=64] {'mem'}, dimensions={0} | all-to-all | bytes 1835008 | tf_op jit(solution)/shard_map/all_to_all | solution.py:320
  60.6 2.6 %unpack.2.box.notes_box.notes_own.own = bf16[656,640]{1,0:T(8,128)(2,1)} custom-call(bf16[64,56,128]{2,1,0:T(8,128)(2,1)} %all_to_all.15.arrived), custom_call_target="tpu_custom_call" | custom-call | flops 16777216 | bytes 2097152 | tf_op jit(solution)/shard_map/unpack/pallas_call | solution.py:46
  63.2 5.6 %collective-permute-start = (bf16[656,640]{1,0:T(8,128)(2,1)}, bf16[656,640]{1,0:T(8,128)(2,1)S(1)}, u32[]{:S(2)}, u32[]{:S(2)}) collective-permute-start(bf16[656,640]{1,0:T(8,128)(2,1)} %unpack.2.box.notes_box.notes_own.own), channel_id=1, source_target_pairs={{0,64},{64,0},{1,65},{65,1},{2,66},{66,2},{3,67},{67,3},{4,68},{68... | collective-permute-start | bytes 2519048 | tf_op jit(solution)/shard_map/ppermute | solution.py:273
  69.5 3.9 %sums_one.2.refs_0_ = bf16[1152,640]{1,0:T(8,128)(2,1)} custom-call(s32[2]{0:T(128)} %pad_add_fusion.where, bf16[656,640]{1,0:T(8,128)(2,1)} %unpack.2.box.notes_box.notes_own.own), custom_call_target="tpu_custom_call" | custom-call | flops 2147483648 | bytes 2097152 | tf_op jit(solution)/shard_map/sums_one/pallas_call | solution.py:46
  74.3 4.4 %sums_one.3 = bf16[1152,640]{1,0:T(8,128)(2,1)} custom-call(s32[2]{0:T(128)} %pad_add_fusion.where, bf16[656,640]{1,0:T(8,128)(2,1)} %copy-done.11, bf16[1152,640]{1,0:T(8,128)(2,1)} %sums_one.2.refs_0_), custom_call_target="tpu_custom_call" | custom-call | flops 2147483648 | bytes 2097152 | tf_op jit(solution)/shard_map/sums_one/pallas_call | solution.py:46
  79.7 23.4 %all_to_all.16.arrived = bf16[64,32,128]{2,1,0:T(8,128)(2,1)} all-to-all(bf16[64,32,128]{2,1,0:T(8,128)(2,1)S(1)} %copy-done), channel_id=1, replica_groups=mesh['x'=8,'core'=2,'mem'=64] {'mem'}, dimensions={0} | all-to-all | bytes 1048576 | tf_op jit(solution)/shard_map/all_to_all | solution.py:320
  105.1 4.1 %collective-permute-start.1 = (bf16[640,384]{1,0:T(8,128)(2,1)}, bf16[640,384]{1,0:T(8,128)(2,1)S(1)}, u32[]{:S(2)}, u32[]{:S(2)}) collective-permute-start(bf16[640,384]{1,0:T(8,128)(2,1)} %unpack.3.box.own), channel_id=1, source_target_pairs={{0,64},{64,0},{1,65},{65,1},{2,66},{66,2},{3,67},{67,3},{4,68},{68... | collective-permute-start | bytes 1474568 | tf_op jit(solution)/shard_map/ppermute | solution.py:273
  109.2 2.9 %sums_two.2 = (bf16[128,384]{1,0:T(8,128)(2,1)}, bf16[128,384]{1,0:T(8,128)(2,1)}, bf16[128,384]{1,0:T(8,128)(2,1)}, bf16[128,384]{1,0:T(8,128)(2,1)}, bf16[128,...) custom-call(s32[2]{0:T(128)} %pad_add_fusion.where, ...), custom_call_target="tpu_custom_call" | custom-call | flops 2147483648 | bytes 2097152 | tf_op jit(solution)/shard_map/sums_two/pallas_call | solution.py:46
  112.8 3.2 %sums_two.3 = (bf16[128,384]{1,0:T(8,128)(2,1)}, bf16[128,384]{1,0:T(8,128)(2,1)}, bf16[128,384]{1,0:T(8,128)(2,1)}, bf16[128,384]{1,0:T(8,128)(2,1)}, bf16[128,...) custom-call(s32[2]{0:T(128)} %pad_add_fusion.where, ...), custom_call_target="tpu_custom_call" | custom-call | flops 2147483648 | bytes 2097152 | tf_op jit(solution)/shard_map/sums_two/pallas_call | solution.py:46
  116.0 4.6 %collective-permute-start.6 = (bf16[128,128]{1,0:T(8,128)(2,1)}, bf16[128,128]{1,0:T(8,128)(2,1)S(1)}, u32[]{:S(2)}, u32[]{:S(2)}) collective-permute-start(bf16[128,128]{1,0:T(8,128)(2,1)} %get-tuple-element.44), channel_id=1, source_target_pairs={{0,896},{128,0},{256,128},{384,256},{512,384},{640,512},{768,640},... | collective-permute-start | bytes 98312 | tf_op jit(solution)/shard_map/ppermute | solution.py:273
  126.9 4.6 %collective-permute-start.7 = (bf16[128,384]{1,0:T(8,128)(2,1)S(1)}, bf16[128,384]{1,0:T(8,128)(2,1)S(1)}, u32[]{:S(2)}, u32[]{:S(2)}) collective-permute-start(bf16[128,384]{1,0:T(8,128)(2,1)S(1)} %pad_maximum_fusion.1), channel_id=1, source_target_pairs={{0,896},{128,0},{256,128},{384,256},{512,384},{640,512},{768,640},... | collective-permute-start | bytes 294920 | tf_op jit(solution)/shard_map/ppermute | solution.py:273
  133.6 4.6 %collective-permute-start.8 = (bf16[128,384]{1,0:T(8,128)(2,1)S(1)}, bf16[128,384]{1,0:T(8,128)(2,1)S(1)}, u32[]{:S(2)}, u32[]{:S(2)}) collective-permute-start(bf16[128,384]{1,0:T(8,128)(2,1)S(1)} %add_convert_fusion.1), channel_id=1, source_target_pairs={{0,896},{128,0},{256,128},{384,256},{512,384},{640,512},{768,640},... | collective-permute-start | bytes 294920 | tf_op jit(solution)/shard_map/ppermute | solution.py:273
  140.8 4.0 %collective-permute-start.9 = (bf16[128,384]{1,0:T(8,128)(2,1)S(1)}, bf16[128,384]{1,0:T(8,128)(2,1)S(1)}, u32[]{:S(2)}, u32[]{:S(2)}) collective-permute-start(bf16[128,384]{1,0:T(8,128)(2,1)S(1)} %add_convert_fusion), channel_id=1, source_target_pairs={{0,896},{128,0},{256,128},{384,256},{512,384},{640,512},{768,640},... | collective-permute-start | bytes 294920 | tf_op jit(solution)/shard_map/ppermute | solution.py:273
  147.2 6.1 %collective-permute-done.5.above = bf16[128,384]{1,0:T(8,128)(2,1)S(1)} collective-permute-done((bf16[128,384]{1,0:T(8,128)(2,1)S(1)}, bf16[128,384]{1,0:T(8,128)(2,1)S(1)}, u32[]{:S(2)}, u32[]{:S(2)}) %collective-permute-start.5) | collective-permute-done | bytes 98336 | tf_op jit(solution)/shard_map/ppermute | solution.py:273
  158.1 3.4 %collective-permute-start.13 = (bf16[128,384]{1,0:T(8,128)(2,1)}, bf16[128,384]{1,0:T(8,128)(2,1)S(1)}, u32[]{:S(2)}, u32[]{:S(2)}) collective-permute-start(bf16[128,384]{1,0:T(8,128)(2,1)} %get-tuple-element.47.refs_0_), channel_id=1, source_target_pairs={{0,128},{128,256},{256,384},{384,512},{512,640},{640,768},{768,896... | collective-permute-start | bytes 294920 | tf_op jit(solution)/shard_map/ppermute | solution.py:273
  162.6 3.3 %collective-permute-start.11 = (bf16[128,384]{1,0:T(8,128)(2,1)S(1)}, bf16[128,384]{1,0:T(8,128)(2,1)S(1)}, u32[]{:S(2)}, u32[]{:S(2)}) collective-permute-start(bf16[128,384]{1,0:T(8,128)(2,1)S(1)} %collective-permute-done.10.refs_1_), channel_id=1, source_target_pairs={{0,896},{128,0},{256,128},{384,256},{512,384},{640,512},{768,640},... | collective-permute-start | bytes 294920 | tf_op jit(solution)/shard_map/ppermute | solution.py:273
  168.0 4.5 %collective-permute-start.12 = (bf16[128,384]{1,0:T(8,128)(2,1)S(1)}, bf16[128,384]{1,0:T(8,128)(2,1)S(1)}, u32[]{:S(2)}, u32[]{:S(2)}) collective-permute-start(bf16[128,384]{1,0:T(8,128)(2,1)S(1)} %collective-permute-done.11.refs_3_), channel_id=1, source_target_pairs={{0,896},{128,0},{256,128},{384,256},{512,384},{640,512},{768,640},... | collective-permute-start | bytes 294920 | tf_op jit(solution)/shard_map/ppermute | solution.py:273
  174.4 4.6 %collective-permute-start.17 = (bf16[128,128]{1,0:T(8,128)(2,1)S(1)}, bf16[128,128]{1,0:T(8,128)(2,1)S(1)}, u32[]{:S(2)}, u32[]{:S(2)}) collective-permute-start(bf16[128,128]{1,0:T(8,128)(2,1)S(1)} %slice.63), channel_id=1, source_target_pairs={{0,896},{128,0},{256,128},{384,256},{512,384},{640,512},{768,640},... | collective-permute-start | bytes 98312 | tf_op jit(solution)/shard_map/ppermute | solution.py:273
  181.2 3.9 %score.3.refs_1_ = f32[2,640]{1,0:T(2,128)} custom-call(s32[2]{0:T(128)} %pad_add_fusion.where, bf16[656,640]{1,0:T(8,128)(2,1)} %unpack.2.box.notes_box.notes_own.own, bf16[656,640]{1,0:T(8,128)(2,1)} %copy-done.11, bf16[640,384]{1,0:T(8,128)(2,1)} %unpack.3.box.own, bf16[640,384]{1,0:T(8,128)(2,1)} %copy-done.12, ...), custom_call_target="tpu_custom_call" | custom-call | flops 2147483648 | bytes 2097152 | tf_op jit(solution)/shard_map/score/pallas_call | solution.py:46
  186.6 5.9 %score.4.refs_3_ = f32[2,640]{1,0:T(2,128)} custom-call(s32[2]{0:T(128)} %pad_add_fusion.where, bf16[656,640]{1,0:T(8,128)(2,1)} %unpack.2.box.notes_box.notes_own.own, bf16[656,640]{1,0:T(8,128)(2,1)} %copy-done.11, bf16[656,640]{1,0:T(8,128)(2,1)} %unpack.2.box.notes_box.notes_own.own, bf16[656,640]{1,0:T(8,128)(2,1)} %copy-done.11, ...), custom_call_target="tpu_custom_call" | custom-call | flops 2147483648 | bytes 2097152 | tf_op jit(solution)/shard_map/score/pallas_call | solution.py:46
  192.6 3.4 %score.5 = f32[2,640]{1,0:T(2,128)} custom-call(s32[2]{0:T(128)} %pad_add_fusion.where, bf16[656,640]{1,0:T(8,128)(2,1)} %unpack.2.box.notes_box.notes_own.own, bf16[656,640]{1,0:T(8,128)(2,1)} %copy-done.11, bf16[640,384]{1,0:T(8,128)(2,1)} %unpack.3.box.own, bf16[640,384]{1,0:T(8,128)(2,1)} %copy-done.12, bf16[128,384]{1,0:T(8,128)(2,1)} %copy-done.9, ...), custom_call_target="tpu_custom_call" | custom-call | flops 2147483648 | bytes 2097152 | tf_op jit(solution)/shard_map/score/pallas_call | solution.py:46
  196.8 9.7 %collective-permute-start.18 = (f32[640]{0:T(1024)S(1)}, f32[640]{0:T(1024)S(1)}, u32[]{:S(2)}, u32[]{:S(2)}) collective-permute-start(f32[640]{0:T(1024)S(1)} %get-tuple-element.48), channel_id=1, source_target_pairs={{0,64},{64,0},{1,65},{65,1},{2,66},{66,2},{3,67},{67,3},{4,68},{68... | collective-permute-start | bytes 7688 | tf_op jit(solution)/shard_map/ppermute | solution.py:273
  207.6 18.8 %all_to_all.17 = f32[64,1,10]{2,1,0:T(1,128)S(1)} all-to-all(f32[64,1,10]{2,1,0:T(1,128)S(1)} %bitcast.11), channel_id=1, replica_groups=mesh['x'=8,'core'=2,'mem'=64] {'mem'}, dimensions={0} | all-to-all | bytes 5120 | tf_op jit(solution)/shard_map/all_to_all | solution.py:320
  (95 shorter events, 36.4 us)
Async XLA Ops:
  7.2 117.0 %reduce-scatter.2.cloned.1.call-start = ((), (), s32[]{:S(2)}) async-start(), calls=%async_computation.4 | async-start | bytes 1658880 | tf_op jit(solution)/shard_map/reduce_scatter | solution.py:352
  63.2 10.2 %collective-permute-start = (bf16[656,640]{1,0:T(8,128)(2,1)}, bf16[656,640]{1,0:T(8,128)(2,1)S(1)}, u32[]{:S(2)}, u32[]{:S(2)}) collective-permute-start(bf16[656,640]{1,0:T(8,128)(2,1)} %unpack.2.box.notes_box.notes_own.own), channel_id=1, source_target_pairs={{0,64},{64,0},{1,65},{65,1},{2,66},{66,2},{3,67},{67,3},{4,68},{68... | collective-permute-start | bytes 2519048 | tf_op jit(solution)/shard_map/ppermute | solution.py:273
  78.7 107.9 %all-gather.2.cloned.1.call-start = ((), (), s32[]{:S(2)}) async-start(), calls=%async_computation.5 | async-start | bytes 1474560 | tf_op jit(solution)/shard_map/all_gather | solution.py:367
  105.1 7.0 %collective-permute-start.1 = (bf16[640,384]{1,0:T(8,128)(2,1)}, bf16[640,384]{1,0:T(8,128)(2,1)S(1)}, u32[]{:S(2)}, u32[]{:S(2)}) collective-permute-start(bf16[640,384]{1,0:T(8,128)(2,1)} %unpack.3.box.own), channel_id=1, source_target_pairs={{0,64},{64,0},{1,65},{65,1},{2,66},{66,2},{3,67},{67,3},{4,68},{68... | collective-permute-start | bytes 1474568 | tf_op jit(solution)/shard_map/ppermute | solution.py:273
  116.0 24.7 %copy-start.5 = (bf16[128,384]{1,0:T(8,128)(2,1)S(1)}, bf16[128,384]{1,0:T(8,128)(2,1)}, u32[]{:S(2)}) copy-start(bf16[128,384]{1,0:T(8,128)(2,1)} %get-tuple-element.41) | copy-start | bytes 294916
  116.0 29.2 %copy-start.4 = (bf16[128,384]{1,0:T(8,128)(2,1)S(1)}, bf16[128,384]{1,0:T(8,128)(2,1)}, u32[]{:S(2)}) copy-start(bf16[128,384]{1,0:T(8,128)(2,1)} %get-tuple-element.37) | copy-start | bytes 294916
  116.0 10.1 %collective-permute-start.6 = (bf16[128,128]{1,0:T(8,128)(2,1)}, bf16[128,128]{1,0:T(8,128)(2,1)S(1)}, u32[]{:S(2)}, u32[]{:S(2)}) collective-permute-start(bf16[128,128]{1,0:T(8,128)(2,1)} %get-tuple-element.44), channel_id=1, source_target_pairs={{0,896},{128,0},{256,128},{384,256},{512,384},{640,512},{768,640},... | collective-permute-start | bytes 98312 | tf_op jit(solution)/shard_map/ppermute | solution.py:273
  121.4 10.1 %collective-permute-start.2 = (bf16[128,256]{1,0:T(8,128)(2,1)}, bf16[128,256]{1,0:T(8,128)(2,1)S(1)}, u32[]{:S(2)}, u32[]{:S(2)}) collective-permute-start(bf16[128,256]{1,0:T(8,128)(2,1)} %get-tuple-element.40), channel_id=1, source_target_pairs={{0,128},{128,256},{256,384},{384,512},{512,640},{640,768},{768,896... | collective-permute-start | bytes 196616 | tf_op jit(solution)/shard_map/ppermute | solution.py:273
  126.9 6.6 %collective-permute-start.7 = (bf16[128,384]{1,0:T(8,128)(2,1)S(1)}, bf16[128,384]{1,0:T(8,128)(2,1)S(1)}, u32[]{:S(2)}, u32[]{:S(2)}) collective-permute-start(bf16[128,384]{1,0:T(8,128)(2,1)S(1)} %pad_maximum_fusion.1), channel_id=1, source_target_pairs={{0,896},{128,0},{256,128},{384,256},{512,384},{640,512},{768,640},... | collective-permute-start | bytes 294920 | tf_op jit(solution)/shard_map/ppermute | solution.py:273
  131.6 6.6 %collective-permute-start.3 = (bf16[128,384]{1,0:T(8,128)(2,1)S(1)}, bf16[128,384]{1,0:T(8,128)(2,1)S(1)}, u32[]{:S(2)}, u32[]{:S(2)}) collective-permute-start(bf16[128,384]{1,0:T(8,128)(2,1)S(1)} %pad_maximum_fusion), channel_id=1, source_target_pairs={{0,128},{128,256},{256,384},{384,512},{512,640},{640,768},{768,896... | collective-permute-start | bytes 294920 | tf_op jit(solution)/shard_map/ppermute | solution.py:273
  133.6 7.2 %collective-permute-start.8 = (bf16[128,384]{1,0:T(8,128)(2,1)S(1)}, bf16[128,384]{1,0:T(8,128)(2,1)S(1)}, u32[]{:S(2)}, u32[]{:S(2)}) collective-permute-start(bf16[128,384]{1,0:T(8,128)(2,1)S(1)} %add_convert_fusion.1), channel_id=1, source_target_pairs={{0,896},{128,0},{256,128},{384,256},{512,384},{640,512},{768,640},... | collective-permute-start | bytes 294920 | tf_op jit(solution)/shard_map/ppermute | solution.py:273
  138.2 7.1 %collective-permute-start.4 = (bf16[128,384]{1,0:T(8,128)(2,1)S(1)}, bf16[128,384]{1,0:T(8,128)(2,1)S(1)}, u32[]{:S(2)}, u32[]{:S(2)}) collective-permute-start(bf16[128,384]{1,0:T(8,128)(2,1)S(1)} %add_convert_fusion.3), channel_id=1, source_target_pairs={{0,128},{128,256},{256,384},{384,512},{512,640},{640,768},{768,896... | collective-permute-start | bytes 294920 | tf_op jit(solution)/shard_map/ppermute | solution.py:273
  140.8 6.5 %collective-permute-start.9 = (bf16[128,384]{1,0:T(8,128)(2,1)S(1)}, bf16[128,384]{1,0:T(8,128)(2,1)S(1)}, u32[]{:S(2)}, u32[]{:S(2)}) collective-permute-start(bf16[128,384]{1,0:T(8,128)(2,1)S(1)} %add_convert_fusion), channel_id=1, source_target_pairs={{0,896},{128,0},{256,128},{384,256},{512,384},{640,512},{768,640},... | collective-permute-start | bytes 294920 | tf_op jit(solution)/shard_map/ppermute | solution.py:273
  145.3 8.1 %collective-permute-start.5 = (bf16[128,384]{1,0:T(8,128)(2,1)S(1)}, bf16[128,384]{1,0:T(8,128)(2,1)S(1)}, u32[]{:S(2)}, u32[]{:S(2)}) collective-permute-start(bf16[128,384]{1,0:T(8,128)(2,1)S(1)} %add_convert_fusion.2), channel_id=1, source_target_pairs={{0,128},{128,256},{256,384},{384,512},{512,640},{640,768},{768,896... | collective-permute-start | bytes 294920 | tf_op jit(solution)/shard_map/ppermute | solution.py:273
  156.2 6.4 %collective-permute-start.10 = (bf16[128,384]{1,0:T(8,128)(2,1)}, bf16[128,384]{1,0:T(8,128)(2,1)S(1)}, u32[]{:S(2)}, u32[]{:S(2)}) collective-permute-start(bf16[128,384]{1,0:T(8,128)(2,1)} %get-tuple-element.47.refs_0_), channel_id=1, source_target_pairs={{0,896},{128,0},{256,128},{384,256},{512,384},{640,512},{768,640},... | collective-permute-start | bytes 294920 | tf_op jit(solution)/shard_map/ppermute | solution.py:273
  158.1 7.8 %collective-permute-start.13 = (bf16[128,384]{1,0:T(8,128)(2,1)}, bf16[128,384]{1,0:T(8,128)(2,1)S(1)}, u32[]{:S(2)}, u32[]{:S(2)}) collective-permute-start(bf16[128,384]{1,0:T(8,128)(2,1)} %get-tuple-element.47.refs_0_), channel_id=1, source_target_pairs={{0,128},{128,256},{256,384},{384,512},{512,640},{640,768},{768,896... | collective-permute-start | bytes 294920 | tf_op jit(solution)/shard_map/ppermute | solution.py:273
  162.6 5.3 %collective-permute-start.11 = (bf16[128,384]{1,0:T(8,128)(2,1)S(1)}, bf16[128,384]{1,0:T(8,128)(2,1)S(1)}, u32[]{:S(2)}, u32[]{:S(2)}) collective-permute-start(bf16[128,384]{1,0:T(8,128)(2,1)S(1)} %collective-permute-done.10.refs_1_), channel_id=1, source_target_pairs={{0,896},{128,0},{256,128},{384,256},{512,384},{640,512},{768,640},... | collective-permute-start | bytes 294920 | tf_op jit(solution)/shard_map/ppermute | solution.py:273
  165.9 6.6 %collective-permute-start.14 = (bf16[128,384]{1,0:T(8,128)(2,1)S(1)}, bf16[128,384]{1,0:T(8,128)(2,1)S(1)}, u32[]{:S(2)}, u32[]{:S(2)}) collective-permute-start(bf16[128,384]{1,0:T(8,128)(2,1)S(1)} %collective-permute-done.13.refs_2_), channel_id=1, source_target_pairs={{0,128},{128,256},{256,384},{384,512},{512,640},{640,768},{768,896... | collective-permute-start | bytes 294920 | tf_op jit(solution)/shard_map/ppermute | solution.py:273
  168.0 6.4 %collective-permute-start.12 = (bf16[128,384]{1,0:T(8,128)(2,1)S(1)}, bf16[128,384]{1,0:T(8,128)(2,1)S(1)}, u32[]{:S(2)}, u32[]{:S(2)}) collective-permute-start(bf16[128,384]{1,0:T(8,128)(2,1)S(1)} %collective-permute-done.11.refs_3_), channel_id=1, source_target_pairs={{0,896},{128,0},{256,128},{384,256},{512,384},{640,512},{768,640},... | collective-permute-start | bytes 294920 | tf_op jit(solution)/shard_map/ppermute | solution.py:273
  172.5 6.6 %collective-permute-start.15 = (bf16[128,384]{1,0:T(8,128)(2,1)S(1)}, bf16[128,384]{1,0:T(8,128)(2,1)S(1)}, u32[]{:S(2)}, u32[]{:S(2)}) collective-permute-start(bf16[128,384]{1,0:T(8,128)(2,1)S(1)} %collective-permute-done.14.refs_4_), channel_id=1, source_target_pairs={{0,128},{128,256},{256,384},{384,512},{512,640},{640,768},{768,896... | collective-permute-start | bytes 294920 | tf_op jit(solution)/shard_map/ppermute | solution.py:273
  174.4 10.7 %collective-permute-start.17 = (bf16[128,128]{1,0:T(8,128)(2,1)S(1)}, bf16[128,128]{1,0:T(8,128)(2,1)S(1)}, u32[]{:S(2)}, u32[]{:S(2)}) collective-permute-start(bf16[128,128]{1,0:T(8,128)(2,1)S(1)} %slice.63), channel_id=1, source_target_pairs={{0,896},{128,0},{256,128},{384,256},{512,384},{640,512},{768,640},... | collective-permute-start | bytes 98312 | tf_op jit(solution)/shard_map/ppermute | solution.py:273
  179.1 6.9 %collective-permute-start.16 = (bf16[128,256]{1,0:T(8,128)(2,1)S(1)}, bf16[128,256]{1,0:T(8,128)(2,1)S(1)}, u32[]{:S(2)}, u32[]{:S(2)}) collective-permute-start(bf16[128,256]{1,0:T(8,128)(2,1)S(1)} %slice.62), channel_id=1, source_target_pairs={{0,128},{128,256},{256,384},{384,512},{512,640},{640,768},{768,896... | collective-permute-start | bytes 196616 | tf_op jit(solution)/shard_map/ppermute | solution.py:273
  192.6 35.1 %copy-start.10 = (s32[1,512]{1,0:T(1,128)S(1)}, s32[1,512]{1,0:T(1,128)}, u32[]{:S(2)}) copy-start(s32[1,512]{1,0:T(1,128)} %get-tuple-element.46) | copy-start | bytes 6148
  196.8 10.5 %collective-permute-start.18 = (f32[640]{0:T(1024)S(1)}, f32[640]{0:T(1024)S(1)}, u32[]{:S(2)}, u32[]{:S(2)}) collective-permute-start(f32[640]{0:T(1024)S(1)} %get-tuple-element.48), channel_id=1, source_target_pairs={{0,64},{64,0},{1,65},{65,1},{2,66},{66,2},{3,67},{67,3},{4,68},{68... | collective-permute-start | bytes 7688 | tf_op jit(solution)/shard_map/ppermute | solution.py:273
  (14 other events, 137.2 us)
Sparse Core Ops, SparseCore 0:
  78.8 35.5 reduce-scatter.1
  126.2 35.6 all-gather.1

commit v4 on v3

v4 whole, which is shorter than its diff:
```python
import functools

import jax
import jax.numpy as jnp
from jax import lax
from jax.experimental import pallas as pl
from jax.experimental.pallas import tpu as pltpu
from jax.sharding import Mesh
from jax.sharding import PartitionSpec as P

F32 = jnp.float32
BF16 = jnp.bfloat16
LANES = 128
TILE = 8
NOTES = 16
LIMIT = 40 * 2**20
SMEM = pl.BlockSpec(memory_space=pltpu.SMEM)
VMEM = pl.BlockSpec(memory_space=pltpu.VMEM)


def rows_of(shape):
    return lax.broadcasted_iota(jnp.int32, shape, 0).astype(F32)


def lanes_of(shape):
    return lax.broadcasted_iota(jnp.int32, shape, 1).astype(F32)


def hot(condition):
    return jnp.where(condition, 1.0, 0.0).astype(BF16)


def dot(a, b, contract):
    return lax.dot_general(a, b, (contract, ((), ())), preferred_element_type=F32)


def whole(a, size):
    return jnp.floor((a + 0.5) * (1.0 / size))


def call(kernel, name, out_shape, flops, *args, scalars=None):
    specs = [VMEM] * len(args)
    if scalars is not None:
        specs = [SMEM] + specs
        args = (scalars,) + args
    return pl.pallas_call(
        kernel,
        in_specs=specs,
        out_shape=out_shape,
        compiler_params=pltpu.CompilerParams(vmem_limit_bytes=LIMIT),
        cost_estimate=pl.CostEstimate(flops=flops, bytes_accessed=2**21, transcendentals=0),
        name=name,
    )(*args)


def prepare(members, capacity, first, second, table, embeddings, payload, place):
    vectors = first.shape[1]
    parts = embeddings.shape[1] // LANES
    slots = table[...]
    local = slots & (LANES - 1)
    owner = (slots // LANES) & (members - 1)
    group = slots // (LANES * members)
    planes = jnp.concatenate([local, owner, group], axis=1).astype(F32).astype(BF16)

    def look_up(ids):
        row = (ids // LANES).astype(F32)
        lane = (ids & (LANES - 1)).astype(F32)
        found = dot(planes, hot(rows_of((table.shape[0], vectors)) == row), ((0,), (0,)))
        mask = rows_of((LANES, vectors)) == lane

        def pick(k):
            return jnp.sum(
                jnp.where(mask, found[k * LANES : (k + 1) * LANES], 0.0), axis=0, keepdims=True
            )

        return pick(0), pick(1), pick(2)

    first_local, first_owner, first_group = look_up(first[...])
    second_local, _, second_group = look_up(second[...])
    is_owner = rows_of((members, vectors)) == first_owner
    before = hot(rows_of((vectors, vectors)) < lanes_of((vectors, vectors)))
    earlier = dot(hot(is_owner), before, ((1,), (0,)))
    rank = jnp.sum(jnp.where(is_owner, earlier, 0.0), axis=0, keepdims=True)
    place[...] = (first_owner * capacity + rank).astype(jnp.int32)
    spot = jnp.where(rank < TILE, first_owner * TILE + rank, rank * members + first_owner)
    order = hot(rows_of((members * capacity, vectors)) == spot)
    packed = dot(order, embeddings[...], ((1,), (0,)))
    ranked = rows_of((16, vectors)) == rank
    digits = [first_group + 1.0, first_local, second_group + 1.0, second_local]
    spread = [jnp.where(ranked, digit, 0.0) for digit in digits]
    spread.append(jnp.zeros((LANES - 16 * len(digits), vectors), F32))
    labels = dot(hot(is_owner), jnp.concatenate(spread, axis=0).astype(BF16), ((1,), (1,)))
    pieces = [
        packed[: TILE * members, j * LANES : (j + 1) * LANES].reshape(members, TILE, LANES)
        for j in range(parts)
    ]
    rest = [
        packed[p * members : (p + 1) * members, j * LANES : (j + 1) * LANES]
        for p in range(TILE, capacity)
        for j in range(parts)
    ]
    for k in range(0, len(rest), TILE):
        pieces.append(jnp.stack(rest[k : k + TILE], axis=1))
    pieces.append(jnp.broadcast_to(labels[:, None, :], (members, TILE, LANES)))
    payload[...] = jnp.concatenate(pieces, axis=1).astype(BF16)


def unpack(capacity, arrived, box):
    members = arrived.shape[0]
    count = members * capacity
    parts = box.shape[1] // LANES
    values = arrived[...].astype(F32)
    for j in range(parts):
        at = slice(j * LANES, (j + 1) * LANES)
        box[: TILE * members, at] = (
            values[:, j * TILE : (j + 1) * TILE].reshape(TILE * members, LANES).astype(BF16)
        )
        for p in range(TILE, capacity):
            box[p * members : (p + 1) * members, at] = values[:, p * parts + j].astype(BF16)
    labels = values[:, capacity * parts].astype(BF16)
    vector = lanes_of((members, count))
    from_member = jnp.where(
        vector < TILE * members, whole(vector, TILE), vector - members * whole(vector, members)
    )
    found = dot(labels, hot(rows_of((members, count)) == from_member), ((0,), (0,)))
    vector = lanes_of((16, count))
    rank = jnp.where(
        vector < TILE * members, vector - TILE * whole(vector, TILE), whole(vector, members)
    )
    ranked = rows_of((16, count)) == rank
    rows = [
        jnp.sum(jnp.where(ranked, found[k * 16 : (k + 1) * 16], 0.0), axis=0, keepdims=True)
        for k in range(4)
    ]
    notes = jnp.concatenate(rows + [jnp.zeros((NOTES - 4, count), F32)], axis=0)
    if count < box.shape[1]:
        notes = jnp.concatenate(
            [notes, jnp.zeros((NOTES, box.shape[1] - count), F32)], axis=1
        )
    box[count : count + NOTES] = notes.astype(BF16)


def index(chips, where, notes, k):
    group = notes[2 * k : 2 * k + 1] - 1.0
    local = notes[2 * k + 1 : 2 * k + 2]
    chip = whole(group, 2)
    core = group - 2.0 * chip
    own_core = where[1].astype(F32)
    ahead = (chip - where[0].astype(F32)) * (1.0 - 2.0 * own_core)
    ahead = jnp.where(ahead < 0.0, ahead + chips, ahead)
    mine = (group >= 0.0) & (core == own_core)
    return jnp.where(mine, ahead * LANES + local, -1.0)


def sums(chips, count, where, box, *refs):
    earlier, outs = refs[: len(refs) - chips - 1], refs[len(refs) - chips - 1 :]
    width = box.shape[1]
    notes = box[count : count + NOTES, :count].astype(F32)
    table = hot(rows_of((chips * LANES, count)) == index(chips, where, notes, 0))
    total = dot(table, box[0:count, :], ((1,), (0,)))
    hits = dot(jnp.ones((NOTES, count), BF16), table, ((1,), (1,)))
    high = whole(hits, 256)
    left = hits - 256.0 * high
    middle = whole(left, 16)
    low = left - 16.0 * middle
    cut = width // 2
    for k in range(chips):
        at = slice(k * LANES, (k + 1) * LANES)
        digits = [low[:, at], middle[:, at], high[:, at]]
        digits.append(jnp.zeros((NOTES, width - 3 * LANES), F32))
        block = jnp.concatenate([total[at], jnp.concatenate(digits, axis=1)], axis=0)
        places = [(k, block)]
        if k == chips // 2:
            places = [(k, block[:, :cut]), (chips, block[:, cut:])]
        for place, value in places:
            if earlier:
                value = value + earlier[place][...].astype(F32)
            outs[place][...] = value.astype(BF16)


def counts_of(digits):
    identity = hot(rows_of((LANES, LANES)) == lanes_of((LANES, LANES)))

    def column(k):
        return dot(identity, digits[:, k * LANES : (k + 1) * LANES], ((1,), (1,)))[:, 0:1]

    return column(0) + 16.0 * column(1) + 256.0 * column(2)


def refit(mine, above, below, old, fresh):
    counts = counts_of(
        add(add(mine[LANES:], above[LANES:]), below[LANES:])
    )
    total = mine[:LANES].astype(F32) + above[:LANES].astype(F32) + below[:LANES].astype(F32)
    fresh[...] = ((total + old[...].astype(F32)) / (counts + 1.0)).astype(BF16)


def score(chips, count, places, where, own, other, *refs):
    blocks, out = refs[: len(places)], refs[-1]
    before = refs[len(places) : -1]
    values = jnp.concatenate([block[...] for block in blocks], axis=0)
    size = jnp.sum(values.astype(F32) ** 2, axis=1, keepdims=True)
    row = jnp.concatenate([rows_of((LANES, count)) + place for place in places], axis=0)
    totals = []
    for box in (own, other):
        notes = box[count : count + NOTES, :count].astype(F32)
        distance = size - 2.0 * dot(values, box[0:count, :], ((1,), (1,)))
        is_first = row == index(chips, where, notes, 0)
        is_second = row == index(chips, where, notes, 1)
        totals.append(
            jnp.sum(
                jnp.where(is_second, distance, 0.0) - jnp.where(is_first, distance, 0.0),
                axis=0,
                keepdims=True,
            )
        )
    total = jnp.concatenate(totals, axis=0)
    for earlier in before:
        total = total + earlier[...]
    out[...] = total


def add(a, b):
    return (a.astype(F32) + b.astype(F32)).astype(BF16)


def ring_sum(up, down, blocks):
    cut = blocks[4].shape[1]
    above = up(blocks[4])
    below = down(blocks[8])
    above = up(jnp.concatenate([add(blocks[3][:, :cut], above), blocks[3][:, cut:]], axis=1))
    below = down(jnp.concatenate([blocks[5][:, :cut], add(blocks[5][:, cut:], below)], axis=1))
    above = up(add(blocks[2], above))
    below = down(add(blocks[6], below))
    above = up(add(blocks[1], above))
    below = down(add(blocks[7], below))
    return blocks[0], above, below


def ring_gather(up, down, cut, block):
    above, below = [block], [block]
    for _ in range(3):
        above.append(up(above[-1]))
        below.append(down(below[-1]))
    far = jnp.concatenate([up(above[3][:, :cut]), down(below[3][:, cut:])], axis=1)
    return [block, below[1], below[2], below[3], far, above[3], above[2], above[1]]


def on_device(embeddings, assignment, second_choice, list_slot, old_centroids):
    vectors, width = embeddings.shape
    lists = old_centroids.shape[0]
    members = lax.axis_size("mem")
    chips = lax.axis_size("x")
    capacity = vectors // members + 2
    count = members * capacity
    half = width // 2

    def along(step):
        pairs = [(2 * i, 2 * ((i + step) % chips)) for i in range(chips)]
        pairs += [(2 * i + 1, 2 * ((i - step) % chips) + 1) for i in range(chips)]
        return lambda a: lax.ppermute(a, ("x", "core"), pairs)

    up, down = along(1), along(-1)

    def across(a):
        return lax.ppermute(a, "core", [(0, 1), (1, 0)])

    def shape(*dims, kind=BF16):
        return jax.ShapeDtypeStruct(dims, kind)

    def exchange(a):
        return lax.all_to_all(a, "mem", split_axis=0, concat_axis=0, tiled=True)

    where = jnp.stack([lax.axis_index("x"), lax.axis_index("core")]).astype(jnp.int32)
    payload, place = call(
        functools.partial(prepare, members, capacity),
        "prepare",
        (
            shape(members, capacity * width // LANES + TILE, LANES),
            shape(1, vectors, kind=jnp.int32),
        ),
        2**31,
        assignment.reshape(1, vectors),
        second_choice.reshape(1, vectors),
        list_slot.reshape(-1, LANES),
        embeddings,
    )
    arrived = exchange(payload)
    own = call(
        functools.partial(unpack, capacity), "unpack", shape(count + NOTES, width), 2**24, arrived
    )
    other = across(own)
    kernel = functools.partial(sums, chips, count)
    outs = [shape(lists + NOTES, half if k == chips // 2 else width) for k in range(chips)]
    outs.append(shape(lists + NOTES, half))
    blocks = call(kernel, "sums", outs, 2**31, own, scalars=where)
    blocks = call(kernel, "sums", outs, 2**31, other, *blocks, scalars=where)
    fresh = call(
        refit, "refit", shape(lists, width), 2**24, *ring_sum(up, down, blocks), old_centroids
    )
    gathered = ring_gather(up, down, half, fresh)

    def scored(near, *rest):
        return call(
            functools.partial(score, chips, count, [k * LANES for k in near]),
            "score",
            shape(2, count, kind=F32),
            2**31,
            own,
            other,
            *[gathered[k] for k in near],
            *rest,
            scalars=where,
        )

    total = scored([0, 1, 7, 2, 6])
    total = scored([3, 5, 4], total)
    margin = (total[0] + across(total[1])) * (1.0 / width)
    margin = jnp.concatenate(
        [
            margin[: TILE * members].reshape(members, TILE),
            margin[TILE * members :].reshape(capacity - TILE, members).T,
        ],
        axis=1,
    )
    returned = exchange(margin.reshape(members, 1, capacity))
    spots = jnp.arange(count, dtype=jnp.int32)
    margins = jnp.sum(
        jnp.where(place.reshape(vectors, 1) == spots[None, :], returned.reshape(1, count), 0.0),
        axis=1,
    )
    return fresh, margins


def solution(mesh):
    groups, members = mesh.devices.shape
    chip_mesh = Mesh(mesh.devices.reshape(groups // 2, 2, members), ("x", "core", "mem"))
    everywhere = ("x", "core", "mem")
    placed = (
        P(everywhere, None),
        P(everywhere),
        P(everywhere),
        P(),
        P(everywhere, None),
    )
    return jax.shard_map(
        on_device,
        mesh=chip_mesh,
        in_specs=placed,
        out_specs=(P(everywhere, None), P(everywhere)),
        check_vma=False,
    )
```

time: 237 us -> 199 us (0.84)
  Pallas kernels: 41.6 us -> 15.3 us
  waiting for transfers between devices: 10.1 us -> 24.9 us
  between operations: 14.5 us -> 1 us
  blocking collectives: 90.3 us -> 76.9 us
  starting transfers between devices: 68.4 us -> 72.7 us
    pallas_call x12 -> x7, Pallas kernels: 41.6 us -> 15.3 us  [call(): pl.pallas_call(kernel, in_specs=specs, out_shape=out_shape, compiler_para...]
    ppermute x19 -> x18, waiting for transfers between devices: 10.1 us -> 24.9 us  [the longest x16 24.1 us: along(): return lambda a: lax.ppermute(a, ('x', 'core'), pairs)]
    all_to_all x3 -> x2, blocking collectives: 90.3 us -> 76.9 us  [exchange(): return lax.all_to_all(a, 'mem', split_axis=0, concat_axis=0, tiled=True)]
    ppermute x19 -> x18, starting transfers between devices: 68.3 us -> 72.7 us  [the longest x16 56.2 us: along(): return lambda a: lax.ppermute(a, ('x', 'core'), pairs)]
  transfers between devices with their start and end apart: 21 -> 18, of which waited for: 6 -> 12; matrix products, arithmetic and copies ran while one was open for 2% -> 0% of each run, Pallas kernels for 8% -> 3%
where the time goes in v4:
time: 199 us
  blocking collectives  76.9 us (39%)
  starting transfers between devices  72.7 us (37%)
  waiting for transfers between devices  24.9 us (13%)
  Pallas kernels  15.3 us (8%)
  local copies, waits for them, and re-layouts  5.55 us (3%)
  other arithmetic  2.2 us (1%)
    all_to_all x2, blocking collectives, exchange(): return lax.all_to_all(a, 'mem', split_axis=0, concat_axis=0, tiled=True)  76.9 us
    ppermute x16, starting transfers between devices, along(): return lambda a: lax.ppermute(a, ('x', 'core'), pairs)  56.2 us
    ppermute x16, waiting for transfers between devices, along(): return lambda a: lax.ppermute(a, ('x', 'core'), pairs)  24.1 us
    ppermute x2, starting transfers between devices, across(): return lax.ppermute(a, 'core', [(0, 1), (1, 0)])  16.4 us
    pallas_call x7, Pallas kernels, call(): pl.pallas_call(kernel, in_specs=specs, out_shape=out_shape, compiler_para...  15.3 us
    unnamed x12, local copies, waits for them, and re-layouts  4.57 us
  transfers between devices with their start and end apart: 18, of which 12 were waited for; matrix products, arithmetic and copies ran while one was open for 0% of the time, Pallas kernels for 3%

profile of v4, /device:TPU:1, one launch (start us, length us, event | category | flops | bytes accessed | tf_op | source)
XLA Modules:
  0.0 198.6 jit_solution(126734561817928925)
XLA Ops:
  4.3 2.7 %prepare.1 = (bf16[64,88,128]{2,1,0:T(8,128)(2,1)S(1)}, s32[1,512]{1,0:T(1,128)S(1)}) custom-call(s32[1,512]{1,0:T(1,128)S(1)} %bitcast.12, s32[1,512]{1,0:T(1,128)S(1)} %bitcast.13, s32[1024,128]{1,0:T(8,128)S(1)} %bitcast.11, bf16[512,1024]{1,0:T(8,128)(2,1)S(1)} %copy-done.2), custom_call_target="tpu_custom_call" | custom-call | flops 2147483648 | bytes 2097152 | tf_op jit(solution)/shard_map/prepare/pallas_call | solution.py:46
  7.0 58.6 %all_to_all.10.arrived = bf16[64,88,128]{2,1,0:T(8,128)(2,1)S(1)} all-to-all(bf16[64,88,128]{2,1,0:T(8,128)(2,1)S(1)} %get-tuple-element.22), channel_id=1, replica_groups=mesh['x'=8,'core'=2,'mem'=64] {'mem'}, dimensions={0} | all-to-all | bytes 2883584 | tf_op jit(solution)/shard_map/all_to_all | solution.py:272
  66.3 6.1 %collective-permute-start = (bf16[656,1024]{1,0:T(8,128)(2,1)S(1)}, bf16[656,1024]{1,0:T(8,128)(2,1)S(1)}, u32[]{:S(2)}, u32[]{:S(2)}) collective-permute-start(bf16[656,1024]{1,0:T(8,128)(2,1)S(1)} %unpack.1.box.own), channel_id=1, source_target_pairs={{0,64},{64,0},{1,65},{65,1},{2,66},{66,2},{3,67},{67,3},{4,68},{68... | collective-permute-start | bytes 4030472 | tf_op jit(solution)/shard_map/ppermute | solution.py:266
  72.5 2.6 %sums.2 = (bf16[144,1024]{1,0:T(8,128)(2,1)S(1)}, bf16[144,1024]{1,0:T(8,128)(2,1)S(1)}, bf16[144,1024]{1,0:T(8,128)(2,1)S(1)}, bf16[144,1024]{1,0:T(8,128)(2,1)...) custom-call(s32[2]{0:T(128)S(1)} %pad_add_fusion.where, ...), custom_call_target="tpu_custom_call" | custom-call | flops 2147483648 | bytes 2097152 | tf_op jit(solution)/shard_map/sums/pallas_call | solution.py:46
  75.1 2.7 %sums.3 = (bf16[144,1024]{1,0:T(8,128)(2,1)S(1)}, bf16[144,1024]{1,0:T(8,128)(2,1)S(1)}, bf16[144,1024]{1,0:T(8,128)(2,1)S(1)}, bf16[144,1024]{1,0:T(8,128)(2,1)...) custom-call(s32[2]{0:T(128)S(1)} %pad_add_fusion.where, ...), custom_call_target="tpu_custom_call" | custom-call | flops 2147483648 | bytes 2097152 | tf_op jit(solution)/shard_map/sums/pallas_call | solution.py:46
  77.8 3.1 %collective-permute-start.5 = (bf16[144,512]{1,0:T(8,128)(2,1)S(1)}, bf16[144,512]{1,0:T(8,128)(2,1)S(1)}, u32[]{:S(2)}, u32[]{:S(2)}) collective-permute-start(bf16[144,512]{1,0:T(8,128)(2,1)S(1)} %get-tuple-element.40), channel_id=1, source_target_pairs={{0,896},{128,0},{256,128},{384,256},{512,384},{640,512},{768,640},... | collective-permute-start | bytes 442376 | tf_op jit(solution)/shard_map/ppermute | solution.py:261
  80.9 3.4 %collective-permute-start.1 = (bf16[144,512]{1,0:T(8,128)(2,1)S(1)}, bf16[144,512]{1,0:T(8,128)(2,1)S(1)}, u32[]{:S(2)}, u32[]{:S(2)}) collective-permute-start(bf16[144,512]{1,0:T(8,128)(2,1)S(1)} %get-tuple-element.36), channel_id=1, source_target_pairs={{0,128},{128,256},{256,384},{384,512},{512,640},{640,768},{768,896... | collective-permute-start | bytes 442376 | tf_op jit(solution)/shard_map/ppermute | solution.py:261
  85.0 2.2 %collective-permute-start.6 = (bf16[144,1024]{1,0:T(8,128)(2,1)S(1)}, bf16[144,1024]{1,0:T(8,128)(2,1)S(1)}, u32[]{:S(2)}, u32[]{:S(2)}) collective-permute-start(bf16[144,1024]{1,0:T(8,128)(2,1)S(1)} %pad_maximum_fusion.1), channel_id=1, source_target_pairs={{0,896},{128,0},{256,128},{384,256},{512,384},{640,512},{768,640},... | collective-permute-start | bytes 884744 | tf_op jit(solution)/shard_map/ppermute | solution.py:261
  87.3 4.6 %collective-permute-start.2 = (bf16[144,1024]{1,0:T(8,128)(2,1)S(1)}, bf16[144,1024]{1,0:T(8,128)(2,1)S(1)}, u32[]{:S(2)}, u32[]{:S(2)}) collective-permute-start(bf16[144,1024]{1,0:T(8,128)(2,1)S(1)} %pad_maximum_fusion), channel_id=1, source_target_pairs={{0,128},{128,256},{256,384},{384,512},{512,640},{640,768},{768,896... | collective-permute-start | bytes 884744 | tf_op jit(solution)/shard_map/ppermute | solution.py:261
  95.7 2.9 %collective-permute-done.2 = bf16[144,1024]{1,0:T(8,128)(2,1)S(1)} collective-permute-done((bf16[144,1024]{1,0:T(8,128)(2,1)S(1)}, bf16[144,1024]{1,0:T(8,128)(2,1)S(1)}, u32[]{:S(2)}, u32[]{:S(2)}) %collective-permute-start.2) | collective-permute-done | bytes 294944 | tf_op jit(solution)/shard_map/ppermute | solution.py:261
  98.7 5.1 %collective-permute-start.3 = (bf16[144,1024]{1,0:T(8,128)(2,1)S(1)}, bf16[144,1024]{1,0:T(8,128)(2,1)S(1)}, u32[]{:S(2)}, u32[]{:S(2)}) collective-permute-start(bf16[144,1024]{1,0:T(8,128)(2,1)S(1)} %add_convert_fusion.3), channel_id=1, source_target_pairs={{0,128},{128,256},{256,384},{384,512},{512,640},{640,768},{768,896... | collective-permute-start | bytes 884744 | tf_op jit(solution)/shard_map/ppermute | solution.py:261
  105.9 3.8 %collective-permute-done.3 = bf16[144,1024]{1,0:T(8,128)(2,1)S(1)} collective-permute-done((bf16[144,1024]{1,0:T(8,128)(2,1)S(1)}, bf16[144,1024]{1,0:T(8,128)(2,1)S(1)}, u32[]{:S(2)}, u32[]{:S(2)}) %collective-permute-start.3) | collective-permute-done | bytes 294944 | tf_op jit(solution)/shard_map/ppermute | solution.py:261
  109.9 5.3 %collective-permute-start.4 = (bf16[144,1024]{1,0:T(8,128)(2,1)S(1)}, bf16[144,1024]{1,0:T(8,128)(2,1)S(1)}, u32[]{:S(2)}, u32[]{:S(2)}) collective-permute-start(bf16[144,1024]{1,0:T(8,128)(2,1)S(1)} %add_convert_fusion.2), channel_id=1, source_target_pairs={{0,128},{128,256},{256,384},{384,512},{512,640},{640,768},{768,896... | collective-permute-start | bytes 884744 | tf_op jit(solution)/shard_map/ppermute | solution.py:261
  115.2 5.0 %collective-permute-done.4.above = bf16[144,1024]{1,0:T(8,128)(2,1)S(1)} collective-permute-done((bf16[144,1024]{1,0:T(8,128)(2,1)S(1)}, bf16[144,1024]{1,0:T(8,128)(2,1)S(1)}, u32[]{:S(2)}, u32[]{:S(2)}) %collective-permute-start.4) | collective-permute-done | bytes 294944 | tf_op jit(solution)/shard_map/ppermute | solution.py:261
  121.2 5.3 %collective-permute-start.12 = (bf16[128,1024]{1,0:T(8,128)(2,1)}, bf16[128,1024]{1,0:T(8,128)(2,1)S(1)}, u32[]{:S(2)}, u32[]{:S(2)}) collective-permute-start(bf16[128,1024]{1,0:T(8,128)(2,1)} %refit.1.refs_0_), channel_id=1, source_target_pairs={{0,128},{128,256},{256,384},{384,512},{512,640},{640,768},{768,896... | collective-permute-start | bytes 786440 | tf_op jit(solution)/shard_map/ppermute | solution.py:261
  130.2 4.9 %collective-permute-start.13 = (bf16[128,1024]{1,0:T(8,128)(2,1)S(1)}, bf16[128,1024]{1,0:T(8,128)(2,1)S(1)}, u32[]{:S(2)}, u32[]{:S(2)}) collective-permute-start(bf16[128,1024]{1,0:T(8,128)(2,1)S(1)} %collective-permute-done.12.refs_2_), channel_id=1, source_target_pairs={{0,128},{128,256},{256,384},{384,512},{512,640},{640,768},{768,896... | collective-permute-start | bytes 786440 | tf_op jit(solution)/shard_map/ppermute | solution.py:261
  138.5 2.7 %collective-permute-done.13.refs_4_ = bf16[128,1024]{1,0:T(8,128)(2,1)S(1)} collective-permute-done((bf16[128,1024]{1,0:T(8,128)(2,1)S(1)}, bf16[128,1024]{1,0:T(8,128)(2,1)S(1)}, u32[]{:S(2)}, u32[]{:S(2)}) %collective-permute-start.13) | collective-permute-done | bytes 262176 | tf_op jit(solution)/shard_map/ppermute | solution.py:261
  141.2 5.3 %collective-permute-start.14 = (bf16[128,1024]{1,0:T(8,128)(2,1)S(1)}, bf16[128,1024]{1,0:T(8,128)(2,1)S(1)}, u32[]{:S(2)}, u32[]{:S(2)}) collective-permute-start(bf16[128,1024]{1,0:T(8,128)(2,1)S(1)} %collective-permute-done.13.refs_4_), channel_id=1, source_target_pairs={{0,128},{128,256},{256,384},{384,512},{512,640},{640,768},{768,896... | collective-permute-start | bytes 786440 | tf_op jit(solution)/shard_map/ppermute | solution.py:261
  148.4 3.3 %collective-permute-done.14.refs_1_ = bf16[128,1024]{1,0:T(8,128)(2,1)S(1)} collective-permute-done((bf16[128,1024]{1,0:T(8,128)(2,1)S(1)}, bf16[128,1024]{1,0:T(8,128)(2,1)S(1)}, u32[]{:S(2)}, u32[]{:S(2)}) %collective-permute-start.14) | collective-permute-done | bytes 262176 | tf_op jit(solution)/shard_map/ppermute | solution.py:261
  151.7 5.3 %collective-permute-start.15 = (bf16[128,512]{1,0:T(8,128)(2,1)S(1)}, bf16[128,512]{1,0:T(8,128)(2,1)S(1)}, u32[]{:S(2)}, u32[]{:S(2)}) collective-permute-start(bf16[128,512]{1,0:T(8,128)(2,1)S(1)} %slice.62), channel_id=1, source_target_pairs={{0,128},{128,256},{256,384},{384,512},{512,640},{640,768},{768,896... | collective-permute-start | bytes 393224 | tf_op jit(solution)/shard_map/ppermute | solution.py:261
  160.2 3.2 %score.2.refs_3_ = f32[2,640]{1,0:T(2,128)S(1)} custom-call(s32[2]{0:T(128)S(1)} %pad_add_fusion.where, bf16[656,1024]{1,0:T(8,128)(2,1)S(1)} %unpack.1.box.own, bf16[656,1024]{1,0:T(8,128)(2,1)S(1)} %collective-permute-done.box.other, bf16[128,1024]{1,0:T(8,128)(2,1)S(1)} %copy-done.1, bf16[128,1024]{1,0:T(8,128)(2,1)S(1)} %collective-permute-done.9.refs_1_, ...), custom_call_target="tpu_custom_call" | custom-call | flops 2147483648 | bytes 2097152 | tf_op jit(solution)/shard_map/score/pallas_call | solution.py:46
  164.1 2.3 %score.3 = f32[2,640]{1,0:T(2,128)S(1)} custom-call(s32[2]{0:T(128)S(1)} %pad_add_fusion.where, bf16[656,1024]{1,0:T(8,128)(2,1)S(1)} %unpack.1.box.own, bf16[656,1024]{1,0:T(8,128)(2,1)S(1)} %collective-permute-done.box.other, bf16[128,1024]{1,0:T(8,128)(2,1)S(1)} %collective-permute-done.11.refs_0_, bf16[128,1024]{1,0:T(8,128)(2,1)S(1)} %collective-permute-done.14.refs_1_, ...), custom_call_target="tpu_custom_call" | custom-call | flops 2147483648 | bytes 2097152 | tf_op jit(solution)/shard_map/score/pallas_call | solution.py:46
  166.4 10.3 %collective-permute-start.17 = (f32[640]{0:T(1024)S(1)}, f32[640]{0:T(1024)S(1)}, u32[]{:S(2)}, u32[]{:S(2)}) collective-permute-start(f32[640]{0:T(1024)S(1)} %get-tuple-element.42), channel_id=1, source_target_pairs={{0,64},{64,0},{1,65},{65,1},{2,66},{66,2},{3,67},{67,3},{4,68},{68... | collective-permute-start | bytes 7688 | tf_op jit(solution)/shard_map/ppermute | solution.py:266
  177.9 18.4 %all_to_all.11 = f32[64,1,10]{2,1,0:T(1,128)S(1)} all-to-all(f32[64,1,10]{2,1,0:T(1,128)S(1)} %bitcast.15), channel_id=1, replica_groups=mesh['x'=8,'core'=2,'mem'=64] {'mem'}, dimensions={0} | all-to-all | bytes 5120 | tf_op jit(solution)/shard_map/all_to_all | solution.py:272
  (59 shorter events, 28.3 us)
Async XLA Ops:
  0.6 1.2 copy-start.2
  1.9 1.0 copy-start.3
  2.9 0.7 copy-start.4
  3.6 0.7 copy-start.5
  66.3 8.8 %collective-permute-start = (bf16[656,1024]{1,0:T(8,128)(2,1)S(1)}, bf16[656,1024]{1,0:T(8,128)(2,1)S(1)}, u32[]{:S(2)}, u32[]{:S(2)}) collective-permute-start(bf16[656,1024]{1,0:T(8,128)(2,1)S(1)} %unpack.1.box.own), channel_id=1, source_target_pairs={{0,64},{64,0},{1,65},{65,1},{2,66},{66,2},{3,67},{67,3},{4,68},{68... | collective-permute-start | bytes 4030472 | tf_op jit(solution)/shard_map/ppermute | solution.py:266
  77.8 7.1 %collective-permute-start.5 = (bf16[144,512]{1,0:T(8,128)(2,1)S(1)}, bf16[144,512]{1,0:T(8,128)(2,1)S(1)}, u32[]{:S(2)}, u32[]{:S(2)}) collective-permute-start(bf16[144,512]{1,0:T(8,128)(2,1)S(1)} %get-tuple-element.40), channel_id=1, source_target_pairs={{0,896},{128,0},{256,128},{384,256},{512,384},{640,512},{768,640},... | collective-permute-start | bytes 442376 | tf_op jit(solution)/shard_map/ppermute | solution.py:261
  80.9 6.2 %collective-permute-start.1 = (bf16[144,512]{1,0:T(8,128)(2,1)S(1)}, bf16[144,512]{1,0:T(8,128)(2,1)S(1)}, u32[]{:S(2)}, u32[]{:S(2)}) collective-permute-start(bf16[144,512]{1,0:T(8,128)(2,1)S(1)} %get-tuple-element.36), channel_id=1, source_target_pairs={{0,128},{128,256},{256,384},{384,512},{512,640},{640,768},{768,896... | collective-permute-start | bytes 442376 | tf_op jit(solution)/shard_map/ppermute | solution.py:261
  85.0 8.7 %collective-permute-start.6 = (bf16[144,1024]{1,0:T(8,128)(2,1)S(1)}, bf16[144,1024]{1,0:T(8,128)(2,1)S(1)}, u32[]{:S(2)}, u32[]{:S(2)}) collective-permute-start(bf16[144,1024]{1,0:T(8,128)(2,1)S(1)} %pad_maximum_fusion.1), channel_id=1, source_target_pairs={{0,896},{128,0},{256,128},{384,256},{512,384},{640,512},{768,640},... | collective-permute-start | bytes 884744 | tf_op jit(solution)/shard_map/ppermute | solution.py:261
  87.3 11.3 %collective-permute-start.2 = (bf16[144,1024]{1,0:T(8,128)(2,1)S(1)}, bf16[144,1024]{1,0:T(8,128)(2,1)S(1)}, u32[]{:S(2)}, u32[]{:S(2)}) collective-permute-start(bf16[144,1024]{1,0:T(8,128)(2,1)S(1)} %pad_maximum_fusion), channel_id=1, source_target_pairs={{0,128},{128,256},{256,384},{384,512},{512,640},{640,768},{768,896... | collective-permute-start | bytes 884744 | tf_op jit(solution)/shard_map/ppermute | solution.py:261
  93.7 10.2 %collective-permute-start.7 = (bf16[144,1024]{1,0:T(8,128)(2,1)S(1)}, bf16[144,1024]{1,0:T(8,128)(2,1)S(1)}, u32[]{:S(2)}, u32[]{:S(2)}) collective-permute-start(bf16[144,1024]{1,0:T(8,128)(2,1)S(1)} %add_convert_fusion.1), channel_id=1, source_target_pairs={{0,896},{128,0},{256,128},{384,256},{512,384},{640,512},{768,640},... | collective-permute-start | bytes 884744 | tf_op jit(solution)/shard_map/ppermute | solution.py:261
  98.6 21.7 %copy-start = (bf16[128,1024]{1,0:T(8,128)(2,1)S(1)}, bf16[128,1024]{1,0:T(8,128)(2,1)}, u32[]{:S(2)}) copy-start(bf16[128,1024]{1,0:T(8,128)(2,1)} %old.1) | copy-start | bytes 786436
  98.7 11.1 %collective-permute-start.3 = (bf16[144,1024]{1,0:T(8,128)(2,1)S(1)}, bf16[144,1024]{1,0:T(8,128)(2,1)S(1)}, u32[]{:S(2)}, u32[]{:S(2)}) collective-permute-start(bf16[144,1024]{1,0:T(8,128)(2,1)S(1)} %add_convert_fusion.3), channel_id=1, source_target_pairs={{0,128},{128,256},{256,384},{384,512},{512,640},{640,768},{768,896... | collective-permute-start | bytes 884744 | tf_op jit(solution)/shard_map/ppermute | solution.py:261
  104.0 11.2 %collective-permute-start.8 = (bf16[144,1024]{1,0:T(8,128)(2,1)S(1)}, bf16[144,1024]{1,0:T(8,128)(2,1)S(1)}, u32[]{:S(2)}, u32[]{:S(2)}) collective-permute-start(bf16[144,1024]{1,0:T(8,128)(2,1)S(1)} %add_convert_fusion), channel_id=1, source_target_pairs={{0,896},{128,0},{256,128},{384,256},{512,384},{640,512},{768,640},... | collective-permute-start | bytes 884744 | tf_op jit(solution)/shard_map/ppermute | solution.py:261
  109.9 10.4 %collective-permute-start.4 = (bf16[144,1024]{1,0:T(8,128)(2,1)S(1)}, bf16[144,1024]{1,0:T(8,128)(2,1)S(1)}, u32[]{:S(2)}, u32[]{:S(2)}) collective-permute-start(bf16[144,1024]{1,0:T(8,128)(2,1)S(1)} %add_convert_fusion.2), channel_id=1, source_target_pairs={{0,128},{128,256},{256,384},{384,512},{512,640},{640,768},{768,896... | collective-permute-start | bytes 884744 | tf_op jit(solution)/shard_map/ppermute | solution.py:261
  121.2 8.9 %collective-permute-start.12 = (bf16[128,1024]{1,0:T(8,128)(2,1)}, bf16[128,1024]{1,0:T(8,128)(2,1)S(1)}, u32[]{:S(2)}, u32[]{:S(2)}) collective-permute-start(bf16[128,1024]{1,0:T(8,128)(2,1)} %refit.1.refs_0_), channel_id=1, source_target_pairs={{0,128},{128,256},{256,384},{384,512},{512,640},{640,768},{768,896... | collective-permute-start | bytes 786440 | tf_op jit(solution)/shard_map/ppermute | solution.py:261
  126.6 10.1 %collective-permute-start.9 = (bf16[128,1024]{1,0:T(8,128)(2,1)}, bf16[128,1024]{1,0:T(8,128)(2,1)S(1)}, u32[]{:S(2)}, u32[]{:S(2)}) collective-permute-start(bf16[128,1024]{1,0:T(8,128)(2,1)} %refit.1.refs_0_), channel_id=1, source_target_pairs={{0,896},{128,0},{256,128},{384,256},{512,384},{640,512},{768,640},... | collective-permute-start | bytes 786440 | tf_op jit(solution)/shard_map/ppermute | solution.py:261
  130.2 11.0 %collective-permute-start.13 = (bf16[128,1024]{1,0:T(8,128)(2,1)S(1)}, bf16[128,1024]{1,0:T(8,128)(2,1)S(1)}, u32[]{:S(2)}, u32[]{:S(2)}) collective-permute-start(bf16[128,1024]{1,0:T(8,128)(2,1)S(1)} %collective-permute-done.12.refs_2_), channel_id=1, source_target_pairs={{0,128},{128,256},{256,384},{384,512},{512,640},{640,768},{768,896... | collective-permute-start | bytes 786440 | tf_op jit(solution)/shard_map/ppermute | solution.py:261
  136.6 9.8 %collective-permute-start.10 = (bf16[128,1024]{1,0:T(8,128)(2,1)S(1)}, bf16[128,1024]{1,0:T(8,128)(2,1)S(1)}, u32[]{:S(2)}, u32[]{:S(2)}) collective-permute-start(bf16[128,1024]{1,0:T(8,128)(2,1)S(1)} %collective-permute-done.9.refs_1_), channel_id=1, source_target_pairs={{0,896},{128,0},{256,128},{384,256},{512,384},{640,512},{768,640},... | collective-permute-start | bytes 786440 | tf_op jit(solution)/shard_map/ppermute | solution.py:261
  141.2 10.5 %collective-permute-start.14 = (bf16[128,1024]{1,0:T(8,128)(2,1)S(1)}, bf16[128,1024]{1,0:T(8,128)(2,1)S(1)}, u32[]{:S(2)}, u32[]{:S(2)}) collective-permute-start(bf16[128,1024]{1,0:T(8,128)(2,1)S(1)} %collective-permute-done.13.refs_4_), channel_id=1, source_target_pairs={{0,128},{128,256},{256,384},{384,512},{512,640},{640,768},{768,896... | collective-permute-start | bytes 786440 | tf_op jit(solution)/shard_map/ppermute | solution.py:261
  146.5 10.6 %collective-permute-start.11 = (bf16[128,1024]{1,0:T(8,128)(2,1)S(1)}, bf16[128,1024]{1,0:T(8,128)(2,1)S(1)}, u32[]{:S(2)}, u32[]{:S(2)}) collective-permute-start(bf16[128,1024]{1,0:T(8,128)(2,1)S(1)} %collective-permute-done.10.refs_3_), channel_id=1, source_target_pairs={{0,896},{128,0},{256,128},{384,256},{512,384},{640,512},{768,640},... | collective-permute-start | bytes 786440 | tf_op jit(solution)/shard_map/ppermute | solution.py:261
  151.7 11.7 %collective-permute-start.15 = (bf16[128,512]{1,0:T(8,128)(2,1)S(1)}, bf16[128,512]{1,0:T(8,128)(2,1)S(1)}, u32[]{:S(2)}, u32[]{:S(2)}) collective-permute-start(bf16[128,512]{1,0:T(8,128)(2,1)S(1)} %slice.62), channel_id=1, source_target_pairs={{0,128},{128,256},{256,384},{384,512},{512,640},{640,768},{768,896... | collective-permute-start | bytes 393224 | tf_op jit(solution)/shard_map/ppermute | solution.py:261
  157.1 6.9 %collective-permute-start.16 = (bf16[128,512]{1,0:T(8,128)(2,1)S(1)}, bf16[128,512]{1,0:T(8,128)(2,1)S(1)}, u32[]{:S(2)}, u32[]{:S(2)}) collective-permute-start(bf16[128,512]{1,0:T(8,128)(2,1)S(1)} %slice.63), channel_id=1, source_target_pairs={{0,896},{128,0},{256,128},{384,256},{512,384},{640,512},{768,640},... | collective-permute-start | bytes 393224 | tf_op jit(solution)/shard_map/ppermute | solution.py:261
  159.2 1.0 copy-start.1
  166.4 11.1 %collective-permute-start.17 = (f32[640]{0:T(1024)S(1)}, f32[640]{0:T(1024)S(1)}, u32[]{:S(2)}, u32[]{:S(2)}) collective-permute-start(f32[640]{0:T(1024)S(1)} %get-tuple-element.42), channel_id=1, source_target_pairs={{0,64},{64,0},{1,65},{65,1},{2,66},{66,2},{3,67},{67,3},{4,68},{68... | collective-permute-start | bytes 7688 | tf_op jit(solution)/shard_map/ppermute | solution.py:266

commit v5 on v4

v5 whole, which is shorter than its diff:
```python
import functools

import jax
import jax.numpy as jnp
from jax import lax
from jax.experimental import pallas as pl
from jax.experimental.pallas import tpu as pltpu
from jax.sharding import Mesh
from jax.sharding import PartitionSpec as P

F32 = jnp.float32
BF16 = jnp.bfloat16
LANES = 128
TILE = 8
NOTES = 32
LIMIT = 40 * 2**20
SMEM = pl.BlockSpec(memory_space=pltpu.SMEM)
VMEM = pl.BlockSpec(memory_space=pltpu.VMEM)


def rows_of(shape):
    return lax.broadcasted_iota(jnp.int32, shape, 0).astype(F32)


def lanes_of(shape):
    return lax.broadcasted_iota(jnp.int32, shape, 1).astype(F32)


def hot(condition):
    return jnp.where(condition, 1.0, 0.0).astype(BF16)


def dot(a, b, contract):
    return lax.dot_general(a, b, (contract, ((), ())), preferred_element_type=F32)


def whole(a, size):
    return jnp.floor((a + 0.5) * (1.0 / size))


def call(kernel, name, out_shape, flops, *args, scalars=None, scratch=()):
    specs = [VMEM] * len(args)
    if scalars is not None:
        specs = [SMEM] + specs
        args = (scalars,) + args
    return pl.pallas_call(
        kernel,
        in_specs=specs,
        out_shape=out_shape,
        scratch_shapes=scratch,
        compiler_params=pltpu.CompilerParams(vmem_limit_bytes=LIMIT),
        cost_estimate=pl.CostEstimate(flops=flops, bytes_accessed=2**21, transcendentals=0),
        name=name,
    )(*args)


def prepare(members, capacity, first, second, table, embeddings, payload, place):
    vectors = first.shape[1]
    parts = embeddings.shape[1] // LANES
    slots = table[...]
    local = slots & (LANES - 1)
    owner = (slots // LANES) & (members - 1)
    group = slots // (LANES * members)
    planes = jnp.concatenate([local, owner, group], axis=1).astype(F32).astype(BF16)

    def look_up(ids):
        row = (ids // LANES).astype(F32)
        lane = (ids & (LANES - 1)).astype(F32)
        found = dot(planes, hot(rows_of((table.shape[0], vectors)) == row), ((0,), (0,)))
        mask = rows_of((LANES, vectors)) == lane

        def pick(k):
            return jnp.sum(
                jnp.where(mask, found[k * LANES : (k + 1) * LANES], 0.0), axis=0, keepdims=True
            )

        return pick(0), pick(1), pick(2)

    first_local, first_owner, first_group = look_up(first[...])
    second_local, _, second_group = look_up(second[...])
    is_owner = rows_of((members, vectors)) == first_owner
    before = hot(rows_of((vectors, vectors)) < lanes_of((vectors, vectors)))
    earlier = dot(hot(is_owner), before, ((1,), (0,)))
    rank = jnp.sum(jnp.where(is_owner, earlier, 0.0), axis=0, keepdims=True)
    place[...] = (first_owner * capacity + rank).astype(jnp.int32)
    spot = jnp.where(rank < TILE, first_owner * TILE + rank, rank * members + first_owner)
    order = hot(rows_of((members * capacity, vectors)) == spot)
    packed = dot(order, embeddings[...], ((1,), (0,)))
    ranked = rows_of((16, vectors)) == rank
    digits = [first_group + 1.0, first_local, second_group + 1.0, second_local]
    spread = [jnp.where(ranked, digit, 0.0) for digit in digits]
    spread.append(jnp.zeros((LANES - 16 * len(digits), vectors), F32))
    labels = dot(hot(is_owner), jnp.concatenate(spread, axis=0).astype(BF16), ((1,), (1,)))
    pieces = [
        packed[: TILE * members, j * LANES : (j + 1) * LANES].reshape(members, TILE, LANES)
        for j in range(parts)
    ]
    rest = [
        packed[p * members : (p + 1) * members, j * LANES : (j + 1) * LANES]
        for p in range(TILE, capacity)
        for j in range(parts)
    ]
    for k in range(0, len(rest), TILE):
        pieces.append(jnp.stack(rest[k : k + TILE], axis=1))
    pieces.append(jnp.broadcast_to(labels[:, None, :], (members, TILE, LANES)))
    payload[...] = jnp.concatenate(pieces, axis=1).astype(BF16)


def spread(capacity, arrived, old, out):
    members = arrived.shape[0]
    count = members * capacity
    chips, rows, _ = out.shape
    slots = rows - NOTES - LANES
    values = arrived[...].astype(F32)
    labels = values[:, capacity * chips].astype(BF16)
    vector = lanes_of((members, slots))
    from_member = jnp.where(
        vector < TILE * members, whole(vector, TILE), vector - members * whole(vector, members)
    )
    found = dot(labels, hot(rows_of((members, slots)) == from_member), ((0,), (0,)))
    vector = lanes_of((16, slots))
    rank = jnp.where(
        vector < TILE * members, vector - TILE * whole(vector, TILE), whole(vector, members)
    )
    ranked = rows_of((16, slots)) == rank
    notes = []
    for k in range(4):
        row = jnp.sum(jnp.where(ranked, found[k * 16 : (k + 1) * 16], 0.0), axis=0, keepdims=True)
        notes += [row[:, q : q + LANES] for q in range(0, slots, LANES)]
    notes.append(jnp.zeros((NOTES - len(notes), LANES), F32))
    notes = jnp.concatenate(notes, axis=0).astype(BF16)
    for j in range(chips):
        out[j, : TILE * members] = (
            values[:, j * TILE : (j + 1) * TILE].reshape(TILE * members, LANES).astype(BF16)
        )
        for p in range(TILE, capacity):
            out[j, p * members : (p + 1) * members] = values[:, p * chips + j].astype(BF16)
        if slots > count:
            out[j, count:slots] = jnp.zeros((slots - count, LANES), BF16)
        out[j, slots : slots + NOTES] = notes
        out[j, slots + NOTES :] = old[:, j * LANES : (j + 1) * LANES]


def labels_of(slots, notes, k):
    chunks = slots // LANES

    def row(d):
        return jnp.concatenate(
            [notes[d * chunks + q : d * chunks + q + 1] for q in range(chunks)], axis=1
        )

    return row(2 * k) - 1.0, row(2 * k + 1)


def sums(groups, where, columns, out, total):
    chips, rows, _ = columns.shape
    slots = rows - NOTES - LANES
    total[...] = jnp.zeros(total.shape, F32)

    def step(s, _):
        notes = columns[s, slots : slots + NOTES].astype(F32)
        group, local = labels_of(slots, notes, 0)
        at = hot(rows_of((LANES, slots)) == local)
        table = jnp.concatenate([at * hot(group == float(g)) for g in range(groups)], axis=0)
        vectors = jnp.concatenate(
            [columns[s, 0:slots], jnp.ones((slots, LANES), BF16)], axis=1
        )
        total[...] += dot(table, vectors, ((1,), (0,)))
        return 0

    lax.fori_loop(0, chips, step, 0)
    identity = rows_of((LANES, LANES)) == lanes_of((LANES, LANES))
    counts = []
    for g in range(groups):
        at = slice(g * LANES, (g + 1) * LANES)
        old = columns[g // 2, slots + NOTES :].astype(F32)
        old = jnp.where(where[1] == g % 2, old, 0.0)
        out[at] = (total[at, :LANES] + old).astype(BF16)
        counts.append(
            jnp.sum(jnp.where(identity, total[at, LANES:], 0.0), axis=0, keepdims=True)
        )
    counts = jnp.concatenate(counts, axis=0)
    high = whole(counts, 256)
    out[groups * LANES : groups * (LANES + 1)] = (counts - 256.0 * high).astype(BF16)
    out[groups * (LANES + 1) :] = high.astype(BF16)


def refit(groups, where, columns, mine, theirs, parts, margins, fresh):
    chips, rows, _ = columns.shape
    slots = rows - NOTES - LANES
    lists = groups * LANES

    def counts_of(sums):
        low = sums[lists : lists + groups].astype(F32)
        return low + 256.0 * sums[lists + groups :].astype(F32)

    counts = counts_of(mine) + counts_of(theirs) + 1.0
    identity = rows_of((LANES, LANES)) == lanes_of((LANES, LANES))
    sizes = []
    for g in range(groups):
        at = slice(g * LANES, (g + 1) * LANES)
        divisor = jnp.sum(jnp.where(identity, counts[g : g + 1], 0.0), axis=1, keepdims=True)
        total = mine[at].astype(F32) + theirs[at].astype(F32)
        value = (total / divisor).astype(BF16)
        fresh[at] = value
        sizes.append(jnp.sum(value.astype(F32) ** 2, axis=1, keepdims=True))
    for s in range(chips):
        one = fresh[2 * s * LANES : (2 * s + 1) * LANES]
        two = fresh[(2 * s + 1) * LANES : (2 * s + 2) * LANES]
        parts[s] = jnp.where(where[1] == 0, one.astype(F32), two.astype(F32)).astype(BF16)

    def step(s, _):
        notes = columns[s, slots : slots + NOTES].astype(F32)
        product = dot(fresh[...], columns[s, 0:slots], ((1,), (1,)))
        distances = [
            sizes[g] - 2.0 * product[g * LANES : (g + 1) * LANES] for g in range(groups)
        ]

        def pick(k):
            group, local = labels_of(slots, notes, k)
            found = jnp.zeros((LANES, slots), F32)
            for g in range(groups):
                found = jnp.where(group == float(g), distances[g], found)
            return jnp.where(rows_of((LANES, slots)) == local, found, 0.0)

        margins[pl.ds(s, 1), :] = jnp.sum(pick(1) - pick(0), axis=0, keepdims=True)
        return 0

    lax.fori_loop(0, chips, step, 0)


def on_device(embeddings, assignment, second_choice, list_slot, old_centroids):
    vectors, width = embeddings.shape
    lists = old_centroids.shape[0]
    members = lax.axis_size("mem")
    chips = lax.axis_size("x")
    capacity = vectors // members + 2
    count = members * capacity

    groups = 2 * chips
    slots = count + -count % LANES

    def across(a):
        return lax.ppermute(a, "core", [(0, 1), (1, 0)])

    def shape(*dims, kind=BF16):
        return jax.ShapeDtypeStruct(dims, kind)

    def exchange(axis, a):
        return lax.all_to_all(a, axis, split_axis=0, concat_axis=0, tiled=True)

    where = jnp.stack([lax.axis_index("x"), lax.axis_index("core")]).astype(jnp.int32)
    payload, place = call(
        functools.partial(prepare, members, capacity),
        "prepare",
        (
            shape(members, capacity * width // LANES + TILE, LANES),
            shape(1, vectors, kind=jnp.int32),
        ),
        2**31,
        assignment.reshape(1, vectors),
        second_choice.reshape(1, vectors),
        list_slot.reshape(-1, LANES),
        embeddings,
    )
    arrived = exchange("mem", payload)
    sent = call(
        functools.partial(spread, capacity),
        "spread",
        shape(chips, slots + NOTES + LANES, LANES),
        2**24,
        arrived,
        old_centroids,
    )
    columns = exchange("x", sent)
    mine = call(
        functools.partial(sums, groups),
        "sums",
        shape(groups * (LANES + 2), LANES),
        2**32,
        columns,
        scalars=where,
        scratch=[pltpu.VMEM((groups * LANES, 2 * LANES), F32)],
    )
    parts, scores = call(
        functools.partial(refit, groups),
        "refit",
        (shape(chips, lists, LANES), shape(chips, slots, kind=F32)),
        2**32,
        columns,
        mine,
        across(mine),
        scalars=where,
        scratch=[pltpu.VMEM((groups * LANES, LANES), BF16)],
    )
    scores = exchange("x", scores.reshape(chips, 1, slots))
    margin = jnp.sum(scores.reshape(chips, slots), axis=0) * (1.0 / width)
    fresh = exchange("x", parts).swapaxes(0, 1).reshape(lists, width)
    margin = jnp.concatenate(
        [
            margin[: TILE * members].reshape(members, TILE),
            margin[TILE * members : count].reshape(capacity - TILE, members).T,
        ],
        axis=1,
    )
    returned = exchange("mem", margin.reshape(members, 1, capacity))
    spots = jnp.arange(count, dtype=jnp.int32)
    margins = jnp.sum(
        jnp.where(place.reshape(vectors, 1) == spots[None, :], returned.reshape(1, count), 0.0),
        axis=1,
    )
    return fresh, margins


def solution(mesh):
    groups, members = mesh.devices.shape
    chip_mesh = Mesh(mesh.devices.reshape(groups // 2, 2, members), ("x", "core", "mem"))
    everywhere = ("x", "core", "mem")
    placed = (
        P(everywhere, None),
        P(everywhere),
        P(everywhere),
        P(),
        P(everywhere, None),
    )
    return jax.shard_map(
        on_device,
        mesh=chip_mesh,
        in_specs=placed,
        out_specs=(P(everywhere, None), P(everywhere)),
        check_vma=False,
    )
```

time: 199 us -> 186 us (0.935)
  starting transfers between devices: 72.7 us -> 15.6 us
  waiting for transfers between devices: 24.9 us -> 47.1 us
  blocking collectives: 76.9 us -> 88.1 us
  Pallas kernels: 15.3 us -> 25.4 us
    ppermute x16 -> x0, starting transfers between devices: 56.2 us -> none  [along(): return lambda a: lax.ppermute(a, ('x', 'core'), pairs)]
    all_to_all x0 -> x2, waiting for transfers between devices: none -> 45.5 us  [exchange(): return lax.all_to_all(a, axis, split_axis=0, concat_axis=0, tiled=True)]
    ppermute x16 -> x0, waiting for transfers between devices: 24.1 us -> none  [along(): return lambda a: lax.ppermute(a, ('x', 'core'), pairs)]
    all_to_all x2 -> x3, blocking collectives: 76.9 us -> 88.1 us  [exchange(): return lax.all_to_all(a, axis, split_axis=0, concat_axis=0, tiled=True)]
    ppermute x2 -> x1, starting transfers between devices: 16.4 us -> 5.67 us  [across(): return lax.ppermute(a, 'core', [(0, 1), (1, 0)])]
    pallas_call x7 -> x4, Pallas kernels: 15.3 us -> 25.4 us  [call(): pl.pallas_call(kernel, in_specs=specs, out_shape=out_shape, scratch_shape...]
    all_to_all x0 -> x2, starting transfers between devices: none -> 9.91 us  [exchange(): return lax.all_to_all(a, axis, split_axis=0, concat_axis=0, tiled=True)]
    unnamed x12 -> x11, local copies, waits for them, and re-layouts: 4.57 us -> 4.48 us
  transfers between devices with their start and end apart: 18 -> 3, of which waited for: 12 -> 3; matrix products, arithmetic and copies ran while one was open for 0% -> 1% of each run, Pallas kernels for 3% -> 0%
where the time goes in v5:
time: 186 us; the launch traced here: 184 us
  blocking collectives  88.1 us (47%)
  waiting for transfers between devices  47.1 us (25%)
  Pallas kernels  25.4 us (14%)
  starting transfers between devices  15.6 us (8%)
  local copies, waits for them, and re-layouts  5.59 us (3%)
    all_to_all x3, blocking collectives, exchange(): return lax.all_to_all(a, axis, split_axis=0, concat_axis=0, tiled=True)  88.1 us
    all_to_all x2, waiting for transfers between devices, exchange(): return lax.all_to_all(a, axis, split_axis=0, concat_axis=0, tiled=True)  45.5 us
    pallas_call x4, Pallas kernels, call(): pl.pallas_call(kernel, in_specs=specs, out_shape=out_shape, scratch_shape...  25.4 us
    all_to_all x2, starting transfers between devices, exchange(): return lax.all_to_all(a, axis, split_axis=0, concat_axis=0, tiled=True)  9.91 us
    ppermute x1, starting transfers between devices, across(): return lax.ppermute(a, 'core', [(0, 1), (1, 0)])  5.67 us
    unnamed x11, local copies, waits for them, and re-layouts  4.48 us
  transfers between devices with their start and end apart: 3, of which 3 were waited for; matrix products, arithmetic and copies ran while one was open for 1% of the time, Pallas kernels for 0%

profile of v5, /device:TPU:1, one launch (start us, length us, event | category | flops | bytes accessed | tf_op | source)
XLA Modules:
  0.0 184.2 jit_solution(5975092378050847200)
XLA Ops:
  0.6 1.2 copy-done.1
  1.9 1.0 copy-done.2
  2.9 0.7 copy-done.3
  3.6 0.7 copy-done.4
  4.3 2.7 %prepare.1 = (bf16[64,88,128]{2,1,0:T(8,128)(2,1)S(1)}, s32[1,512]{1,0:T(1,128)S(1)}) custom-call(s32[1,512]{1,0:T(1,128)S(1)} %bitcast.16, s32[1,512]{1,0:T(1,128)S(1)} %bitcast.17, s32[1024,128]{1,0:T(8,128)S(1)} %bitcast.15, bf16[512,1024]{1,0:T(8,128)(2,1)S(1)} %copy-done.1), custom_call_target="tpu_custom_call" | custom-call | flops 2147483648 | bytes 2097152 | tf_op jit(solution)/shard_map/prepare/pallas_call | solution.py:46
  7.0 58.7 %all_to_all.25.arrived = bf16[64,88,128]{2,1,0:T(8,128)(2,1)S(1)} all-to-all(bf16[64,88,128]{2,1,0:T(8,128)(2,1)S(1)} %get-tuple-element.6), channel_id=1, replica_groups=mesh['x'=8,'core'=2,'mem'=64] {'mem'}, dimensions={0} | all-to-all | bytes 2883584 | tf_op jit(solution)/shard_map/all_to_all | solution.py:250
  65.7 1.9 %spread.1 = bf16[8,800,128]{2,1,0:T(8,128)(2,1)} custom-call(bf16[64,88,128]{2,1,0:T(8,128)(2,1)S(1)} %all_to_all.25.arrived, bf16[128,1024]{1,0:T(8,128)(2,1)S(1)} %copy-done), custom_call_target="tpu_custom_call" | custom-call | flops 16777216 | bytes 2097152 | tf_op jit(solution)/shard_map/spread/pallas_call | solution.py:46
  67.6 6.5 %all-to-all-start.1 = ((bf16[8,800,128]{2,1,0:T(8,128)(2,1)}), bf16[8,800,128]{2,1,0:T(8,128)(2,1)S(1)}, u32[]{:S(2)}, u32[]{:S(2)}) async-start(bf16[8,800,128]{2,1,0:T(8,128)(2,1)} %spread.1), calls=%async_computation.1 | async-start | bytes 3276800 | tf_op jit(solution)/shard_map/all_to_all | solution.py:250
  74.2 38.5 %all-to-all-done.1.columns = bf16[8,800,128]{2,1,0:T(8,128)(2,1)S(1)} async-done(((bf16[8,800,128]{2,1,0:T(8,128)(2,1)}), bf16[8,800,128]{2,1,0:T(8,128)(2,1)S(1)}, u32[]{:S(2)}, u32[]{:S(2)}) %all-to-all-start.1) | async-done | bytes 1638432 | tf_op jit(solution)/shard_map/all_to_all | solution.py:250
  112.7 8.8 %sums.1.mine = bf16[2080,128]{1,0:T(8,128)(2,1)S(1)} custom-call(s32[2]{0:T(128)S(1)} %pad_add_fusion.where, bf16[8,800,128]{2,1,0:T(8,128)(2,1)S(1)} %all-to-all-done.1.columns), custom_call_target="tpu_custom_call" | custom-call | flops 4294967296 | bytes 2097152 | tf_op jit(solution)/shard_map/sums/pallas_call | solution.py:46
  121.5 5.7 %collective-permute-start = (bf16[2080,128]{1,0:T(8,128)(2,1)S(1)}, bf16[2080,128]{1,0:T(8,128)(2,1)S(1)}, u32[]{:S(2)}, u32[]{:S(2)}) collective-permute-start(bf16[2080,128]{1,0:T(8,128)(2,1)S(1)} %sums.1.mine), channel_id=1, source_target_pairs={{0,64},{64,0},{1,65},{65,1},{2,66},{66,2},{3,67},{67,3},{4,68},{68... | collective-permute-start | bytes 1597448 | tf_op jit(solution)/shard_map/ppermute | solution.py:244
  127.2 1.5 collective-permute-done.theirs
  128.7 11.9 %refit.1 = (bf16[8,128,128]{2,1,0:T(8,128)(2,1)}, f32[8,640]{1,0:T(8,128)S(1)}) custom-call(s32[2]{0:T(128)S(1)} %pad_add_fusion.where, bf16[8,800,128]{2,1,0:T(8,128)(2,1)S(1)} %all-to-all-done.1.columns, bf16[2080,128]{1,0:T(8,128)(2,1)S(1)} %sums.1.mine, bf16[2080,128]{1,0:T(8,128)(2,1)S(1)} %collective-permute-done.theirs), custom_call_target="tpu_custom_call" | custom-call | flops 4294967296 | bytes 2097152 | tf_op jit(solution)/shard_map/refit/pallas_call | solution.py:46
  140.6 9.0 %all_to_all.26 = f32[8,1,640]{2,1,0:T(1,128)S(1)} all-to-all(f32[8,1,640]{2,1,0:T(1,128)S(1)} %copy.17), channel_id=1, replica_groups=mesh['x'=8,'core'=2,'mem'=64] {'x'}, dimensions={0} | all-to-all | bytes 40960 | tf_op jit(solution)/shard_map/all_to_all | solution.py:250
  149.9 0.1 copy.18
  150.0 20.4 %all_to_all.27 = f32[64,1,10]{2,1,0:T(1,128)S(1)} all-to-all(f32[64,1,10]{2,1,0:T(1,128)S(1)} %bitcast.21), channel_id=1, replica_groups=mesh['x'=8,'core'=2,'mem'=64] {'mem'}, dimensions={0} | all-to-all | bytes 5120 | tf_op jit(solution)/shard_map/all_to_all | solution.py:250
  170.5 3.4 %all-to-all-start.2 = ((bf16[8,128,128]{2,1,0:T(8,128)(2,1)}), bf16[8,128,128]{2,1,0:T(8,128)(2,1)S(1)}, u32[]{:S(2)}, u32[]{:S(2)}) async-start(bf16[8,128,128]{2,1,0:T(8,128)(2,1)} %get-tuple-element.7), calls=%async_computation.2 | async-start | bytes 524288 | tf_op jit(solution)/shard_map/all_to_all | solution.py:250
  173.9 0.5 broadcast.9
  174.4 0.7 reduce.4
  175.1 0.1 broadcast_in_dim.15
  175.3 0.9 select_reduce_fusion
  176.1 7.0 %all-to-all-done.2 = bf16[8,128,128]{2,1,0:T(8,128)(2,1)S(1)} async-done(((bf16[8,128,128]{2,1,0:T(8,128)(2,1)}), bf16[8,128,128]{2,1,0:T(8,128)(2,1)S(1)}, u32[]{:S(2)}, u32[]{:S(2)}) %all-to-all-start.2) | async-done | bytes 262176 | tf_op jit(solution)/shard_map/all_to_all | solution.py:250
  183.2 0.2 copy.16
  183.4 0.9 copy.20
  (15 shorter events, 0.4 us)
Async XLA Ops:
  0.6 1.2 copy-start.1
  1.9 1.0 copy-start.2
  2.9 0.7 copy-start.3
  3.6 0.7 copy-start.4
  7.0 58.7 %copy-start = (bf16[128,1024]{1,0:T(8,128)(2,1)S(1)}, bf16[128,1024]{1,0:T(8,128)(2,1)}, u32[]{:S(2)}) copy-start(bf16[128,1024]{1,0:T(8,128)(2,1)} %old.1) | copy-start | bytes 786436
  67.6 45.1 %all-to-all-start.1 = ((bf16[8,800,128]{2,1,0:T(8,128)(2,1)}), bf16[8,800,128]{2,1,0:T(8,128)(2,1)S(1)}, u32[]{:S(2)}, u32[]{:S(2)}) async-start(bf16[8,800,128]{2,1,0:T(8,128)(2,1)} %spread.1), calls=%async_computation.1 | async-start | bytes 3276800 | tf_op jit(solution)/shard_map/all_to_all | solution.py:250
  121.5 7.2 %collective-permute-start = (bf16[2080,128]{1,0:T(8,128)(2,1)S(1)}, bf16[2080,128]{1,0:T(8,128)(2,1)S(1)}, u32[]{:S(2)}, u32[]{:S(2)}) collective-permute-start(bf16[2080,128]{1,0:T(8,128)(2,1)S(1)} %sums.1.mine), channel_id=1, source_target_pairs={{0,64},{64,0},{1,65},{65,1},{2,66},{66,2},{3,67},{67,3},{4,68},{68... | collective-permute-start | bytes 1597448 | tf_op jit(solution)/shard_map/ppermute | solution.py:244
  170.5 12.7 %all-to-all-start.2 = ((bf16[8,128,128]{2,1,0:T(8,128)(2,1)}), bf16[8,128,128]{2,1,0:T(8,128)(2,1)S(1)}, u32[]{:S(2)}, u32[]{:S(2)}) async-start(bf16[8,128,128]{2,1,0:T(8,128)(2,1)} %get-tuple-element.7), calls=%async_computation.2 | async-start | bytes 524288 | tf_op jit(solution)/shard_map/all_to_all | solution.py:250

commit v6 on v5

--- a/solution.py
+++ b/solution.py
@@ -38,8 +38,8 @@
     return jnp.floor((a + 0.5) * (1.0 / size))
 
 
-def call(kernel, name, out_shape, flops, *args, scalars=None, scratch=()):
-    specs = [VMEM] * len(args)
+def call(kernel, name, out_shape, flops, *args, scalars=None, scratch=(), space=VMEM, limit=LIMIT):
+    specs = [space] * len(args)
     if scalars is not None:
         specs = [SMEM] + specs
         args = (scalars,) + args
@@ -48,13 +48,23 @@
         in_specs=specs,
         out_shape=out_shape,
         scratch_shapes=scratch,
-        compiler_params=pltpu.CompilerParams(vmem_limit_bytes=LIMIT),
+        compiler_params=pltpu.CompilerParams(vmem_limit_bytes=limit),
         cost_estimate=pl.CostEstimate(flops=flops, bytes_accessed=2**21, transcendentals=0),
         name=name,
     )(*args)
 
 
-def prepare(members, capacity, first, second, table, embeddings, payload, place):
+def prepare(members, capacity, *refs):
+    sources, (payload, place), scratch = refs[:4], refs[4:6], refs[6:]
+    first, second, table, embeddings, sems = scratch
+    copies = [
+        pltpu.make_async_copy(source, to, sems.at[n])
+        for n, (source, to) in enumerate(zip(sources, scratch))
+    ]
+    for copy in copies:
+        copy.start()
+    for copy in copies[:3]:
+        copy.wait()
     vectors = first.shape[1]
     parts = embeddings.shape[1] // LANES
     slots = table[...]
@@ -85,6 +95,7 @@
     place[...] = (first_owner * capacity + rank).astype(jnp.int32)
     spot = jnp.where(rank < TILE, first_owner * TILE + rank, rank * members + first_owner)
     order = hot(rows_of((members * capacity, vectors)) == spot)
+    copies[3].wait()
     packed = dot(order, embeddings[...], ((1,), (0,)))
     ranked = rows_of((16, vectors)) == rank
     digits = [first_group + 1.0, first_local, second_group + 1.0, second_local]
@@ -106,11 +117,11 @@
     payload[...] = jnp.concatenate(pieces, axis=1).astype(BF16)
 
 
-def spread(capacity, arrived, old, out):
+def spread(capacity, arrived, out):
     members = arrived.shape[0]
     count = members * capacity
     chips, rows, _ = out.shape
-    slots = rows - NOTES - LANES
+    slots = rows - NOTES
     values = arrived[...].astype(F32)
     labels = values[:, capacity * chips].astype(BF16)
     vector = lanes_of((members, slots))
@@ -137,8 +148,7 @@
             out[j, p * members : (p + 1) * members] = values[:, p * chips + j].astype(BF16)
         if slots > count:
             out[j, count:slots] = jnp.zeros((slots - count, LANES), BF16)
-        out[j, slots : slots + NOTES] = notes
-        out[j, slots + NOTES :] = old[:, j * LANES : (j + 1) * LANES]
+        out[j, slots:] = notes
 
 
 def labels_of(slots, notes, k):
@@ -152,42 +162,65 @@
     return row(2 * k) - 1.0, row(2 * k + 1)
 
 
-def sums(groups, where, columns, out, total):
+def turn(where, old, *outs):
+    chips = len(outs)
+    for d in range(chips):
+        at = lax.rem(where[0] + d, chips)
+        outs[d][...] = old[:, pl.ds(pl.multiple_of(at * LANES, LANES), LANES)]
+
+
+def bare(wide):
+    return jnp.concatenate([wide, jnp.ones(wide.shape, BF16)], axis=1)
+
+
+def pair_of(columns, slots, t):
+    both = [columns[2 * t + n, 0:slots] for n in range(2)]
+    notes = [columns[2 * t + n, slots:].astype(F32) for n in range(2)]
+
+    def labels(k):
+        found = [labels_of(slots, note, k) for note in notes]
+        return (
+            jnp.concatenate([found[0][0], found[1][0]], axis=1),
+            jnp.concatenate([found[0][1], found[1][1]], axis=1),
+        )
+
+    return bare(jnp.concatenate(both, axis=0)), labels
+
+
+def sums(groups, where, columns, *refs):
+    olds, (out, total) = refs[:-2], refs[-2:]
     chips, rows, _ = columns.shape
-    slots = rows - NOTES - LANES
+    slots = rows - NOTES
     total[...] = jnp.zeros(total.shape, F32)
 
-    def step(s, _):
-        notes = columns[s, slots : slots + NOTES].astype(F32)
-        group, local = labels_of(slots, notes, 0)
-        at = hot(rows_of((LANES, slots)) == local)
+    def step(t, _):
+        vectors, labels = pair_of(columns, slots, t)
+        group, local = labels(0)
+        at = hot(rows_of((LANES, 2 * slots)) == local)
         table = jnp.concatenate([at * hot(group == float(g)) for g in range(groups)], axis=0)
-        vectors = jnp.concatenate(
-            [columns[s, 0:slots], jnp.ones((slots, LANES), BF16)], axis=1
-        )
         total[...] += dot(table, vectors, ((1,), (0,)))
         return 0
 
-    lax.fori_loop(0, chips, step, 0)
+    lax.fori_loop(0, chips // 2, step, 0)
     identity = rows_of((LANES, LANES)) == lanes_of((LANES, LANES))
     counts = []
     for g in range(groups):
         at = slice(g * LANES, (g + 1) * LANES)
-        old = columns[g // 2, slots + NOTES :].astype(F32)
-        old = jnp.where(where[1] == g % 2, old, 0.0)
-        out[at] = (total[at, :LANES] + old).astype(BF16)
         counts.append(
             jnp.sum(jnp.where(identity, total[at, LANES:], 0.0), axis=0, keepdims=True)
         )
+    for d, old in enumerate(olds):
+        chip = lax.rem(where[0] + chips - d, chips)
+        at = pl.ds(pl.multiple_of((2 * chip + where[1]) * LANES, LANES), LANES)
+        total[at, :LANES] += old[...].astype(F32)
+    out[: groups * LANES] = total[:, :LANES].astype(BF16)
     counts = jnp.concatenate(counts, axis=0)
     high = whole(counts, 256)
     out[groups * LANES : groups * (LANES + 1)] = (counts - 256.0 * high).astype(BF16)
     out[groups * (LANES + 1) :] = high.astype(BF16)
 
 
-def refit(groups, where, columns, mine, theirs, parts, margins, fresh):
-    chips, rows, _ = columns.shape
-    slots = rows - NOTES - LANES
+def refit(groups, where, mine, theirs, parts, lists_of):
     lists = groups * LANES
 
     def counts_of(sums):
@@ -196,37 +229,48 @@
 
     counts = counts_of(mine) + counts_of(theirs) + 1.0
     identity = rows_of((LANES, LANES)) == lanes_of((LANES, LANES))
-    sizes = []
+    lane = lanes_of((LANES, LANES))
+    values = []
     for g in range(groups):
         at = slice(g * LANES, (g + 1) * LANES)
         divisor = jnp.sum(jnp.where(identity, counts[g : g + 1], 0.0), axis=1, keepdims=True)
         total = mine[at].astype(F32) + theirs[at].astype(F32)
-        value = (total / divisor).astype(BF16)
-        fresh[at] = value
-        sizes.append(jnp.sum(value.astype(F32) ** 2, axis=1, keepdims=True))
-    for s in range(chips):
-        one = fresh[2 * s * LANES : (2 * s + 1) * LANES]
-        two = fresh[(2 * s + 1) * LANES : (2 * s + 2) * LANES]
-        parts[s] = jnp.where(where[1] == 0, one.astype(F32), two.astype(F32)).astype(BF16)
-
-    def step(s, _):
-        notes = columns[s, slots : slots + NOTES].astype(F32)
-        product = dot(fresh[...], columns[s, 0:slots], ((1,), (1,)))
-        distances = [
-            sizes[g] - 2.0 * product[g * LANES : (g + 1) * LANES] for g in range(groups)
-        ]
+        value = (total / divisor).astype(BF16).astype(F32)
+        values.append(value)
+        size = jnp.sum(value * value, axis=1, keepdims=True)
+        one = size.astype(BF16).astype(F32)
+        two = (size - one).astype(BF16).astype(F32)
+        three = size - one - two
+        sizes = jnp.where(lane == 0.0, one, jnp.where(lane == 1.0, two, 0.0))
+        sizes = jnp.where(lane == 2.0, three, sizes)
+        lists_of[at] = jnp.concatenate([-2.0 * value, sizes], axis=1).astype(BF16)
+    for s in range(groups // 2):
+        parts[s] = jnp.where(where[1] == 0, values[2 * s], values[2 * s + 1]).astype(BF16)
+
+
+def score(groups, columns, lists_of, margins):
+    chips, rows, _ = columns.shape
+    slots = rows - NOTES
+
+    def step(t, _):
+        vectors, labels = pair_of(columns, slots, t)
+        distance = dot(lists_of[...], vectors, ((1,), (1,)))
 
         def pick(k):
-            group, local = labels_of(slots, notes, k)
-            found = jnp.zeros((LANES, slots), F32)
+            group, local = labels(k)
+            found = jnp.zeros((LANES, 2 * slots), F32)
             for g in range(groups):
-                found = jnp.where(group == float(g), distances[g], found)
-            return jnp.where(rows_of((LANES, slots)) == local, found, 0.0)
-
-        margins[pl.ds(s, 1), :] = jnp.sum(pick(1) - pick(0), axis=0, keepdims=True)
+                found = jnp.where(
+                    group == float(g), distance[g * LANES : (g + 1) * LANES], found
+                )
+            return jnp.where(rows_of((LANES, 2 * slots)) == local, found, 0.0)
+
+        margin = jnp.sum(pick(1) - pick(0), axis=0, keepdims=True)
+        margins[pl.ds(2 * t, 1), :] = margin[:, :slots]
+        margins[pl.ds(2 * t + 1, 1), :] = margin[:, slots:]
         return 0
 
-    lax.fori_loop(0, chips, step, 0)
+    lax.fori_loop(0, chips // 2, step, 0)
 
 
 def on_device(embeddings, assignment, second_choice, list_slot, old_centroids):
@@ -262,15 +306,27 @@
         second_choice.reshape(1, vectors),
         list_slot.reshape(-1, LANES),
         embeddings,
+        scratch=[
+            pltpu.VMEM((1, vectors), jnp.int32),
+            pltpu.VMEM((1, vectors), jnp.int32),
+            pltpu.VMEM((list_slot.shape[0] // LANES, LANES), jnp.int32),
+            pltpu.VMEM((vectors, width), BF16),
+            pltpu.SemaphoreType.DMA((4,)),
+        ],
+        space=pl.BlockSpec(memory_space=pl.ANY),
+        limit=60 * 2**20,
     )
     arrived = exchange("mem", payload)
+    turned = call(turn, "turn", [shape(lists, LANES)] * chips, 2**20, old_centroids, scalars=where)
+    olds = [turned[0]]
+    for d in range(1, chips):
+        olds.append(lax.ppermute(turned[d], "x", [(i, (i + d) % chips) for i in range(chips)]))
     sent = call(
         functools.partial(spread, capacity),
         "spread",
-        shape(chips, slots + NOTES + LANES, LANES),
+        shape(chips, slots + NOTES, LANES),
         2**24,
         arrived,
-        old_centroids,
     )
     columns = exchange("x", sent)
     mine = call(
@@ -279,23 +335,32 @@
         shape(groups * (LANES + 2), LANES),
         2**32,
         columns,
+        *olds,
         scalars=where,
         scratch=[pltpu.VMEM((groups * LANES, 2 * LANES), F32)],
     )
-    parts, scores = call(
+    parts, lists_of = call(
         functools.partial(refit, groups),
         "refit",
-        (shape(chips, lists, LANES), shape(chips, slots, kind=F32)),
-        2**32,
-        columns,
+        (shape(chips, lists, LANES), shape(groups * LANES, 2 * LANES)),
+        2**24,
         mine,
         across(mine),
         scalars=where,
-        scratch=[pltpu.VMEM((groups * LANES, LANES), BF16)],
-    )
+    )
+    returned_parts = exchange("x", parts)
+    scores = call(
+        functools.partial(score, groups),
+        "score",
+        shape(chips, slots, kind=F32),
+        2**33,
+        columns,
+        lists_of,
+    )
+    scores, returned_parts = lax.optimization_barrier((scores, returned_parts))
+    fresh = returned_parts.swapaxes(0, 1).reshape(lists, width)
     scores = exchange("x", scores.reshape(chips, 1, slots))
     margin = jnp.sum(scores.reshape(chips, slots), axis=0) * (1.0 / width)
-    fresh = exchange("x", parts).swapaxes(0, 1).reshape(lists, width)
     margin = jnp.concatenate(
         [
             margin[: TILE * members].reshape(members, TILE),

time: 186 us -> 185 us (level)
  starting transfers between devices: 15.6 us -> 61.3 us
  waiting for transfers between devices: 47.1 us -> 20.6 us
  blocking collectives: 88.1 us -> 69.7 us
  local copies, waits for them, and re-layouts: 5.59 us -> 2 us
    all_to_all x2 -> x3, waiting for transfers between devices: 45.5 us -> 11.9 us  [exchange(): return lax.all_to_all(a, axis, split_axis=0, concat_axis=0, tiled=True)]
    ppermute x0 -> x7, starting transfers between devices: none -> 31.9 us  [on_device(): lax.ppermute(turned[d], 'x', [(i, (i + d) % chips) for i in range(chips)])]
    all_to_all x3 -> x2, blocking collectives: 88.1 us -> 69.7 us  [exchange(): return lax.all_to_all(a, axis, split_axis=0, concat_axis=0, tiled=True)]
    all_to_all x2 -> x3, starting transfers between devices: 9.91 us -> 20.9 us  [exchange(): return lax.all_to_all(a, axis, split_axis=0, concat_axis=0, tiled=True)]
    ppermute x0 -> x7, waiting for transfers between devices: none -> 7.11 us  [on_device(): lax.ppermute(turned[d], 'x', [(i, (i + d) % chips) for i in range(chips)])]
    unnamed x11 -> x5, local copies, waits for them, and re-layouts: 4.48 us -> 0.86 us
    ppermute x1, starting transfers between devices: 5.67 us -> 8.53 us  [across(): return lax.ppermute(a, 'core', [(0, 1), (1, 0)])]
    pallas_call x4 -> x6, Pallas kernels: 25.4 us -> 26.2 us  [call(): pl.pallas_call(kernel, in_specs=specs, out_shape=out_shape, scratch_shape...]
  transfers between devices with their start and end apart: 3 -> 11, of which waited for: 3 -> 5; matrix products, arithmetic and copies ran while one was open for 1% -> 1% of each run, Pallas kernels for 0% -> 5%
where the time goes in v6:
time: 185 us; the launch traced here: 183 us
  blocking collectives  69.7 us (38%)
  starting transfers between devices  61.3 us (33%)
  Pallas kernels  26.2 us (14%)
  waiting for transfers between devices  20.6 us (11%)
  other arithmetic  2.39 us (1%)
  local copies, waits for them, and re-layouts  2 us (1%)
    all_to_all x2, blocking collectives, exchange(): return lax.all_to_all(a, axis, split_axis=0, concat_axis=0, tiled=True)  69.7 us
    ppermute x7, starting transfers between devices, on_device(): lax.ppermute(turned[d], 'x', [(i, (i + d) % chips) for i in range(chips)])  31.9 us
    pallas_call x6, Pallas kernels, call(): pl.pallas_call(kernel, in_specs=specs, out_shape=out_shape, scratch_shape...  26.2 us
    all_to_all x3, starting transfers between devices, exchange(): return lax.all_to_all(a, axis, split_axis=0, concat_axis=0, tiled=True)  20.9 us
    all_to_all x3, waiting for transfers between devices, exchange(): return lax.all_to_all(a, axis, split_axis=0, concat_axis=0, tiled=True)  11.9 us
    ppermute x1, starting transfers between devices, across(): return lax.ppermute(a, 'core', [(0, 1), (1, 0)])  8.53 us
    ppermute x7, waiting for transfers between devices, on_device(): lax.ppermute(turned[d], 'x', [(i, (i + d) % chips) for i in range(chips)])  7.11 us
  transfers between devices with their start and end apart: 11, of which 5 were waited for; matrix products, arithmetic and copies ran while one was open for 1% of the time, Pallas kernels for 5%

profile of v6, /device:TPU:1, one launch (start us, length us, event | category | flops | bytes accessed | tf_op | source)
XLA Modules:
  0.0 183.0 jit_solution(10514080996964754125)
XLA Ops:
  0.6 5.2 %prepare.1 = (bf16[64,88,128]{2,1,0:T(8,128)(2,1)}, s32[1,512]{1,0:T(1,128)}) custom-call(s32[1,512]{1,0:T(1,128)} %bitcast.19, s32[1,512]{1,0:T(1,128)} %bitcast.20, s32[1024,128]{1,0:T(8,128)} %bitcast.18, bf16[512,1024]{1,0:T(8,128)(2,1)} %refs_3_.1), custom_call_target="tpu_custom_call" | custom-call | flops 2147483648 | bytes 2097152 | tf_op jit(solution)/shard_map/prepare/pallas_call | solution.py:46
  5.9 58.8 %all_to_all.25.arrived = bf16[64,88,128]{2,1,0:T(8,128)(2,1)S(1)} all-to-all(bf16[64,88,128]{2,1,0:T(8,128)(2,1)} %get-tuple-element.16), channel_id=1, replica_groups=mesh['x'=8,'core'=2,'mem'=64] {'mem'}, dimensions={0} | all-to-all | bytes 2883584 | tf_op jit(solution)/shard_map/all_to_all | solution.py:294
  64.6 1.8 %spread.1 = bf16[8,672,128]{2,1,0:T(8,128)(2,1)} custom-call(bf16[64,88,128]{2,1,0:T(8,128)(2,1)S(1)} %all_to_all.25.arrived), custom_call_target="tpu_custom_call" | custom-call | flops 16777216 | bytes 2097152 | tf_op jit(solution)/shard_map/spread/pallas_call | solution.py:46
  66.5 6.6 %all-to-all-start.1 = ((bf16[8,672,128]{2,1,0:T(8,128)(2,1)}), bf16[8,672,128]{2,1,0:T(8,128)(2,1)S(1)}, u32[]{:S(2)}, u32[]{:S(2)}) async-start(bf16[8,672,128]{2,1,0:T(8,128)(2,1)} %spread.1), calls=%async_computation.1 | async-start | bytes 2752512 | tf_op jit(solution)/shard_map/all_to_all | solution.py:294
  73.8 3.4 %collective-permute-start = (bf16[128,128]{1,0:T(8,128)(2,1)S(1)}, bf16[128,128]{1,0:T(8,128)(2,1)S(1)}, u32[]{:S(2)}, u32[]{:S(2)}) collective-permute-start(bf16[128,128]{1,0:T(8,128)(2,1)S(1)} %get-tuple-element.18), channel_id=1, source_target_pairs={{0,128},{128,256},{256,384},{384,512},{512,640},{640,768},{768,896... | collective-permute-start | bytes 98312 | tf_op jit(solution)/shard_map/ppermute | solution.py:323
  77.2 4.0 %collective-permute-start.1 = (bf16[128,128]{1,0:T(8,128)(2,1)S(1)}, bf16[128,128]{1,0:T(8,128)(2,1)S(1)}, u32[]{:S(2)}, u32[]{:S(2)}) collective-permute-start(bf16[128,128]{1,0:T(8,128)(2,1)S(1)} %get-tuple-element.19), channel_id=1, source_target_pairs={{0,256},{128,384},{256,512},{384,640},{512,768},{640,896},{768,0},... | collective-permute-start | bytes 98312 | tf_op jit(solution)/shard_map/ppermute | solution.py:323
  81.2 4.3 %collective-permute-start.2 = (bf16[128,128]{1,0:T(8,128)(2,1)S(1)}, bf16[128,128]{1,0:T(8,128)(2,1)S(1)}, u32[]{:S(2)}, u32[]{:S(2)}) collective-permute-start(bf16[128,128]{1,0:T(8,128)(2,1)S(1)} %get-tuple-element.20), channel_id=1, source_target_pairs={{0,384},{128,512},{256,640},{384,768},{512,896},{640,0},{768,128},... | collective-permute-start | bytes 98312 | tf_op jit(solution)/shard_map/ppermute | solution.py:323
  85.5 4.0 %collective-permute-start.3 = (bf16[128,128]{1,0:T(8,128)(2,1)S(1)}, bf16[128,128]{1,0:T(8,128)(2,1)S(1)}, u32[]{:S(2)}, u32[]{:S(2)}) collective-permute-start(bf16[128,128]{1,0:T(8,128)(2,1)S(1)} %get-tuple-element.21), channel_id=1, source_target_pairs={{0,512},{128,640},{256,768},{384,896},{512,0},{640,128},{768,256},... | collective-permute-start | bytes 98312 | tf_op jit(solution)/shard_map/ppermute | solution.py:323
  89.5 4.3 %collective-permute-start.4 = (bf16[128,128]{1,0:T(8,128)(2,1)S(1)}, bf16[128,128]{1,0:T(8,128)(2,1)S(1)}, u32[]{:S(2)}, u32[]{:S(2)}) collective-permute-start(bf16[128,128]{1,0:T(8,128)(2,1)S(1)} %get-tuple-element.22), channel_id=1, source_target_pairs={{0,640},{128,768},{256,896},{384,0},{512,128},{640,256},{768,384},... | collective-permute-start | bytes 98312 | tf_op jit(solution)/shard_map/ppermute | solution.py:323
  93.8 6.1 %collective-permute-done.refs_1_ = bf16[128,128]{1,0:T(8,128)(2,1)S(1)} collective-permute-done((bf16[128,128]{1,0:T(8,128)(2,1)S(1)}, bf16[128,128]{1,0:T(8,128)(2,1)S(1)}, u32[]{:S(2)}, u32[]{:S(2)}) %collective-permute-start) | collective-permute-done | bytes 32800 | tf_op jit(solution)/shard_map/ppermute | solution.py:323
  99.9 4.7 %collective-permute-start.5 = (bf16[128,128]{1,0:T(8,128)(2,1)S(1)}, bf16[128,128]{1,0:T(8,128)(2,1)S(1)}, u32[]{:S(2)}, u32[]{:S(2)}) collective-permute-start(bf16[128,128]{1,0:T(8,128)(2,1)S(1)} %get-tuple-element.23), channel_id=1, source_target_pairs={{0,768},{128,896},{256,0},{384,128},{512,256},{640,384},{768,512},... | collective-permute-start | bytes 98312 | tf_op jit(solution)/shard_map/ppermute | solution.py:323
  104.6 7.2 %collective-permute-start.6 = (bf16[128,128]{1,0:T(8,128)(2,1)S(1)}, bf16[128,128]{1,0:T(8,128)(2,1)S(1)}, u32[]{:S(2)}, u32[]{:S(2)}) collective-permute-start(bf16[128,128]{1,0:T(8,128)(2,1)S(1)} %get-tuple-element.24), channel_id=1, source_target_pairs={{0,896},{128,0},{256,128},{384,256},{512,384},{640,512},{768,640},... | collective-permute-start | bytes 98312 | tf_op jit(solution)/shard_map/ppermute | solution.py:323
  111.9 1.0 collective-permute-done.6.refs_7_
  112.8 7.0 %sums.1.mine = bf16[2080,128]{1,0:T(8,128)(2,1)S(1)} custom-call(s32[2]{0:T(128)S(1)} %pad_add_fusion.where, bf16[8,672,128]{2,1,0:T(8,128)(2,1)S(1)} %all-to-all-done.1.columns, bf16[128,128]{1,0:T(8,128)(2,1)S(1)} %get-tuple-element.17.refs_0_, bf16[128,128]{1,0:T(8,128)(2,1)S(1)} %collective-permute-done.refs_1_, ...), custom_call_target="tpu_custom_call" | custom-call | flops 4294967296 | bytes 2097152 | tf_op jit(solution)/shard_map/sums/pallas_call | solution.py:46
  119.9 8.5 %collective-permute-start.7 = (bf16[2080,128]{1,0:T(8,128)(2,1)S(1)}, bf16[2080,128]{1,0:T(8,128)(2,1)S(1)}, u32[]{:S(2)}, u32[]{:S(2)}) collective-permute-start(bf16[2080,128]{1,0:T(8,128)(2,1)S(1)} %sums.1.mine), channel_id=1, source_target_pairs={{0,64},{64,0},{1,65},{65,1},{2,66},{66,2},{3,67},{67,3},{4,68},{68... | collective-permute-start | bytes 1597448 | tf_op jit(solution)/shard_map/ppermute | solution.py:288
  128.4 1.5 collective-permute-done.7.theirs
  129.9 2.6 %refit.1 = (bf16[8,128,128]{2,1,0:T(8,128)(2,1)}, bf16[2048,256]{1,0:T(8,128)(2,1)S(1)}) custom-call(s32[2]{0:T(128)S(1)} %pad_add_fusion.where, bf16[2080,128]{1,0:T(8,128)(2,1)S(1)} %sums.1.mine, bf16[2080,128]{1,0:T(8,128)(2,1)S(1)} %collective-permute-done.7.theirs), custom_call_target="tpu_custom_call" | custom-call | flops 16777216 | bytes 2097152 | tf_op jit(solution)/shard_map/refit/pallas_call | solution.py:46
  132.5 4.5 %all-to-all-start.2 = ((bf16[8,128,128]{2,1,0:T(8,128)(2,1)}), bf16[8,128,128]{2,1,0:T(8,128)(2,1)S(1)}, u32[]{:S(2)}, u32[]{:S(2)}) async-start(bf16[8,128,128]{2,1,0:T(8,128)(2,1)} %get-tuple-element.26), calls=%async_computation.2 | async-start | bytes 524288 | tf_op jit(solution)/shard_map/all_to_all | solution.py:294
  137.0 8.9 %score.1 = f32[8,640]{1,0:T(8,128)S(1)} custom-call(bf16[8,672,128]{2,1,0:T(8,128)(2,1)S(1)} %all-to-all-done.1.columns, bf16[2048,256]{1,0:T(8,128)(2,1)S(1)} %get-tuple-element.25.lists_of), custom_call_target="tpu_custom_call" | custom-call | flops 8589934592 | bytes 2097152 | tf_op jit(solution)/shard_map/score/pallas_call | solution.py:46
  145.9 2.1 %all-to-all-done.2 = bf16[8,128,128]{2,1,0:T(8,128)(2,1)S(1)} async-done(((bf16[8,128,128]{2,1,0:T(8,128)(2,1)}), bf16[8,128,128]{2,1,0:T(8,128)(2,1)S(1)}, u32[]{:S(2)}, u32[]{:S(2)}) %all-to-all-start.2) | async-done | bytes 262176 | tf_op jit(solution)/shard_map/all_to_all | solution.py:294
  148.1 11.0 %all_to_all.26 = f32[8,1,640]{2,1,0:T(1,128)S(1)} all-to-all(f32[8,1,640]{2,1,0:T(1,128)S(1)} %copy.17), channel_id=1, replica_groups=mesh['x'=8,'core'=2,'mem'=64] {'x'}, dimensions={0} | all-to-all | bytes 40960 | tf_op jit(solution)/shard_map/all_to_all | solution.py:294
  160.1 9.8 %all-to-all-start.4 = ((f32[64,1,10]{2,1,0:T(1,128)}), f32[64,1,10]{2,1,0:T(1,128)S(1)}, u32[]{:S(2)}, u32[]{:S(2)}) async-start(f32[64,1,10]{2,1,0:T(1,128)} %bitcast.11), calls=%async_computation.4 | async-start | bytes 65536 | tf_op jit(solution)/shard_map/all_to_all | solution.py:294
  170.9 9.8 %all-to-all-done.4 = f32[64,1,10]{2,1,0:T(1,128)S(1)} async-done(((f32[64,1,10]{2,1,0:T(1,128)}), f32[64,1,10]{2,1,0:T(1,128)S(1)}, u32[]{:S(2)}, u32[]{:S(2)}) %all-to-all-start.4) | async-done | bytes 2592 | tf_op jit(solution)/shard_map/all_to_all | solution.py:294
  182.1 0.9 select_reduce_fusion
  (26 shorter events, 4.1 us)
Async XLA Ops:
  66.5 6.7 %copy-start = (bf16[128,1024]{1,0:T(8,128)(2,1)S(1)}, bf16[128,1024]{1,0:T(8,128)(2,1)}, u32[]{:S(2)}) copy-start(bf16[128,1024]{1,0:T(8,128)(2,1)} %old.1) | copy-start | bytes 786436
  66.5 46.4 %all-to-all-start.1 = ((bf16[8,672,128]{2,1,0:T(8,128)(2,1)}), bf16[8,672,128]{2,1,0:T(8,128)(2,1)S(1)}, u32[]{:S(2)}, u32[]{:S(2)}) async-start(bf16[8,672,128]{2,1,0:T(8,128)(2,1)} %spread.1), calls=%async_computation.1 | async-start | bytes 2752512 | tf_op jit(solution)/shard_map/all_to_all | solution.py:294
  73.8 26.1 %collective-permute-start = (bf16[128,128]{1,0:T(8,128)(2,1)S(1)}, bf16[128,128]{1,0:T(8,128)(2,1)S(1)}, u32[]{:S(2)}, u32[]{:S(2)}) collective-permute-start(bf16[128,128]{1,0:T(8,128)(2,1)S(1)} %get-tuple-element.18), channel_id=1, source_target_pairs={{0,128},{128,256},{256,384},{384,512},{512,640},{640,768},{768,896... | collective-permute-start | bytes 98312 | tf_op jit(solution)/shard_map/ppermute | solution.py:323
  77.2 27.5 %collective-permute-start.1 = (bf16[128,128]{1,0:T(8,128)(2,1)S(1)}, bf16[128,128]{1,0:T(8,128)(2,1)S(1)}, u32[]{:S(2)}, u32[]{:S(2)}) collective-permute-start(bf16[128,128]{1,0:T(8,128)(2,1)S(1)} %get-tuple-element.19), channel_id=1, source_target_pairs={{0,256},{128,384},{256,512},{384,640},{512,768},{640,896},{768,0},... | collective-permute-start | bytes 98312 | tf_op jit(solution)/shard_map/ppermute | solution.py:323
  81.2 30.7 %collective-permute-start.2 = (bf16[128,128]{1,0:T(8,128)(2,1)S(1)}, bf16[128,128]{1,0:T(8,128)(2,1)S(1)}, u32[]{:S(2)}, u32[]{:S(2)}) collective-permute-start(bf16[128,128]{1,0:T(8,128)(2,1)S(1)} %get-tuple-element.20), channel_id=1, source_target_pairs={{0,384},{128,512},{256,640},{384,768},{512,896},{640,0},{768,128},... | collective-permute-start | bytes 98312 | tf_op jit(solution)/shard_map/ppermute | solution.py:323
  85.5 26.4 %collective-permute-start.3 = (bf16[128,128]{1,0:T(8,128)(2,1)S(1)}, bf16[128,128]{1,0:T(8,128)(2,1)S(1)}, u32[]{:S(2)}, u32[]{:S(2)}) collective-permute-start(bf16[128,128]{1,0:T(8,128)(2,1)S(1)} %get-tuple-element.21), channel_id=1, source_target_pairs={{0,512},{128,640},{256,768},{384,896},{512,0},{640,128},{768,256},... | collective-permute-start | bytes 98312 | tf_op jit(solution)/shard_map/ppermute | solution.py:323
  89.5 22.4 %collective-permute-start.4 = (bf16[128,128]{1,0:T(8,128)(2,1)S(1)}, bf16[128,128]{1,0:T(8,128)(2,1)S(1)}, u32[]{:S(2)}, u32[]{:S(2)}) collective-permute-start(bf16[128,128]{1,0:T(8,128)(2,1)S(1)} %get-tuple-element.22), channel_id=1, source_target_pairs={{0,640},{128,768},{256,896},{384,0},{512,128},{640,256},{768,384},... | collective-permute-start | bytes 98312 | tf_op jit(solution)/shard_map/ppermute | solution.py:323
  99.9 12.0 %collective-permute-start.5 = (bf16[128,128]{1,0:T(8,128)(2,1)S(1)}, bf16[128,128]{1,0:T(8,128)(2,1)S(1)}, u32[]{:S(2)}, u32[]{:S(2)}) collective-permute-start(bf16[128,128]{1,0:T(8,128)(2,1)S(1)} %get-tuple-element.23), channel_id=1, source_target_pairs={{0,768},{128,896},{256,0},{384,128},{512,256},{640,384},{768,512},... | collective-permute-start | bytes 98312 | tf_op jit(solution)/shard_map/ppermute | solution.py:323
  104.6 8.2 %collective-permute-start.6 = (bf16[128,128]{1,0:T(8,128)(2,1)S(1)}, bf16[128,128]{1,0:T(8,128)(2,1)S(1)}, u32[]{:S(2)}, u32[]{:S(2)}) collective-permute-start(bf16[128,128]{1,0:T(8,128)(2,1)S(1)} %get-tuple-element.24), channel_id=1, source_target_pairs={{0,896},{128,0},{256,128},{384,256},{512,384},{640,512},{768,640},... | collective-permute-start | bytes 98312 | tf_op jit(solution)/shard_map/ppermute | solution.py:323
  119.9 10.1 %collective-permute-start.7 = (bf16[2080,128]{1,0:T(8,128)(2,1)S(1)}, bf16[2080,128]{1,0:T(8,128)(2,1)S(1)}, u32[]{:S(2)}, u32[]{:S(2)}) collective-permute-start(bf16[2080,128]{1,0:T(8,128)(2,1)S(1)} %sums.1.mine), channel_id=1, source_target_pairs={{0,64},{64,0},{1,65},{65,1},{2,66},{66,2},{3,67},{67,3},{4,68},{68... | collective-permute-start | bytes 1597448 | tf_op jit(solution)/shard_map/ppermute | solution.py:288
  132.5 15.5 %all-to-all-start.2 = ((bf16[8,128,128]{2,1,0:T(8,128)(2,1)}), bf16[8,128,128]{2,1,0:T(8,128)(2,1)S(1)}, u32[]{:S(2)}, u32[]{:S(2)}) async-start(bf16[8,128,128]{2,1,0:T(8,128)(2,1)} %get-tuple-element.26), calls=%async_computation.2 | async-start | bytes 524288 | tf_op jit(solution)/shard_map/all_to_all | solution.py:294
  145.9 36.2 %copy-start.1 = (s32[1,512]{1,0:T(1,128)S(1)}, s32[1,512]{1,0:T(1,128)}, u32[]{:S(2)}) copy-start(s32[1,512]{1,0:T(1,128)} %get-tuple-element.28) | copy-start | bytes 6148
  160.1 20.6 %all-to-all-start.4 = ((f32[64,1,10]{2,1,0:T(1,128)}), f32[64,1,10]{2,1,0:T(1,128)S(1)}, u32[]{:S(2)}, u32[]{:S(2)}) async-start(f32[64,1,10]{2,1,0:T(1,128)} %bitcast.11), calls=%async_computation.4 | async-start | bytes 65536 | tf_op jit(solution)/shard_map/all_to_all | solution.py:294

commit v7 on v6

--- a/solution.py
+++ b/solution.py
@@ -321,6 +321,7 @@
     olds = [turned[0]]
     for d in range(1, chips):
         olds.append(lax.ppermute(turned[d], "x", [(i, (i + d) % chips) for i in range(chips)]))
+    arrived, *olds = lax.optimization_barrier((arrived, *olds))
     sent = call(
         functools.partial(spread, capacity),
         "spread",

time: 185 us -> 173 us (0.935)
  blocking collectives: 69.7 us -> 46.8 us
  starting transfers between devices: 61.3 us -> 73.2 us
    all_to_all x2, blocking collectives: 69.7 us -> 46.8 us  [exchange(): return lax.all_to_all(a, axis, split_axis=0, concat_axis=0, tiled=True)]
    all_to_all x3, starting transfers between devices: 20.9 us -> 37.3 us  [exchange(): return lax.all_to_all(a, axis, split_axis=0, concat_axis=0, tiled=True)]
    ppermute x7, waiting for transfers between devices: 7.11 us -> 1.85 us  [on_device(): lax.ppermute(turned[d], 'x', [(i, (i + d) % chips) for i in range(chips)])]
    all_to_all x3, waiting for transfers between devices: 11.9 us -> 17.1 us  [exchange(): return lax.all_to_all(a, axis, split_axis=0, concat_axis=0, tiled=True)]
    ppermute x7, starting transfers between devices: 31.9 us -> 28.1 us  [on_device(): lax.ppermute(turned[d], 'x', [(i, (i + d) % chips) for i in range(chips)])]
  transfers between devices with their start and end apart: 11 -> 11, of which waited for: 5 -> 5; matrix products, arithmetic and copies ran while one was open for 1% -> 1% of each run, Pallas kernels for 5% -> 6%
where the time goes in v7:
time: 173 us; the launch traced here: 171 us
  starting transfers between devices  73.2 us (42%)
  blocking collectives  46.8 us (27%)
  Pallas kernels  25 us (14%)
  waiting for transfers between devices  20.5 us (12%)
  other arithmetic  2.39 us (1%)
  local copies, waits for them, and re-layouts  2 us (1%)
    all_to_all x2, blocking collectives, exchange(): return lax.all_to_all(a, axis, split_axis=0, concat_axis=0, tiled=True)  46.8 us
    all_to_all x3, starting transfers between devices, exchange(): return lax.all_to_all(a, axis, split_axis=0, concat_axis=0, tiled=True)  37.3 us
    ppermute x7, starting transfers between devices, on_device(): lax.ppermute(turned[d], 'x', [(i, (i + d) % chips) for i in range(chips)])  28.1 us
    pallas_call x6, Pallas kernels, call(): pl.pallas_call(kernel, in_specs=specs, out_shape=out_shape, scratch_shape...  25 us
    all_to_all x3, waiting for transfers between devices, exchange(): return lax.all_to_all(a, axis, split_axis=0, concat_axis=0, tiled=True)  17.1 us
    ppermute x1, starting transfers between devices, across(): return lax.ppermute(a, 'core', [(0, 1), (1, 0)])  7.83 us
  transfers between devices with their start and end apart: 11, of which 5 were waited for; matrix products, arithmetic and copies ran while one was open for 1% of the time, Pallas kernels for 6%

profile of v7, /device:TPU:1, one launch (start us, length us, event | category | flops | bytes accessed | tf_op | source)
XLA Modules:
  0.0 170.8 jit_solution(5384849126341242027)
XLA Ops:
  0.6 5.2 %prepare.1 = (bf16[64,88,128]{2,1,0:T(8,128)(2,1)}, s32[1,512]{1,0:T(1,128)}) custom-call(s32[1,512]{1,0:T(1,128)} %bitcast.19, s32[1,512]{1,0:T(1,128)} %bitcast.20, s32[1024,128]{1,0:T(8,128)} %bitcast.18, bf16[512,1024]{1,0:T(8,128)(2,1)} %refs_3_.1), custom_call_target="tpu_custom_call" | custom-call | flops 2147483648 | bytes 2097152 | tf_op jit(solution)/shard_map/prepare/pallas_call | solution.py:46
  5.9 24.1 %all-to-all-start = ((bf16[64,88,128]{2,1,0:T(8,128)(2,1)}), bf16[64,88,128]{2,1,0:T(8,128)(2,1)S(1)}, u32[]{:S(2)}, u32[]{:S(2)}) async-start(bf16[64,88,128]{2,1,0:T(8,128)(2,1)} %get-tuple-element.25), calls=%async_computation | async-start | bytes 2883584 | tf_op jit(solution)/shard_map/all_to_all | solution.py:294
  30.7 3.1 %collective-permute-start = (bf16[128,128]{1,0:T(8,128)(2,1)S(1)}, bf16[128,128]{1,0:T(8,128)(2,1)S(1)}, u32[]{:S(2)}, u32[]{:S(2)}) collective-permute-start(bf16[128,128]{1,0:T(8,128)(2,1)S(1)} %get-tuple-element.27), channel_id=1, source_target_pairs={{0,128},{128,256},{256,384},{384,512},{512,640},{640,768},{768,896... | collective-permute-start | bytes 98312 | tf_op jit(solution)/shard_map/ppermute | solution.py:323
  33.8 4.1 %collective-permute-start.1 = (bf16[128,128]{1,0:T(8,128)(2,1)S(1)}, bf16[128,128]{1,0:T(8,128)(2,1)S(1)}, u32[]{:S(2)}, u32[]{:S(2)}) collective-permute-start(bf16[128,128]{1,0:T(8,128)(2,1)S(1)} %get-tuple-element.28), channel_id=1, source_target_pairs={{0,256},{128,384},{256,512},{384,640},{512,768},{640,896},{768,0},... | collective-permute-start | bytes 98312 | tf_op jit(solution)/shard_map/ppermute | solution.py:323
  37.9 4.4 %collective-permute-start.2 = (bf16[128,128]{1,0:T(8,128)(2,1)S(1)}, bf16[128,128]{1,0:T(8,128)(2,1)S(1)}, u32[]{:S(2)}, u32[]{:S(2)}) collective-permute-start(bf16[128,128]{1,0:T(8,128)(2,1)S(1)} %get-tuple-element.29), channel_id=1, source_target_pairs={{0,384},{128,512},{256,640},{384,768},{512,896},{640,0},{768,128},... | collective-permute-start | bytes 98312 | tf_op jit(solution)/shard_map/ppermute | solution.py:323
  42.3 3.9 %collective-permute-start.3 = (bf16[128,128]{1,0:T(8,128)(2,1)S(1)}, bf16[128,128]{1,0:T(8,128)(2,1)S(1)}, u32[]{:S(2)}, u32[]{:S(2)}) collective-permute-start(bf16[128,128]{1,0:T(8,128)(2,1)S(1)} %get-tuple-element.30), channel_id=1, source_target_pairs={{0,512},{128,640},{256,768},{384,896},{512,0},{640,128},{768,256},... | collective-permute-start | bytes 98312 | tf_op jit(solution)/shard_map/ppermute | solution.py:323
  46.1 4.4 %collective-permute-start.4 = (bf16[128,128]{1,0:T(8,128)(2,1)S(1)}, bf16[128,128]{1,0:T(8,128)(2,1)S(1)}, u32[]{:S(2)}, u32[]{:S(2)}) collective-permute-start(bf16[128,128]{1,0:T(8,128)(2,1)S(1)} %get-tuple-element.31), channel_id=1, source_target_pairs={{0,640},{128,768},{256,896},{384,0},{512,128},{640,256},{768,384},... | collective-permute-start | bytes 98312 | tf_op jit(solution)/shard_map/ppermute | solution.py:323
  50.6 5.1 %collective-permute-start.5 = (bf16[128,128]{1,0:T(8,128)(2,1)S(1)}, bf16[128,128]{1,0:T(8,128)(2,1)S(1)}, u32[]{:S(2)}, u32[]{:S(2)}) collective-permute-start(bf16[128,128]{1,0:T(8,128)(2,1)S(1)} %get-tuple-element.32), channel_id=1, source_target_pairs={{0,768},{128,896},{256,0},{384,128},{512,256},{640,384},{768,512},... | collective-permute-start | bytes 98312 | tf_op jit(solution)/shard_map/ppermute | solution.py:323
  55.8 3.1 %collective-permute-start.6 = (bf16[128,128]{1,0:T(8,128)(2,1)S(1)}, bf16[128,128]{1,0:T(8,128)(2,1)S(1)}, u32[]{:S(2)}, u32[]{:S(2)}) collective-permute-start(bf16[128,128]{1,0:T(8,128)(2,1)S(1)} %get-tuple-element.33), channel_id=1, source_target_pairs={{0,896},{128,0},{256,128},{384,256},{512,384},{640,512},{768,640},... | collective-permute-start | bytes 98312 | tf_op jit(solution)/shard_map/ppermute | solution.py:323
  58.9 1.8 %collective-permute-done.6.refs_7_ = bf16[128,128]{1,0:T(8,128)(2,1)S(1)} collective-permute-done((bf16[128,128]{1,0:T(8,128)(2,1)S(1)}, bf16[128,128]{1,0:T(8,128)(2,1)S(1)}, u32[]{:S(2)}, u32[]{:S(2)}) %collective-permute-start.6) | collective-permute-done | bytes 32800 | tf_op jit(solution)/shard_map/ppermute | solution.py:323
  60.7 4.0 %all-to-all-done.arrived = bf16[64,88,128]{2,1,0:T(8,128)(2,1)S(1)} async-done(((bf16[64,88,128]{2,1,0:T(8,128)(2,1)}), bf16[64,88,128]{2,1,0:T(8,128)(2,1)S(1)}, u32[]{:S(2)}, u32[]{:S(2)}) %all-to-all-start) | async-done | bytes 1441824 | tf_op jit(solution)/shard_map/all_to_all | solution.py:294
  65.4 37.1 %all_to_all.25.columns = bf16[8,672,128]{2,1,0:T(8,128)(2,1)S(1)} all-to-all(bf16[8,672,128]{2,1,0:T(8,128)(2,1)S(1)} %spread.1), channel_id=1, replica_groups=mesh['x'=8,'core'=2,'mem'=64] {'x'}, dimensions={0} | all-to-all | bytes 2752512 | tf_op jit(solution)/shard_map/all_to_all | solution.py:294
  102.5 7.0 %sums.1.mine = bf16[2080,128]{1,0:T(8,128)(2,1)S(1)} custom-call(s32[2]{0:T(128)S(1)} %pad_add_fusion.where, bf16[8,672,128]{2,1,0:T(8,128)(2,1)S(1)} %all_to_all.25.columns, bf16[128,128]{1,0:T(8,128)(2,1)S(1)} %get-tuple-element.35.refs_0_, bf16[128,128]{1,0:T(8,128)(2,1)S(1)} %collective-permute-done.refs_1_, ...), custom_call_target="tpu_custom_call" | custom-call | flops 4294967296 | bytes 2097152 | tf_op jit(solution)/shard_map/sums/pallas_call | solution.py:46
  109.5 7.8 %collective-permute-start.7 = (bf16[2080,128]{1,0:T(8,128)(2,1)S(1)}, bf16[2080,128]{1,0:T(8,128)(2,1)S(1)}, u32[]{:S(2)}, u32[]{:S(2)}) collective-permute-start(bf16[2080,128]{1,0:T(8,128)(2,1)S(1)} %sums.1.mine), channel_id=1, source_target_pairs={{0,64},{64,0},{1,65},{65,1},{2,66},{66,2},{3,67},{67,3},{4,68},{68... | collective-permute-start | bytes 1597448 | tf_op jit(solution)/shard_map/ppermute | solution.py:288
  117.3 1.5 collective-permute-done.7.theirs
  118.8 2.6 %refit.1 = (bf16[8,128,128]{2,1,0:T(8,128)(2,1)}, bf16[2048,256]{1,0:T(8,128)(2,1)S(1)}) custom-call(s32[2]{0:T(128)S(1)} %pad_add_fusion.where, bf16[2080,128]{1,0:T(8,128)(2,1)S(1)} %sums.1.mine, bf16[2080,128]{1,0:T(8,128)(2,1)S(1)} %collective-permute-done.7.theirs), custom_call_target="tpu_custom_call" | custom-call | flops 16777216 | bytes 2097152 | tf_op jit(solution)/shard_map/refit/pallas_call | solution.py:46
  121.4 3.4 %all-to-all-start.2 = ((bf16[8,128,128]{2,1,0:T(8,128)(2,1)}), bf16[8,128,128]{2,1,0:T(8,128)(2,1)S(1)}, u32[]{:S(2)}, u32[]{:S(2)}) async-start(bf16[8,128,128]{2,1,0:T(8,128)(2,1)} %get-tuple-element.44), calls=%async_computation.2 | async-start | bytes 524288 | tf_op jit(solution)/shard_map/all_to_all | solution.py:294
  124.9 8.9 %score.1 = f32[8,640]{1,0:T(8,128)S(1)} custom-call(bf16[8,672,128]{2,1,0:T(8,128)(2,1)S(1)} %all_to_all.25.columns, bf16[2048,256]{1,0:T(8,128)(2,1)S(1)} %get-tuple-element.43.lists_of), custom_call_target="tpu_custom_call" | custom-call | flops 8589934592 | bytes 2097152 | tf_op jit(solution)/shard_map/score/pallas_call | solution.py:46
  133.8 3.3 %all-to-all-done.2 = bf16[8,128,128]{2,1,0:T(8,128)(2,1)S(1)} async-done(((bf16[8,128,128]{2,1,0:T(8,128)(2,1)}), bf16[8,128,128]{2,1,0:T(8,128)(2,1)S(1)}, u32[]{:S(2)}, u32[]{:S(2)}) %all-to-all-start.2) | async-done | bytes 262176 | tf_op jit(solution)/shard_map/all_to_all | solution.py:294
  137.2 9.7 %all_to_all.26 = f32[8,1,640]{2,1,0:T(1,128)S(1)} all-to-all(f32[8,1,640]{2,1,0:T(1,128)S(1)} %copy.17), channel_id=1, replica_groups=mesh['x'=8,'core'=2,'mem'=64] {'x'}, dimensions={0} | all-to-all | bytes 40960 | tf_op jit(solution)/shard_map/all_to_all | solution.py:294
  147.9 9.8 %all-to-all-start.4 = ((f32[64,1,10]{2,1,0:T(1,128)}), f32[64,1,10]{2,1,0:T(1,128)S(1)}, u32[]{:S(2)}, u32[]{:S(2)}) async-start(f32[64,1,10]{2,1,0:T(1,128)} %bitcast.11), calls=%async_computation.4 | async-start | bytes 65536 | tf_op jit(solution)/shard_map/all_to_all | solution.py:294
  157.9 0.9 copy.20
  158.7 9.8 %all-to-all-done.4 = f32[64,1,10]{2,1,0:T(1,128)S(1)} async-done(((f32[64,1,10]{2,1,0:T(1,128)}), f32[64,1,10]{2,1,0:T(1,128)S(1)}, u32[]{:S(2)}, u32[]{:S(2)}) %all-to-all-start.4) | async-done | bytes 2592 | tf_op jit(solution)/shard_map/all_to_all | solution.py:294
  169.9 0.9 select_reduce_fusion
  (26 shorter events, 3.9 us)
Async XLA Ops:
  5.9 24.2 %copy-start = (bf16[128,1024]{1,0:T(8,128)(2,1)S(1)}, bf16[128,1024]{1,0:T(8,128)(2,1)}, u32[]{:S(2)}) copy-start(bf16[128,1024]{1,0:T(8,128)(2,1)} %old.1) | copy-start | bytes 786436
  5.9 58.9 %all-to-all-start = ((bf16[64,88,128]{2,1,0:T(8,128)(2,1)}), bf16[64,88,128]{2,1,0:T(8,128)(2,1)S(1)}, u32[]{:S(2)}, u32[]{:S(2)}) async-start(bf16[64,88,128]{2,1,0:T(8,128)(2,1)} %get-tuple-element.25), calls=%async_computation | async-start | bytes 2883584 | tf_op jit(solution)/shard_map/all_to_all | solution.py:294
  30.7 19.9 %collective-permute-start = (bf16[128,128]{1,0:T(8,128)(2,1)S(1)}, bf16[128,128]{1,0:T(8,128)(2,1)S(1)}, u32[]{:S(2)}, u32[]{:S(2)}) collective-permute-start(bf16[128,128]{1,0:T(8,128)(2,1)S(1)} %get-tuple-element.27), channel_id=1, source_target_pairs={{0,128},{128,256},{256,384},{384,512},{512,640},{640,768},{768,896... | collective-permute-start | bytes 98312 | tf_op jit(solution)/shard_map/ppermute | solution.py:323
  33.8 21.9 %collective-permute-start.1 = (bf16[128,128]{1,0:T(8,128)(2,1)S(1)}, bf16[128,128]{1,0:T(8,128)(2,1)S(1)}, u32[]{:S(2)}, u32[]{:S(2)}) collective-permute-start(bf16[128,128]{1,0:T(8,128)(2,1)S(1)} %get-tuple-element.28), channel_id=1, source_target_pairs={{0,256},{128,384},{256,512},{384,640},{512,768},{640,896},{768,0},... | collective-permute-start | bytes 98312 | tf_op jit(solution)/shard_map/ppermute | solution.py:323
  37.9 21.0 %collective-permute-start.2 = (bf16[128,128]{1,0:T(8,128)(2,1)S(1)}, bf16[128,128]{1,0:T(8,128)(2,1)S(1)}, u32[]{:S(2)}, u32[]{:S(2)}) collective-permute-start(bf16[128,128]{1,0:T(8,128)(2,1)S(1)} %get-tuple-element.29), channel_id=1, source_target_pairs={{0,384},{128,512},{256,640},{384,768},{512,896},{640,0},{768,128},... | collective-permute-start | bytes 98312 | tf_op jit(solution)/shard_map/ppermute | solution.py:323
  42.3 16.6 %collective-permute-start.3 = (bf16[128,128]{1,0:T(8,128)(2,1)S(1)}, bf16[128,128]{1,0:T(8,128)(2,1)S(1)}, u32[]{:S(2)}, u32[]{:S(2)}) collective-permute-start(bf16[128,128]{1,0:T(8,128)(2,1)S(1)} %get-tuple-element.30), channel_id=1, source_target_pairs={{0,512},{128,640},{256,768},{384,896},{512,0},{640,128},{768,256},... | collective-permute-start | bytes 98312 | tf_op jit(solution)/shard_map/ppermute | solution.py:323
  46.1 12.7 %collective-permute-start.4 = (bf16[128,128]{1,0:T(8,128)(2,1)S(1)}, bf16[128,128]{1,0:T(8,128)(2,1)S(1)}, u32[]{:S(2)}, u32[]{:S(2)}) collective-permute-start(bf16[128,128]{1,0:T(8,128)(2,1)S(1)} %get-tuple-element.31), channel_id=1, source_target_pairs={{0,640},{128,768},{256,896},{384,0},{512,128},{640,256},{768,384},... | collective-permute-start | bytes 98312 | tf_op jit(solution)/shard_map/ppermute | solution.py:323
  50.6 8.3 %collective-permute-start.5 = (bf16[128,128]{1,0:T(8,128)(2,1)S(1)}, bf16[128,128]{1,0:T(8,128)(2,1)S(1)}, u32[]{:S(2)}, u32[]{:S(2)}) collective-permute-start(bf16[128,128]{1,0:T(8,128)(2,1)S(1)} %get-tuple-element.32), channel_id=1, source_target_pairs={{0,768},{128,896},{256,0},{384,128},{512,256},{640,384},{768,512},... | collective-permute-start | bytes 98312 | tf_op jit(solution)/shard_map/ppermute | solution.py:323
  55.8 5.0 %collective-permute-start.6 = (bf16[128,128]{1,0:T(8,128)(2,1)S(1)}, bf16[128,128]{1,0:T(8,128)(2,1)S(1)}, u32[]{:S(2)}, u32[]{:S(2)}) collective-permute-start(bf16[128,128]{1,0:T(8,128)(2,1)S(1)} %get-tuple-element.33), channel_id=1, source_target_pairs={{0,896},{128,0},{256,128},{384,256},{512,384},{640,512},{768,640},... | collective-permute-start | bytes 98312 | tf_op jit(solution)/shard_map/ppermute | solution.py:323
  109.5 9.4 %collective-permute-start.7 = (bf16[2080,128]{1,0:T(8,128)(2,1)S(1)}, bf16[2080,128]{1,0:T(8,128)(2,1)S(1)}, u32[]{:S(2)}, u32[]{:S(2)}) collective-permute-start(bf16[2080,128]{1,0:T(8,128)(2,1)S(1)} %sums.1.mine), channel_id=1, source_target_pairs={{0,64},{64,0},{1,65},{65,1},{2,66},{66,2},{3,67},{67,3},{4,68},{68... | collective-permute-start | bytes 1597448 | tf_op jit(solution)/shard_map/ppermute | solution.py:288
  121.4 15.7 %all-to-all-start.2 = ((bf16[8,128,128]{2,1,0:T(8,128)(2,1)}), bf16[8,128,128]{2,1,0:T(8,128)(2,1)S(1)}, u32[]{:S(2)}, u32[]{:S(2)}) async-start(bf16[8,128,128]{2,1,0:T(8,128)(2,1)} %get-tuple-element.44), calls=%async_computation.2 | async-start | bytes 524288 | tf_op jit(solution)/shard_map/all_to_all | solution.py:294
  133.8 36.1 %copy-start.1 = (s32[1,512]{1,0:T(1,128)S(1)}, s32[1,512]{1,0:T(1,128)}, u32[]{:S(2)}) copy-start(s32[1,512]{1,0:T(1,128)} %get-tuple-element.46) | copy-start | bytes 6148
  147.9 20.6 %all-to-all-start.4 = ((f32[64,1,10]{2,1,0:T(1,128)}), f32[64,1,10]{2,1,0:T(1,128)S(1)}, u32[]{:S(2)}, u32[]{:S(2)}) async-start(f32[64,1,10]{2,1,0:T(1,128)} %bitcast.11), calls=%async_computation.4 | async-start | bytes 65536 | tf_op jit(solution)/shard_map/all_to_all | solution.py:294

commit v8 on v7

--- a/solution.py
+++ b/solution.py
@@ -12,6 +12,7 @@
 BF16 = jnp.bfloat16
 LANES = 128
 TILE = 8
+BLOCK = 16
 NOTES = 32
 LIMIT = 40 * 2**20
 SMEM = pl.BlockSpec(memory_space=pltpu.SMEM)
@@ -66,7 +67,6 @@
     for copy in copies[:3]:
         copy.wait()
     vectors = first.shape[1]
-    parts = embeddings.shape[1] // LANES
     slots = table[...]
     local = slots & (LANES - 1)
     owner = (slots // LANES) & (members - 1)
@@ -102,53 +102,49 @@
     spread = [jnp.where(ranked, digit, 0.0) for digit in digits]
     spread.append(jnp.zeros((LANES - 16 * len(digits), vectors), F32))
     labels = dot(hot(is_owner), jnp.concatenate(spread, axis=0).astype(BF16), ((1,), (1,)))
-    pieces = [
-        packed[: TILE * members, j * LANES : (j + 1) * LANES].reshape(members, TILE, LANES)
-        for j in range(parts)
-    ]
-    rest = [
-        packed[p * members : (p + 1) * members, j * LANES : (j + 1) * LANES]
-        for p in range(TILE, capacity)
-        for j in range(parts)
-    ]
-    for k in range(0, len(rest), TILE):
-        pieces.append(jnp.stack(rest[k : k + TILE], axis=1))
-    pieces.append(jnp.broadcast_to(labels[:, None, :], (members, TILE, LANES)))
-    payload[...] = jnp.concatenate(pieces, axis=1).astype(BF16)
-
-
-def spread(capacity, arrived, out):
-    members = arrived.shape[0]
+    empty = [jnp.zeros((members, LANES), F32)] * (BLOCK - capacity - 1)
+    for j in range(embeddings.shape[1] // LANES):
+        at = slice(j * LANES, (j + 1) * LANES)
+        rest = [packed[p * members : (p + 1) * members, at] for p in range(TILE, capacity)]
+        block = [
+            packed[: TILE * members, at].reshape(members, TILE, LANES),
+            jnp.stack(rest + [labels] + empty, axis=1),
+        ]
+        payload[j * members : (j + 1) * members] = jnp.concatenate(block, axis=1).astype(BF16)
+
+
+def gather(capacity, arrived, out):
+    chips, rows, _ = out.shape
+    members = arrived.shape[0] // chips
     count = members * capacity
-    chips, rows, _ = out.shape
     slots = rows - NOTES
-    values = arrived[...].astype(F32)
-    labels = values[:, capacity * chips].astype(BF16)
     vector = lanes_of((members, slots))
     from_member = jnp.where(
         vector < TILE * members, whole(vector, TILE), vector - members * whole(vector, members)
     )
-    found = dot(labels, hot(rows_of((members, slots)) == from_member), ((0,), (0,)))
+    from_member = hot(rows_of((members, slots)) == from_member)
     vector = lanes_of((16, slots))
     rank = jnp.where(
         vector < TILE * members, vector - TILE * whole(vector, TILE), whole(vector, members)
     )
     ranked = rows_of((16, slots)) == rank
-    notes = []
-    for k in range(4):
-        row = jnp.sum(jnp.where(ranked, found[k * 16 : (k + 1) * 16], 0.0), axis=0, keepdims=True)
-        notes += [row[:, q : q + LANES] for q in range(0, slots, LANES)]
-    notes.append(jnp.zeros((NOTES - len(notes), LANES), F32))
-    notes = jnp.concatenate(notes, axis=0).astype(BF16)
-    for j in range(chips):
-        out[j, : TILE * members] = (
-            values[:, j * TILE : (j + 1) * TILE].reshape(TILE * members, LANES).astype(BF16)
+    for s in range(chips):
+        values = arrived[s * members : (s + 1) * members].astype(F32)
+        out[s, : TILE * members] = (
+            values[:, :TILE].reshape(TILE * members, LANES).astype(BF16)
         )
         for p in range(TILE, capacity):
-            out[j, p * members : (p + 1) * members] = values[:, p * chips + j].astype(BF16)
+            out[s, p * members : (p + 1) * members] = values[:, p].astype(BF16)
         if slots > count:
-            out[j, count:slots] = jnp.zeros((slots - count, LANES), BF16)
-        out[j, slots:] = notes
+            out[s, count:slots] = jnp.zeros((slots - count, LANES), BF16)
+        found = dot(values[:, capacity].astype(BF16), from_member, ((0,), (0,)))
+        notes = []
+        for k in range(4):
+            row = jnp.where(ranked, found[k * 16 : (k + 1) * 16], 0.0)
+            row = jnp.sum(row, axis=0, keepdims=True)
+            notes += [row[:, q : q + LANES] for q in range(0, slots, LANES)]
+        notes.append(jnp.zeros((NOTES - len(notes), LANES), F32))
+        out[s, slots:] = jnp.concatenate(notes, axis=0).astype(BF16)
 
 
 def labels_of(slots, notes, k):
@@ -298,7 +294,7 @@
         functools.partial(prepare, members, capacity),
         "prepare",
         (
-            shape(members, capacity * width // LANES + TILE, LANES),
+            shape(chips * members, BLOCK, LANES),
             shape(1, vectors, kind=jnp.int32),
         ),
         2**31,
@@ -316,20 +312,19 @@
         space=pl.BlockSpec(memory_space=pl.ANY),
         limit=60 * 2**20,
     )
-    arrived = exchange("mem", payload)
+    arrived = exchange(("x", "mem"), payload)
     turned = call(turn, "turn", [shape(lists, LANES)] * chips, 2**20, old_centroids, scalars=where)
     olds = [turned[0]]
     for d in range(1, chips):
         olds.append(lax.ppermute(turned[d], "x", [(i, (i + d) % chips) for i in range(chips)]))
     arrived, *olds = lax.optimization_barrier((arrived, *olds))
-    sent = call(
-        functools.partial(spread, capacity),
-        "spread",
+    columns = call(
+        functools.partial(gather, capacity),
+        "gather",
         shape(chips, slots + NOTES, LANES),
         2**24,
         arrived,
     )
-    columns = exchange("x", sent)
     mine = call(
         functools.partial(sums, groups),
         "sums",

time: 173 us -> 170 us (0.983)
  blocking collectives: 46.8 us -> 9.57 us
  waiting for transfers between devices: 20.5 us -> 37.8 us
  starting transfers between devices: 73.2 us -> 85.9 us
  local copies, waits for them, and re-layouts: 2 us -> 5.69 us
    all_to_all x2 -> x1, blocking collectives: 46.8 us -> 9.57 us  [exchange(): return lax.all_to_all(a, axis, split_axis=0, concat_axis=0, tiled=True)]
    ppermute x7, waiting for transfers between devices: 1.85 us -> 23 us  [on_device(): lax.ppermute(turned[d], 'x', [(i, (i + d) % chips) for i in range(chips)])]
    all_to_all x3, starting transfers between devices: 37.3 us -> 53.6 us  [exchange(): return lax.all_to_all(a, axis, split_axis=0, concat_axis=0, tiled=True)]
    all_to_all x3, waiting for transfers between devices: 17.1 us -> 13.3 us  [exchange(): return lax.all_to_all(a, axis, split_axis=0, concat_axis=0, tiled=True)]
    unnamed x5 -> x29, local copies, waits for them, and re-layouts: 0.87 us -> 4.54 us
    ppermute x7, starting transfers between devices: 28.1 us -> 25.8 us  [on_device(): lax.ppermute(turned[d], 'x', [(i, (i + d) % chips) for i in range(chips)])]
  transfers between devices with their start and end apart: 11 -> 11, of which waited for: 5 -> 4; matrix products, arithmetic and copies ran while one was open for 1% -> 1% of each run, Pallas kernels for 6% -> 6%
where the time goes in v8:
time: 170 us; the launch traced here: 168 us
  starting transfers between devices  85.9 us (51%)
  waiting for transfers between devices  37.8 us (22%)
  Pallas kernels  25.9 us (15%)
  blocking collectives  9.57 us (6%)
  local copies, waits for them, and re-layouts  5.69 us (3%)
  other arithmetic  2.37 us (1%)
    all_to_all x3, starting transfers between devices, exchange(): return lax.all_to_all(a, axis, split_axis=0, concat_axis=0, tiled=True)  53.6 us
    pallas_call x6, Pallas kernels, call(): pl.pallas_call(kernel, in_specs=specs, out_shape=out_shape, scratch_shape...  25.9 us
    ppermute x7, starting transfers between devices, on_device(): lax.ppermute(turned[d], 'x', [(i, (i + d) % chips) for i in range(chips)])  25.8 us
    ppermute x7, waiting for transfers between devices, on_device(): lax.ppermute(turned[d], 'x', [(i, (i + d) % chips) for i in range(chips)])  23 us
    all_to_all x3, waiting for transfers between devices, exchange(): return lax.all_to_all(a, axis, split_axis=0, concat_axis=0, tiled=True)  13.3 us
    all_to_all x1, blocking collectives, exchange(): return lax.all_to_all(a, axis, split_axis=0, concat_axis=0, tiled=True)  9.57 us
    ppermute x1, starting transfers between devices, across(): return lax.ppermute(a, 'core', [(0, 1), (1, 0)])  6.53 us
    unnamed x29, local copies, waits for them, and re-layouts  4.54 us
  transfers between devices with their start and end apart: 11, of which 4 were waited for; matrix products, arithmetic and copies ran while one was open for 1% of the time, Pallas kernels for 6%

profile of v8, /device:TPU:1, one launch (start us, length us, event | category | flops | bytes accessed | tf_op | source)
XLA Modules:
  0.0 168.2 jit_solution(5793952219058931191)
XLA Ops:
  0.6 5.8 %prepare.1 = (bf16[512,16,128]{2,1,0:T(8,128)(2,1)}, s32[1,512]{1,0:T(1,128)}) custom-call(s32[1,512]{1,0:T(1,128)} %bitcast.19, s32[1,512]{1,0:T(1,128)} %bitcast.20, s32[1024,128]{1,0:T(8,128)} %bitcast.18, bf16[512,1024]{1,0:T(8,128)(2,1)} %refs_3_.1), custom_call_target="tpu_custom_call" | custom-call | flops 2147483648 | bytes 2097152 | tf_op jit(solution)/shard_map/prepare/pallas_call | solution.py:47
  6.4 37.3 %all-to-all-start = ((bf16[512,16,128]{2,1,0:T(8,128)(2,1)}), bf16[512,16,128]{2,1,0:T(8,128)(2,1)S(1)}, u32[]{:S(2)}, u32[]{:S(2)}) async-start(bf16[512,16,128]{2,1,0:T(8,128)(2,1)} %get-tuple-element.25), calls=%async_computation | async-start | bytes 4194304 | tf_op jit(solution)/shard_map/all_to_all | solution.py:290
  44.5 1.9 %collective-permute-start = (bf16[128,128]{1,0:T(8,128)(2,1)S(1)}, bf16[128,128]{1,0:T(8,128)(2,1)S(1)}, u32[]{:S(2)}, u32[]{:S(2)}) collective-permute-start(bf16[128,128]{1,0:T(8,128)(2,1)S(1)} %get-tuple-element.27), channel_id=1, source_target_pairs={{0,128},{128,256},{256,384},{384,512},{512,640},{640,768},{768,896... | collective-permute-start | bytes 98312 | tf_op jit(solution)/shard_map/ppermute | solution.py:319
  46.4 3.1 %collective-permute-start.1 = (bf16[128,128]{1,0:T(8,128)(2,1)S(1)}, bf16[128,128]{1,0:T(8,128)(2,1)S(1)}, u32[]{:S(2)}, u32[]{:S(2)}) collective-permute-start(bf16[128,128]{1,0:T(8,128)(2,1)S(1)} %get-tuple-element.28), channel_id=1, source_target_pairs={{0,256},{128,384},{256,512},{384,640},{512,768},{640,896},{768,0},... | collective-permute-start | bytes 98312 | tf_op jit(solution)/shard_map/ppermute | solution.py:319
  49.6 5.6 %collective-permute-start.2 = (bf16[128,128]{1,0:T(8,128)(2,1)S(1)}, bf16[128,128]{1,0:T(8,128)(2,1)S(1)}, u32[]{:S(2)}, u32[]{:S(2)}) collective-permute-start(bf16[128,128]{1,0:T(8,128)(2,1)S(1)} %get-tuple-element.29), channel_id=1, source_target_pairs={{0,384},{128,512},{256,640},{384,768},{512,896},{640,0},{768,128},... | collective-permute-start | bytes 98312 | tf_op jit(solution)/shard_map/ppermute | solution.py:319
  55.2 2.6 %collective-permute-start.3 = (bf16[128,128]{1,0:T(8,128)(2,1)S(1)}, bf16[128,128]{1,0:T(8,128)(2,1)S(1)}, u32[]{:S(2)}, u32[]{:S(2)}) collective-permute-start(bf16[128,128]{1,0:T(8,128)(2,1)S(1)} %get-tuple-element.30), channel_id=1, source_target_pairs={{0,512},{128,640},{256,768},{384,896},{512,0},{640,128},{768,256},... | collective-permute-start | bytes 98312 | tf_op jit(solution)/shard_map/ppermute | solution.py:319
  57.8 6.1 %collective-permute-start.4 = (bf16[128,128]{1,0:T(8,128)(2,1)S(1)}, bf16[128,128]{1,0:T(8,128)(2,1)S(1)}, u32[]{:S(2)}, u32[]{:S(2)}) collective-permute-start(bf16[128,128]{1,0:T(8,128)(2,1)S(1)} %get-tuple-element.31), channel_id=1, source_target_pairs={{0,640},{128,768},{256,896},{384,0},{512,128},{640,256},{768,384},... | collective-permute-start | bytes 98312 | tf_op jit(solution)/shard_map/ppermute | solution.py:319
  63.9 23.0 %collective-permute-done.refs_1_ = bf16[128,128]{1,0:T(8,128)(2,1)S(1)} collective-permute-done((bf16[128,128]{1,0:T(8,128)(2,1)S(1)}, bf16[128,128]{1,0:T(8,128)(2,1)S(1)}, u32[]{:S(2)}, u32[]{:S(2)}) %collective-permute-start) | collective-permute-done | bytes 32800 | tf_op jit(solution)/shard_map/ppermute | solution.py:319
  86.9 3.6 %collective-permute-start.5 = (bf16[128,128]{1,0:T(8,128)(2,1)S(1)}, bf16[128,128]{1,0:T(8,128)(2,1)S(1)}, u32[]{:S(2)}, u32[]{:S(2)}) collective-permute-start(bf16[128,128]{1,0:T(8,128)(2,1)S(1)} %get-tuple-element.32), channel_id=1, source_target_pairs={{0,768},{128,896},{256,0},{384,128},{512,256},{640,384},{768,512},... | collective-permute-start | bytes 98312 | tf_op jit(solution)/shard_map/ppermute | solution.py:319
  91.2 2.7 %collective-permute-start.6 = (bf16[128,128]{1,0:T(8,128)(2,1)S(1)}, bf16[128,128]{1,0:T(8,128)(2,1)S(1)}, u32[]{:S(2)}, u32[]{:S(2)}) collective-permute-start(bf16[128,128]{1,0:T(8,128)(2,1)S(1)} %get-tuple-element.33), channel_id=1, source_target_pairs={{0,896},{128,0},{256,128},{384,256},{512,384},{640,512},{768,640},... | collective-permute-start | bytes 98312 | tf_op jit(solution)/shard_map/ppermute | solution.py:319
  97.1 1.1 gather.1.columns
  98.3 7.0 %sums.1.mine = bf16[2080,128]{1,0:T(8,128)(2,1)S(1)} custom-call(s32[2]{0:T(128)S(1)} %pad_add_fusion.where, bf16[8,672,128]{2,1,0:T(8,128)(2,1)S(1)} %gather.1.columns, bf16[128,128]{1,0:T(8,128)(2,1)S(1)} %get-tuple-element.35.refs_0_, bf16[128,128]{1,0:T(8,128)(2,1)S(1)} %collective-permute-done.refs_1_, bf16[128,128]{1,0:T(8,128)(2,1)S(1)} %copy-done.2, ...), custom_call_target="tpu_custom_call" | custom-call | flops 4294967296 | bytes 2097152 | tf_op jit(solution)/shard_map/sums/pallas_call | solution.py:47
  105.3 6.5 %collective-permute-start.7 = (bf16[2080,128]{1,0:T(8,128)(2,1)S(1)}, bf16[2080,128]{1,0:T(8,128)(2,1)S(1)}, u32[]{:S(2)}, u32[]{:S(2)}) collective-permute-start(bf16[2080,128]{1,0:T(8,128)(2,1)S(1)} %sums.1.mine), channel_id=1, source_target_pairs={{0,64},{64,0},{1,65},{65,1},{2,66},{66,2},{3,67},{67,3},{4,68},{68... | collective-permute-start | bytes 1597448 | tf_op jit(solution)/shard_map/ppermute | solution.py:284
  111.8 1.5 collective-permute-done.7.theirs
  113.3 2.6 %refit.1 = (bf16[8,128,128]{2,1,0:T(8,128)(2,1)}, bf16[2048,256]{1,0:T(8,128)(2,1)S(1)}) custom-call(s32[2]{0:T(128)S(1)} %pad_add_fusion.where, bf16[2080,128]{1,0:T(8,128)(2,1)S(1)} %sums.1.mine, bf16[2080,128]{1,0:T(8,128)(2,1)S(1)} %collective-permute-done.7.theirs), custom_call_target="tpu_custom_call" | custom-call | flops 16777216 | bytes 2097152 | tf_op jit(solution)/shard_map/refit/pallas_call | solution.py:47
  115.9 3.4 %all-to-all-start.1 = ((bf16[8,128,128]{2,1,0:T(8,128)(2,1)}), bf16[8,128,128]{2,1,0:T(8,128)(2,1)S(1)}, u32[]{:S(2)}, u32[]{:S(2)}) async-start(bf16[8,128,128]{2,1,0:T(8,128)(2,1)} %get-tuple-element.44), calls=%async_computation.1 | async-start | bytes 524288 | tf_op jit(solution)/shard_map/all_to_all | solution.py:290
  119.3 8.8 %score.1 = f32[8,640]{1,0:T(8,128)S(1)} custom-call(bf16[8,672,128]{2,1,0:T(8,128)(2,1)S(1)} %gather.1.columns, bf16[2048,256]{1,0:T(8,128)(2,1)S(1)} %get-tuple-element.43.lists_of), custom_call_target="tpu_custom_call" | custom-call | flops 8589934592 | bytes 2097152 | tf_op jit(solution)/shard_map/score/pallas_call | solution.py:47
  128.1 3.4 %all-to-all-done.1 = bf16[8,128,128]{2,1,0:T(8,128)(2,1)S(1)} async-done(((bf16[8,128,128]{2,1,0:T(8,128)(2,1)}), bf16[8,128,128]{2,1,0:T(8,128)(2,1)S(1)}, u32[]{:S(2)}, u32[]{:S(2)}) %all-to-all-start.1) | async-done | bytes 262176 | tf_op jit(solution)/shard_map/all_to_all | solution.py:290
  131.6 9.6 %all_to_all.20 = f32[8,1,640]{2,1,0:T(1,128)S(1)} all-to-all(f32[8,1,640]{2,1,0:T(1,128)S(1)} %copy.17), channel_id=1, replica_groups=mesh['x'=8,'core'=2,'mem'=64] {'x'}, dimensions={0} | all-to-all | bytes 40960 | tf_op jit(solution)/shard_map/all_to_all | solution.py:290
  142.2 12.9 %all-to-all-start.3 = ((f32[64,1,10]{2,1,0:T(1,128)}), f32[64,1,10]{2,1,0:T(1,128)S(1)}, u32[]{:S(2)}, u32[]{:S(2)}) async-start(f32[64,1,10]{2,1,0:T(1,128)} %bitcast.11), calls=%async_computation.3 | async-start | bytes 65536 | tf_op jit(solution)/shard_map/all_to_all | solution.py:290
  155.2 0.9 copy.20
  156.1 9.8 %all-to-all-done.3 = f32[64,1,10]{2,1,0:T(1,128)S(1)} async-done(((f32[64,1,10]{2,1,0:T(1,128)}), f32[64,1,10]{2,1,0:T(1,128)S(1)}, u32[]{:S(2)}, u32[]{:S(2)}) %all-to-all-start.3) | async-done | bytes 2592 | tf_op jit(solution)/shard_map/all_to_all | solution.py:290
  166.4 0.7 reduce.4
  167.3 0.9 select_reduce_fusion
  (49 shorter events, 6.3 us)
Async XLA Ops:
  6.4 37.4 %copy-start = (bf16[128,1024]{1,0:T(8,128)(2,1)S(1)}, bf16[128,1024]{1,0:T(8,128)(2,1)}, u32[]{:S(2)}) copy-start(bf16[128,1024]{1,0:T(8,128)(2,1)} %old.1) | copy-start | bytes 786436
  6.4 90.6 %all-to-all-start = ((bf16[512,16,128]{2,1,0:T(8,128)(2,1)}), bf16[512,16,128]{2,1,0:T(8,128)(2,1)S(1)}, u32[]{:S(2)}, u32[]{:S(2)}) async-start(bf16[512,16,128]{2,1,0:T(8,128)(2,1)} %get-tuple-element.25), calls=%async_computation | async-start | bytes 4194304 | tf_op jit(solution)/shard_map/all_to_all | solution.py:290
  44.5 42.4 %collective-permute-start = (bf16[128,128]{1,0:T(8,128)(2,1)S(1)}, bf16[128,128]{1,0:T(8,128)(2,1)S(1)}, u32[]{:S(2)}, u32[]{:S(2)}) collective-permute-start(bf16[128,128]{1,0:T(8,128)(2,1)S(1)} %get-tuple-element.27), channel_id=1, source_target_pairs={{0,128},{128,256},{256,384},{384,512},{512,640},{640,768},{768,896... | collective-permute-start | bytes 98312 | tf_op jit(solution)/shard_map/ppermute | solution.py:319
  46.4 44.2 %collective-permute-start.1 = (bf16[128,128]{1,0:T(8,128)(2,1)S(1)}, bf16[128,128]{1,0:T(8,128)(2,1)S(1)}, u32[]{:S(2)}, u32[]{:S(2)}) collective-permute-start(bf16[128,128]{1,0:T(8,128)(2,1)S(1)} %get-tuple-element.28), channel_id=1, source_target_pairs={{0,256},{128,384},{256,512},{384,640},{512,768},{640,896},{768,0},... | collective-permute-start | bytes 98312 | tf_op jit(solution)/shard_map/ppermute | solution.py:319
  49.6 44.4 %collective-permute-start.2 = (bf16[128,128]{1,0:T(8,128)(2,1)S(1)}, bf16[128,128]{1,0:T(8,128)(2,1)S(1)}, u32[]{:S(2)}, u32[]{:S(2)}) collective-permute-start(bf16[128,128]{1,0:T(8,128)(2,1)S(1)} %get-tuple-element.29), channel_id=1, source_target_pairs={{0,384},{128,512},{256,640},{384,768},{512,896},{640,0},{768,128},... | collective-permute-start | bytes 98312 | tf_op jit(solution)/shard_map/ppermute | solution.py:319
  55.2 39.4 %collective-permute-start.3 = (bf16[128,128]{1,0:T(8,128)(2,1)S(1)}, bf16[128,128]{1,0:T(8,128)(2,1)S(1)}, u32[]{:S(2)}, u32[]{:S(2)}) collective-permute-start(bf16[128,128]{1,0:T(8,128)(2,1)S(1)} %get-tuple-element.30), channel_id=1, source_target_pairs={{0,512},{128,640},{256,768},{384,896},{512,0},{640,128},{768,256},... | collective-permute-start | bytes 98312 | tf_op jit(solution)/shard_map/ppermute | solution.py:319
  57.8 37.4 %collective-permute-start.4 = (bf16[128,128]{1,0:T(8,128)(2,1)S(1)}, bf16[128,128]{1,0:T(8,128)(2,1)S(1)}, u32[]{:S(2)}, u32[]{:S(2)}) collective-permute-start(bf16[128,128]{1,0:T(8,128)(2,1)S(1)} %get-tuple-element.31), channel_id=1, source_target_pairs={{0,640},{128,768},{256,896},{384,0},{512,128},{640,256},{768,384},... | collective-permute-start | bytes 98312 | tf_op jit(solution)/shard_map/ppermute | solution.py:319
  86.9 8.9 %collective-permute-start.5 = (bf16[128,128]{1,0:T(8,128)(2,1)S(1)}, bf16[128,128]{1,0:T(8,128)(2,1)S(1)}, u32[]{:S(2)}, u32[]{:S(2)}) collective-permute-start(bf16[128,128]{1,0:T(8,128)(2,1)S(1)} %get-tuple-element.32), channel_id=1, source_target_pairs={{0,768},{128,896},{256,0},{384,128},{512,256},{640,384},{768,512},... | collective-permute-start | bytes 98312 | tf_op jit(solution)/shard_map/ppermute | solution.py:319
  90.6 0.6 copy-start.1
  91.2 5.2 %collective-permute-start.6 = (bf16[128,128]{1,0:T(8,128)(2,1)S(1)}, bf16[128,128]{1,0:T(8,128)(2,1)S(1)}, u32[]{:S(2)}, u32[]{:S(2)}) collective-permute-start(bf16[128,128]{1,0:T(8,128)(2,1)S(1)} %get-tuple-element.33), channel_id=1, source_target_pairs={{0,896},{128,0},{256,128},{384,256},{512,384},{640,512},{768,640},... | collective-permute-start | bytes 98312 | tf_op jit(solution)/shard_map/ppermute | solution.py:319
  94.0 0.6 copy-start.3
  94.6 0.6 copy-start.5
  95.2 0.6 copy-start.7
  95.8 0.6 copy-start.9
  97.0 1.2 copy-start.2
  97.0 1.2 copy-start.4
  97.1 1.2 copy-start.6
  97.1 1.2 copy-start.8
  97.1 1.2 copy-start.10
  97.1 1.2 copy-start.12
  105.3 8.1 %collective-permute-start.7 = (bf16[2080,128]{1,0:T(8,128)(2,1)S(1)}, bf16[2080,128]{1,0:T(8,128)(2,1)S(1)}, u32[]{:S(2)}, u32[]{:S(2)}) collective-permute-start(bf16[2080,128]{1,0:T(8,128)(2,1)S(1)} %sums.1.mine), channel_id=1, source_target_pairs={{0,64},{64,0},{1,65},{65,1},{2,66},{66,2},{3,67},{67,3},{4,68},{68... | collective-permute-start | bytes 1597448 | tf_op jit(solution)/shard_map/ppermute | solution.py:284
  115.9 15.6 %all-to-all-start.1 = ((bf16[8,128,128]{2,1,0:T(8,128)(2,1)}), bf16[8,128,128]{2,1,0:T(8,128)(2,1)S(1)}, u32[]{:S(2)}, u32[]{:S(2)}) async-start(bf16[8,128,128]{2,1,0:T(8,128)(2,1)} %get-tuple-element.44), calls=%async_computation.1 | async-start | bytes 524288 | tf_op jit(solution)/shard_map/all_to_all | solution.py:290
  128.1 39.2 %copy-start.13 = (s32[1,512]{1,0:T(1,128)S(1)}, s32[1,512]{1,0:T(1,128)}, u32[]{:S(2)}) copy-start(s32[1,512]{1,0:T(1,128)} %get-tuple-element.46) | copy-start | bytes 6148
  142.2 23.7 %all-to-all-start.3 = ((f32[64,1,10]{2,1,0:T(1,128)}), f32[64,1,10]{2,1,0:T(1,128)S(1)}, u32[]{:S(2)}, u32[]{:S(2)}) async-start(f32[64,1,10]{2,1,0:T(1,128)} %bitcast.11), calls=%async_computation.3 | async-start | bytes 65536 | tf_op jit(solution)/shard_map/all_to_all | solution.py:290
  (1 other events, 0.6 us)

commit v9 on v8

--- a/solution.py
+++ b/solution.py
@@ -14,7 +14,7 @@
 TILE = 8
 BLOCK = 16
 NOTES = 32
-LIMIT = 40 * 2**20
+LIMIT = 28 * 2**20
 SMEM = pl.BlockSpec(memory_space=pltpu.SMEM)
 VMEM = pl.BlockSpec(memory_space=pltpu.VMEM)
 
@@ -158,11 +158,17 @@
     return row(2 * k) - 1.0, row(2 * k + 1)
 
 
-def turn(where, old, *outs):
-    chips = len(outs)
-    for d in range(chips):
-        at = lax.rem(where[0] + d, chips)
-        outs[d][...] = old[:, pl.ds(pl.multiple_of(at * LANES, LANES), LANES)]
+def turn(chips, where, old, other, near, far, *along):
+    def share(a, chip):
+        return a[:, pl.ds(pl.multiple_of(chip * LANES, LANES), LANES)]
+
+    near[...] = share(old, where[0])
+    far[...] = share(old, lax.rem(where[0] + chips // 2, chips))
+    for k, out in enumerate(along, 1):
+        chip = lax.rem(where[0] + chips + (1 - 2 * where[1]) * k, chips)
+        one, two = share(old, chip).astype(F32), share(other, chip).astype(F32)
+        out[:LANES] = jnp.where(where[1] == 0, one, two).astype(BF16)
+        out[LANES:] = jnp.where(where[1] == 0, two, one).astype(BF16)
 
 
 def bare(wide):
@@ -205,9 +211,13 @@
         counts.append(
             jnp.sum(jnp.where(identity, total[at, LANES:], 0.0), axis=0, keepdims=True)
         )
-    for d, old in enumerate(olds):
-        chip = lax.rem(where[0] + chips - d, chips)
+    near, far, *along = olds
+    for old, chip in ((near, where[0]), (far, lax.rem(where[0] + chips // 2, chips))):
         at = pl.ds(pl.multiple_of((2 * chip + where[1]) * LANES, LANES), LANES)
+        total[at, :LANES] += old[...].astype(F32)
+    for k, old in enumerate(along, 1):
+        chip = lax.rem(where[0] + chips - (1 - 2 * where[1]) * k, chips)
+        at = pl.ds(pl.multiple_of(2 * chip * LANES, 2 * LANES), 2 * LANES)
         total[at, :LANES] += old[...].astype(F32)
     out[: groups * LANES] = total[:, :LANES].astype(BF16)
     counts = jnp.concatenate(counts, axis=0)
@@ -313,10 +323,21 @@
         limit=60 * 2**20,
     )
     arrived = exchange(("x", "mem"), payload)
-    turned = call(turn, "turn", [shape(lists, LANES)] * chips, 2**20, old_centroids, scalars=where)
-    olds = [turned[0]]
-    for d in range(1, chips):
-        olds.append(lax.ppermute(turned[d], "x", [(i, (i + d) % chips) for i in range(chips)]))
+    steps = chips // 2
+    near, far, *along = call(
+        functools.partial(turn, chips),
+        "turn",
+        [shape(lists, LANES)] * 2 + [shape(2 * lists, LANES)] * (steps - 1),
+        2**20,
+        old_centroids,
+        across(old_centroids),
+        scalars=where,
+    )
+    olds = [near, lax.ppermute(far, "x", [(i, (i + steps) % chips) for i in range(chips)])]
+    for k in range(1, steps):
+        pairs = [(2 * i, 2 * ((i + k) % chips)) for i in range(chips)]
+        pairs += [(2 * i + 1, 2 * ((i - k) % chips) + 1) for i in range(chips)]
+        olds.append(lax.ppermute(along[k - 1], ("x", "core"), pairs))
     arrived, *olds = lax.optimization_barrier((arrived, *olds))
     columns = call(
         functools.partial(gather, capacity),

time: 170 us -> 165 us (0.971)
  starting transfers between devices: 85.9 us -> 77.3 us
  waiting for transfers between devices: 37.8 us -> 41.7 us
    ppermute x7 -> x4, starting transfers between devices: 25.8 us -> 16.3 us  [the longest x3 9.77 us: on_device(): olds.append(lax.ppermute(along[k - 1], ('x', 'core'), pairs))]
    ppermute x1 -> x2, starting transfers between devices: 6.53 us -> 9.09 us  [across(): return lax.ppermute(a, 'core', [(0, 1), (1, 0)])]
    all_to_all x3, waiting for transfers between devices: 13.3 us -> 15.4 us  [exchange(): return lax.all_to_all(a, axis, split_axis=0, concat_axis=0, tiled=True)]
    unnamed x29 -> x21, local copies, waits for them, and re-layouts: 4.54 us -> 3.34 us
    ppermute x7 -> x4, waiting for transfers between devices: 23 us -> 23.7 us  [the longest x1 23.7 us: on_device(): lax.ppermute(far, 'x', [(i, (i + steps) % chips) for i in range(chips)])]
  transfers between devices with their start and end apart: 11 -> 9, of which waited for: 4 -> 6; matrix products, arithmetic and copies ran while one was open for 1% -> 1% of each run, Pallas kernels for 6% -> 6%
where the time goes in v9:
time: 165 us; the launch traced here: 163 us
  starting transfers between devices  77.3 us (47%)
  waiting for transfers between devices  41.7 us (25%)
  Pallas kernels  25.8 us (16%)
  blocking collectives  10.8 us (7%)
  local copies, waits for them, and re-layouts  4.48 us (3%)
  other arithmetic  2.38 us (1%)
    all_to_all x3, starting transfers between devices, exchange(): return lax.all_to_all(a, axis, split_axis=0, concat_axis=0, tiled=True)  51.9 us
    pallas_call x6, Pallas kernels, call(): pl.pallas_call(kernel, in_specs=specs, out_shape=out_shape, scratch_shape...  25.8 us
    ppermute x1, waiting for transfers between devices, on_device(): lax.ppermute(far, 'x', [(i, (i + steps) % chips) for i in range(chips)])  23.7 us
    all_to_all x3, waiting for transfers between devices, exchange(): return lax.all_to_all(a, axis, split_axis=0, concat_axis=0, tiled=True)  15.4 us
    all_to_all x1, blocking collectives, exchange(): return lax.all_to_all(a, axis, split_axis=0, concat_axis=0, tiled=True)  10.8 us
    ppermute x3, starting transfers between devices, on_device(): olds.append(lax.ppermute(along[k - 1], ('x', 'core'), pairs))  9.77 us
    ppermute x2, starting transfers between devices, across(): return lax.ppermute(a, 'core', [(0, 1), (1, 0)])  9.09 us
    ppermute x1, starting transfers between devices, on_device(): lax.ppermute(far, 'x', [(i, (i + steps) % chips) for i in range(chips)])  6.53 us
  transfers between devices with their start and end apart: 9, of which 6 were waited for; matrix products, arithmetic and copies ran while one was open for 1% of the time, Pallas kernels for 6%

profile of v9, /device:TPU:1, one launch (start us, length us, event | category | flops | bytes accessed | tf_op | source)
XLA Modules:
  0.0 163.4 jit_solution(16704655675594078070)
XLA Ops:
  0.6 5.8 %prepare.1 = (bf16[512,16,128]{2,1,0:T(8,128)(2,1)}, s32[1,512]{1,0:T(1,128)}) custom-call(s32[1,512]{1,0:T(1,128)} %bitcast.19, s32[1,512]{1,0:T(1,128)} %bitcast.20, s32[1024,128]{1,0:T(8,128)} %bitcast.18, bf16[512,1024]{1,0:T(8,128)(2,1)} %refs_3_.1), custom_call_target="tpu_custom_call" | custom-call | flops 2147483648 | bytes 2097152 | tf_op jit(solution)/shard_map/prepare/pallas_call | solution.py:47
  6.4 37.3 %all-to-all-start = ((bf16[512,16,128]{2,1,0:T(8,128)(2,1)}), bf16[512,16,128]{2,1,0:T(8,128)(2,1)S(1)}, u32[]{:S(2)}, u32[]{:S(2)}) async-start(bf16[512,16,128]{2,1,0:T(8,128)(2,1)} %get-tuple-element.19), calls=%async_computation | async-start | bytes 4194304 | tf_op jit(solution)/shard_map/all_to_all | solution.py:300
  43.8 2.9 %collective-permute-start = (bf16[128,1024]{1,0:T(8,128)(2,1)S(1)}, bf16[128,1024]{1,0:T(8,128)(2,1)S(1)}, u32[]{:S(2)}, u32[]{:S(2)}) collective-permute-start(bf16[128,1024]{1,0:T(8,128)(2,1)S(1)} %copy-done), channel_id=1, source_target_pairs={{0,64},{64,0},{1,65},{65,1},{2,66},{66,2},{3,67},{67,3},{4,68},{68... | collective-permute-start | bytes 786440 | tf_op jit(solution)/shard_map/ppermute | solution.py:294
  46.8 1.1 collective-permute-done.other
  49.1 4.3 %collective-permute-start.2 = (bf16[256,128]{1,0:T(8,128)(2,1)S(1)}, bf16[256,128]{1,0:T(8,128)(2,1)S(1)}, u32[]{:S(2)}, u32[]{:S(2)}) collective-permute-start(bf16[256,128]{1,0:T(8,128)(2,1)S(1)} %get-tuple-element.22), channel_id=1, source_target_pairs={{0,128},{128,256},{256,384},{384,512},{512,640},{640,768},{768,896... | collective-permute-start | bytes 196616 | tf_op jit(solution)/shard_map/ppermute | solution.py:340
  53.3 3.1 %collective-permute-start.3 = (bf16[256,128]{1,0:T(8,128)(2,1)S(1)}, bf16[256,128]{1,0:T(8,128)(2,1)S(1)}, u32[]{:S(2)}, u32[]{:S(2)}) collective-permute-start(bf16[256,128]{1,0:T(8,128)(2,1)S(1)} %get-tuple-element.23), channel_id=1, source_target_pairs={{0,256},{128,384},{256,512},{384,640},{512,768},{640,896},{768,0},... | collective-permute-start | bytes 196616 | tf_op jit(solution)/shard_map/ppermute | solution.py:340
  56.5 2.4 %collective-permute-start.4 = (bf16[256,128]{1,0:T(8,128)(2,1)S(1)}, bf16[256,128]{1,0:T(8,128)(2,1)S(1)}, u32[]{:S(2)}, u32[]{:S(2)}) collective-permute-start(bf16[256,128]{1,0:T(8,128)(2,1)S(1)} %get-tuple-element.24), channel_id=1, source_target_pairs={{0,384},{128,512},{256,640},{384,768},{512,896},{640,0},{768,128},... | collective-permute-start | bytes 196616 | tf_op jit(solution)/shard_map/ppermute | solution.py:340
  58.9 6.5 %collective-permute-start.1 = (bf16[128,128]{1,0:T(8,128)(2,1)S(1)}, bf16[128,128]{1,0:T(8,128)(2,1)S(1)}, u32[]{:S(2)}, u32[]{:S(2)}) collective-permute-start(bf16[128,128]{1,0:T(8,128)(2,1)S(1)} %get-tuple-element.21), channel_id=1, source_target_pairs={{0,512},{128,640},{256,768},{384,896},{512,0},{640,128},{768,256},... | collective-permute-start | bytes 98312 | tf_op jit(solution)/shard_map/ppermute | solution.py:336
  65.4 23.7 %collective-permute-done.1.refs_1_ = bf16[128,128]{1,0:T(8,128)(2,1)S(1)} collective-permute-done((bf16[128,128]{1,0:T(8,128)(2,1)S(1)}, bf16[128,128]{1,0:T(8,128)(2,1)S(1)}, u32[]{:S(2)}, u32[]{:S(2)}) %collective-permute-start.1) | collective-permute-done | bytes 32800 | tf_op jit(solution)/shard_map/ppermute | solution.py:336
  90.9 3.3 %all-to-all-done.arrived = bf16[512,16,128]{2,1,0:T(8,128)(2,1)S(1)} async-done(((bf16[512,16,128]{2,1,0:T(8,128)(2,1)}), bf16[512,16,128]{2,1,0:T(8,128)(2,1)S(1)}, u32[]{:S(2)}, u32[]{:S(2)}) %all-to-all-start) | async-done | bytes 2097184 | tf_op jit(solution)/shard_map/all_to_all | solution.py:300
  94.2 1.1 gather.1.columns
  95.4 7.0 %sums.1.mine = bf16[2080,128]{1,0:T(8,128)(2,1)S(1)} custom-call(s32[2]{0:T(128)S(1)} %pad_add_fusion.where, bf16[8,672,128]{2,1,0:T(8,128)(2,1)S(1)} %gather.1.columns, bf16[128,128]{1,0:T(8,128)(2,1)S(1)} %copy-done.6, bf16[128,128]{1,0:T(8,128)(2,1)S(1)} %copy-done.8, bf16[256,128]{1,0:T(8,128)(2,1)S(1)} %collective-permute-done.2.refs_2_, ...), custom_call_target="tpu_custom_call" | custom-call | flops 4294967296 | bytes 2097152 | tf_op jit(solution)/shard_map/sums/pallas_call | solution.py:47
  102.4 6.2 %collective-permute-start.5 = (bf16[2080,128]{1,0:T(8,128)(2,1)S(1)}, bf16[2080,128]{1,0:T(8,128)(2,1)S(1)}, u32[]{:S(2)}, u32[]{:S(2)}) collective-permute-start(bf16[2080,128]{1,0:T(8,128)(2,1)S(1)} %sums.1.mine), channel_id=1, source_target_pairs={{0,64},{64,0},{1,65},{65,1},{2,66},{66,2},{3,67},{67,3},{4,68},{68... | collective-permute-start | bytes 1597448 | tf_op jit(solution)/shard_map/ppermute | solution.py:294
  108.6 1.5 collective-permute-done.5.theirs
  110.2 2.6 %refit.1 = (bf16[8,128,128]{2,1,0:T(8,128)(2,1)}, bf16[2048,256]{1,0:T(8,128)(2,1)S(1)}) custom-call(s32[2]{0:T(128)S(1)} %pad_add_fusion.where, bf16[2080,128]{1,0:T(8,128)(2,1)S(1)} %sums.1.mine, bf16[2080,128]{1,0:T(8,128)(2,1)S(1)} %collective-permute-done.5.theirs), custom_call_target="tpu_custom_call" | custom-call | flops 16777216 | bytes 2097152 | tf_op jit(solution)/shard_map/refit/pallas_call | solution.py:47
  112.8 3.6 %all-to-all-start.1 = ((bf16[8,128,128]{2,1,0:T(8,128)(2,1)}), bf16[8,128,128]{2,1,0:T(8,128)(2,1)S(1)}, u32[]{:S(2)}, u32[]{:S(2)}) async-start(bf16[8,128,128]{2,1,0:T(8,128)(2,1)} %get-tuple-element.32), calls=%async_computation.1 | async-start | bytes 524288 | tf_op jit(solution)/shard_map/all_to_all | solution.py:300
  116.3 8.7 %score.1 = f32[8,640]{1,0:T(8,128)S(1)} custom-call(bf16[8,672,128]{2,1,0:T(8,128)(2,1)S(1)} %gather.1.columns, bf16[2048,256]{1,0:T(8,128)(2,1)S(1)} %get-tuple-element.31.lists_of), custom_call_target="tpu_custom_call" | custom-call | flops 8589934592 | bytes 2097152 | tf_op jit(solution)/shard_map/score/pallas_call | solution.py:47
  125.1 2.3 %all-to-all-done.1 = bf16[8,128,128]{2,1,0:T(8,128)(2,1)S(1)} async-done(((bf16[8,128,128]{2,1,0:T(8,128)(2,1)}), bf16[8,128,128]{2,1,0:T(8,128)(2,1)S(1)}, u32[]{:S(2)}, u32[]{:S(2)}) %all-to-all-start.1) | async-done | bytes 262176 | tf_op jit(solution)/shard_map/all_to_all | solution.py:300
  127.4 10.8 %all_to_all.20 = f32[8,1,640]{2,1,0:T(1,128)S(1)} all-to-all(f32[8,1,640]{2,1,0:T(1,128)S(1)} %copy.17), channel_id=1, replica_groups=mesh['x'=8,'core'=2,'mem'=64] {'x'}, dimensions={0} | all-to-all | bytes 40960 | tf_op jit(solution)/shard_map/all_to_all | solution.py:300
  139.2 11.0 %all-to-all-start.3 = ((f32[64,1,10]{2,1,0:T(1,128)}), f32[64,1,10]{2,1,0:T(1,128)S(1)}, u32[]{:S(2)}, u32[]{:S(2)}) async-start(f32[64,1,10]{2,1,0:T(1,128)} %bitcast.11), calls=%async_computation.3 | async-start | bytes 65536 | tf_op jit(solution)/shard_map/all_to_all | solution.py:300
  150.5 0.9 copy.20
  151.3 9.8 %all-to-all-done.3 = f32[64,1,10]{2,1,0:T(1,128)S(1)} async-done(((f32[64,1,10]{2,1,0:T(1,128)}), f32[64,1,10]{2,1,0:T(1,128)S(1)}, u32[]{:S(2)}, u32[]{:S(2)}) %all-to-all-start.3) | async-done | bytes 2592 | tf_op jit(solution)/shard_map/all_to_all | solution.py:300
  161.6 0.7 reduce.4
  162.5 0.9 select_reduce_fusion
  (37 shorter events, 5.0 us)
Async XLA Ops:
  6.4 37.4 %copy-start = (bf16[128,1024]{1,0:T(8,128)(2,1)S(1)}, bf16[128,1024]{1,0:T(8,128)(2,1)}, u32[]{:S(2)}) copy-start(bf16[128,1024]{1,0:T(8,128)(2,1)} %old.1) | copy-start | bytes 786436
  6.4 87.8 %all-to-all-start = ((bf16[512,16,128]{2,1,0:T(8,128)(2,1)}), bf16[512,16,128]{2,1,0:T(8,128)(2,1)S(1)}, u32[]{:S(2)}, u32[]{:S(2)}) async-start(bf16[512,16,128]{2,1,0:T(8,128)(2,1)} %get-tuple-element.19), calls=%async_computation | async-start | bytes 4194304 | tf_op jit(solution)/shard_map/all_to_all | solution.py:300
  43.8 4.0 %collective-permute-start = (bf16[128,1024]{1,0:T(8,128)(2,1)S(1)}, bf16[128,1024]{1,0:T(8,128)(2,1)S(1)}, u32[]{:S(2)}, u32[]{:S(2)}) collective-permute-start(bf16[128,1024]{1,0:T(8,128)(2,1)S(1)} %copy-done), channel_id=1, source_target_pairs={{0,64},{64,0},{1,65},{65,1},{2,66},{66,2},{3,67},{67,3},{4,68},{68... | collective-permute-start | bytes 786440 | tf_op jit(solution)/shard_map/ppermute | solution.py:294
  48.4 0.6 copy-start.5
  49.1 40.6 %collective-permute-start.2 = (bf16[256,128]{1,0:T(8,128)(2,1)S(1)}, bf16[256,128]{1,0:T(8,128)(2,1)S(1)}, u32[]{:S(2)}, u32[]{:S(2)}) collective-permute-start(bf16[256,128]{1,0:T(8,128)(2,1)S(1)} %get-tuple-element.22), channel_id=1, source_target_pairs={{0,128},{128,256},{256,384},{384,512},{512,640},{640,768},{768,896... | collective-permute-start | bytes 196616 | tf_op jit(solution)/shard_map/ppermute | solution.py:340
  53.3 36.3 %collective-permute-start.3 = (bf16[256,128]{1,0:T(8,128)(2,1)S(1)}, bf16[256,128]{1,0:T(8,128)(2,1)S(1)}, u32[]{:S(2)}, u32[]{:S(2)}) collective-permute-start(bf16[256,128]{1,0:T(8,128)(2,1)S(1)} %get-tuple-element.23), channel_id=1, source_target_pairs={{0,256},{128,384},{256,512},{384,640},{512,768},{640,896},{768,0},... | collective-permute-start | bytes 196616 | tf_op jit(solution)/shard_map/ppermute | solution.py:340
  56.5 33.9 %collective-permute-start.4 = (bf16[256,128]{1,0:T(8,128)(2,1)S(1)}, bf16[256,128]{1,0:T(8,128)(2,1)S(1)}, u32[]{:S(2)}, u32[]{:S(2)}) collective-permute-start(bf16[256,128]{1,0:T(8,128)(2,1)S(1)} %get-tuple-element.24), channel_id=1, source_target_pairs={{0,384},{128,512},{256,640},{384,768},{512,896},{640,0},{768,128},... | collective-permute-start | bytes 196616 | tf_op jit(solution)/shard_map/ppermute | solution.py:340
  58.9 30.2 %collective-permute-start.1 = (bf16[128,128]{1,0:T(8,128)(2,1)S(1)}, bf16[128,128]{1,0:T(8,128)(2,1)S(1)}, u32[]{:S(2)}, u32[]{:S(2)}) collective-permute-start(bf16[128,128]{1,0:T(8,128)(2,1)S(1)} %get-tuple-element.21), channel_id=1, source_target_pairs={{0,512},{128,640},{256,768},{384,896},{512,0},{640,128},{768,256},... | collective-permute-start | bytes 98312 | tf_op jit(solution)/shard_map/ppermute | solution.py:336
  89.1 0.6 copy-start.7
  89.7 0.6 copy-start.1
  90.3 0.6 copy-start.3
  94.2 1.1 copy-start.2
  94.2 1.1 copy-start.4
  94.2 1.1 copy-start.6
  94.2 1.1 copy-start.8
  102.4 7.8 %collective-permute-start.5 = (bf16[2080,128]{1,0:T(8,128)(2,1)S(1)}, bf16[2080,128]{1,0:T(8,128)(2,1)S(1)}, u32[]{:S(2)}, u32[]{:S(2)}) collective-permute-start(bf16[2080,128]{1,0:T(8,128)(2,1)S(1)} %sums.1.mine), channel_id=1, source_target_pairs={{0,64},{64,0},{1,65},{65,1},{2,66},{66,2},{3,67},{67,3},{4,68},{68... | collective-permute-start | bytes 1597448 | tf_op jit(solution)/shard_map/ppermute | solution.py:294
  112.8 14.6 %all-to-all-start.1 = ((bf16[8,128,128]{2,1,0:T(8,128)(2,1)}), bf16[8,128,128]{2,1,0:T(8,128)(2,1)S(1)}, u32[]{:S(2)}, u32[]{:S(2)}) async-start(bf16[8,128,128]{2,1,0:T(8,128)(2,1)} %get-tuple-element.32), calls=%async_computation.1 | async-start | bytes 524288 | tf_op jit(solution)/shard_map/all_to_all | solution.py:300
  125.0 37.5 %copy-start.9 = (s32[1,512]{1,0:T(1,128)S(1)}, s32[1,512]{1,0:T(1,128)}, u32[]{:S(2)}) copy-start(s32[1,512]{1,0:T(1,128)} %get-tuple-element.34) | copy-start | bytes 6148
  139.2 21.9 %all-to-all-start.3 = ((f32[64,1,10]{2,1,0:T(1,128)}), f32[64,1,10]{2,1,0:T(1,128)S(1)}, u32[]{:S(2)}, u32[]{:S(2)}) async-start(f32[64,1,10]{2,1,0:T(1,128)} %bitcast.11), calls=%async_computation.3 | async-start | bytes 65536 | tf_op jit(solution)/shard_map/all_to_all | solution.py:300

commit v10 on v9

--- a/solution.py
+++ b/solution.py
@@ -11,8 +11,8 @@
 F32 = jnp.float32
 BF16 = jnp.bfloat16
 LANES = 128
-TILE = 8
-BLOCK = 16
+ROWS = 4
+WIDE = 3 * LANES
 NOTES = 32
 LIMIT = 28 * 2**20
 SMEM = pl.BlockSpec(memory_space=pltpu.SMEM)
@@ -93,7 +93,7 @@
     earlier = dot(hot(is_owner), before, ((1,), (0,)))
     rank = jnp.sum(jnp.where(is_owner, earlier, 0.0), axis=0, keepdims=True)
     place[...] = (first_owner * capacity + rank).astype(jnp.int32)
-    spot = jnp.where(rank < TILE, first_owner * TILE + rank, rank * members + first_owner)
+    spot = rank * members + first_owner
     order = hot(rows_of((members * capacity, vectors)) == spot)
     copies[3].wait()
     packed = dot(order, embeddings[...], ((1,), (0,)))
@@ -102,15 +102,13 @@
     spread = [jnp.where(ranked, digit, 0.0) for digit in digits]
     spread.append(jnp.zeros((LANES - 16 * len(digits), vectors), F32))
     labels = dot(hot(is_owner), jnp.concatenate(spread, axis=0).astype(BF16), ((1,), (1,)))
-    empty = [jnp.zeros((members, LANES), F32)] * (BLOCK - capacity - 1)
+    empty = [jnp.zeros((members, LANES), F32)] * (ROWS * WIDE // LANES - capacity - 1)
     for j in range(embeddings.shape[1] // LANES):
         at = slice(j * LANES, (j + 1) * LANES)
-        rest = [packed[p * members : (p + 1) * members, at] for p in range(TILE, capacity)]
-        block = [
-            packed[: TILE * members, at].reshape(members, TILE, LANES),
-            jnp.stack(rest + [labels] + empty, axis=1),
-        ]
-        payload[j * members : (j + 1) * members] = jnp.concatenate(block, axis=1).astype(BF16)
+        rows = [packed[p * members : (p + 1) * members, at] for p in range(capacity)]
+        rows += [labels] + empty
+        block = [jnp.stack(rows[t : t + ROWS], axis=1) for t in range(0, len(rows), ROWS)]
+        payload[j * members : (j + 1) * members] = jnp.concatenate(block, axis=2).astype(BF16)
 
 
 def gather(capacity, arrived, out):
@@ -119,25 +117,21 @@
     count = members * capacity
     slots = rows - NOTES
     vector = lanes_of((members, slots))
-    from_member = jnp.where(
-        vector < TILE * members, whole(vector, TILE), vector - members * whole(vector, members)
-    )
+    from_member = vector - members * whole(vector, members)
     from_member = hot(rows_of((members, slots)) == from_member)
-    vector = lanes_of((16, slots))
-    rank = jnp.where(
-        vector < TILE * members, vector - TILE * whole(vector, TILE), whole(vector, members)
-    )
-    ranked = rows_of((16, slots)) == rank
+    ranked = rows_of((16, slots)) == whole(lanes_of((16, slots)), members)
     for s in range(chips):
         values = arrived[s * members : (s + 1) * members].astype(F32)
-        out[s, : TILE * members] = (
-            values[:, :TILE].reshape(TILE * members, LANES).astype(BF16)
-        )
-        for p in range(TILE, capacity):
-            out[s, p * members : (p + 1) * members] = values[:, p].astype(BF16)
+
+        def row(p):
+            start = p // ROWS * LANES
+            return values[:, p % ROWS, start : start + LANES].astype(BF16)
+
+        for p in range(capacity):
+            out[s, p * members : (p + 1) * members] = row(p)
         if slots > count:
             out[s, count:slots] = jnp.zeros((slots - count, LANES), BF16)
-        found = dot(values[:, capacity].astype(BF16), from_member, ((0,), (0,)))
+        found = dot(row(capacity), from_member, ((0,), (0,)))
         notes = []
         for k in range(4):
             row = jnp.where(ranked, found[k * 16 : (k + 1) * 16], 0.0)
@@ -304,7 +298,7 @@
         functools.partial(prepare, members, capacity),
         "prepare",
         (
-            shape(chips * members, BLOCK, LANES),
+            shape(chips * members, ROWS, WIDE),
             shape(1, vectors, kind=jnp.int32),
         ),
         2**31,
@@ -378,13 +372,7 @@
     fresh = returned_parts.swapaxes(0, 1).reshape(lists, width)
     scores = exchange("x", scores.reshape(chips, 1, slots))
     margin = jnp.sum(scores.reshape(chips, slots), axis=0) * (1.0 / width)
-    margin = jnp.concatenate(
-        [
-            margin[: TILE * members].reshape(members, TILE),
-            margin[TILE * members : count].reshape(capacity - TILE, members).T,
-        ],
-        axis=1,
-    )
+    margin = margin[:count].reshape(capacity, members).T
     returned = exchange("mem", margin.reshape(members, 1, capacity))
     spots = jnp.arange(count, dtype=jnp.int32)
     margins = jnp.sum(

time: 165 us -> 155 us (0.939)
  waiting for transfers between devices: 41.7 us -> 33.6 us
  Pallas kernels: 25.8 us -> 28.9 us
  starting transfers between devices: 77.3 us -> 74.8 us
  local copies, waits for them, and re-layouts: 4.48 us -> 2.55 us
    ppermute x1, waiting for transfers between devices: 23.7 us -> 13.3 us  [on_device(): lax.ppermute(far, 'x', [(i, (i + steps) % chips) for i in range(chips)])]
    pallas_call x6, Pallas kernels: 25.8 us -> 28.9 us  [call(): pl.pallas_call(kernel, in_specs=specs, out_shape=out_shape, scratch_shape...]
    unnamed x21 -> x5, local copies, waits for them, and re-layouts: 3.34 us -> 0.87 us
    all_to_all x3, starting transfers between devices: 51.9 us -> 49.7 us  [exchange(): return lax.all_to_all(a, axis, split_axis=0, concat_axis=0, tiled=True)]
    all_to_all x3, waiting for transfers between devices: 15.4 us -> 17.1 us  [exchange(): return lax.all_to_all(a, axis, split_axis=0, concat_axis=0, tiled=True)]
  transfers between devices with their start and end apart: 9 -> 9, of which waited for: 6 -> 7; matrix products, arithmetic and copies ran while one was open for 1% -> 1% of each run, Pallas kernels for 6% -> 6%
where the time goes in v10:
time: 155 us; the launch traced here: 153 us
  starting transfers between devices  74.8 us (48%)
  waiting for transfers between devices  33.6 us (22%)
  Pallas kernels  28.9 us (19%)
  blocking collectives  10.8 us (7%)
  local copies, waits for them, and re-layouts  2.55 us (2%)
  other arithmetic  1.74 us (1%)
    all_to_all x3, starting transfers between devices, exchange(): return lax.all_to_all(a, axis, split_axis=0, concat_axis=0, tiled=True)  49.7 us
    pallas_call x6, Pallas kernels, call(): pl.pallas_call(kernel, in_specs=specs, out_shape=out_shape, scratch_shape...  28.9 us
    all_to_all x3, waiting for transfers between devices, exchange(): return lax.all_to_all(a, axis, split_axis=0, concat_axis=0, tiled=True)  17.1 us
    ppermute x1, waiting for transfers between devices, on_device(): lax.ppermute(far, 'x', [(i, (i + steps) % chips) for i in range(chips)])  13.3 us
    all_to_all x1, blocking collectives, exchange(): return lax.all_to_all(a, axis, split_axis=0, concat_axis=0, tiled=True)  10.8 us
    ppermute x3, starting transfers between devices, on_device(): olds.append(lax.ppermute(along[k - 1], ('x', 'core'), pairs))  9.79 us
    ppermute x2, starting transfers between devices, across(): return lax.ppermute(a, 'core', [(0, 1), (1, 0)])  8.95 us
    ppermute x1, starting transfers between devices, on_device(): lax.ppermute(far, 'x', [(i, (i + steps) % chips) for i in range(chips)])  6.35 us
  transfers between devices with their start and end apart: 9, of which 7 were waited for; matrix products, arithmetic and copies ran while one was open for 1% of the time, Pallas kernels for 6%

profile of v10, /device:TPU:1, one launch (start us, length us, event | category | flops | bytes accessed | tf_op | source)
XLA Modules:
  0.0 153.2 jit_solution(6153585659152706780)
XLA Ops:
  0.6 7.4 %prepare.1 = (bf16[512,4,384]{2,1,0:T(4,128)(2,1)}, s32[1,512]{1,0:T(1,128)}) custom-call(s32[1,512]{1,0:T(1,128)} %bitcast.18, s32[1,512]{1,0:T(1,128)} %bitcast.19, s32[1024,128]{1,0:T(8,128)} %bitcast.17, bf16[512,1024]{1,0:T(8,128)(2,1)} %refs_3_.1), custom_call_target="tpu_custom_call" | custom-call | flops 2147483648 | bytes 2097152 | tf_op jit(solution)/shard_map/prepare/pallas_call | solution.py:47
  8.0 37.3 %all-to-all-start = ((bf16[512,4,384]{2,1,0:T(4,128)(2,1)}), bf16[512,4,384]{2,1,0:T(4,128)(2,1)S(1)}, u32[]{:S(2)}, u32[]{:S(2)}) async-start(bf16[512,4,384]{2,1,0:T(4,128)(2,1)} %get-tuple-element.19), calls=%async_computation | async-start | bytes 3145728 | tf_op jit(solution)/shard_map/all_to_all | solution.py:294
  45.4 2.9 %collective-permute-start = (bf16[128,1024]{1,0:T(8,128)(2,1)S(1)}, bf16[128,1024]{1,0:T(8,128)(2,1)S(1)}, u32[]{:S(2)}, u32[]{:S(2)}) collective-permute-start(bf16[128,1024]{1,0:T(8,128)(2,1)S(1)} %copy-done), channel_id=1, source_target_pairs={{0,64},{64,0},{1,65},{65,1},{2,66},{66,2},{3,67},{67,3},{4,68},{68... | collective-permute-start | bytes 786440 | tf_op jit(solution)/shard_map/ppermute | solution.py:288
  48.4 1.1 collective-permute-done.other
  50.0 4.3 %collective-permute-start.2 = (bf16[256,128]{1,0:T(8,128)(2,1)S(1)}, bf16[256,128]{1,0:T(8,128)(2,1)S(1)}, u32[]{:S(2)}, u32[]{:S(2)}) collective-permute-start(bf16[256,128]{1,0:T(8,128)(2,1)S(1)} %get-tuple-element.22), channel_id=1, source_target_pairs={{0,128},{128,256},{256,384},{384,512},{512,640},{640,768},{768,896... | collective-permute-start | bytes 196616 | tf_op jit(solution)/shard_map/ppermute | solution.py:334
  54.3 3.1 %collective-permute-start.3 = (bf16[256,128]{1,0:T(8,128)(2,1)S(1)}, bf16[256,128]{1,0:T(8,128)(2,1)S(1)}, u32[]{:S(2)}, u32[]{:S(2)}) collective-permute-start(bf16[256,128]{1,0:T(8,128)(2,1)S(1)} %get-tuple-element.23), channel_id=1, source_target_pairs={{0,256},{128,384},{256,512},{384,640},{512,768},{640,896},{768,0},... | collective-permute-start | bytes 196616 | tf_op jit(solution)/shard_map/ppermute | solution.py:334
  57.5 2.4 %collective-permute-start.4 = (bf16[256,128]{1,0:T(8,128)(2,1)S(1)}, bf16[256,128]{1,0:T(8,128)(2,1)S(1)}, u32[]{:S(2)}, u32[]{:S(2)}) collective-permute-start(bf16[256,128]{1,0:T(8,128)(2,1)S(1)} %get-tuple-element.24), channel_id=1, source_target_pairs={{0,384},{128,512},{256,640},{384,768},{512,896},{640,0},{768,128},... | collective-permute-start | bytes 196616 | tf_op jit(solution)/shard_map/ppermute | solution.py:334
  59.8 6.3 %collective-permute-start.1 = (bf16[128,128]{1,0:T(8,128)(2,1)S(1)}, bf16[128,128]{1,0:T(8,128)(2,1)S(1)}, u32[]{:S(2)}, u32[]{:S(2)}) collective-permute-start(bf16[128,128]{1,0:T(8,128)(2,1)S(1)} %get-tuple-element.21), channel_id=1, source_target_pairs={{0,512},{128,640},{256,768},{384,896},{512,0},{640,128},{768,256},... | collective-permute-start | bytes 98312 | tf_op jit(solution)/shard_map/ppermute | solution.py:330
  66.2 13.3 %collective-permute-done.1.refs_1_ = bf16[128,128]{1,0:T(8,128)(2,1)S(1)} collective-permute-done((bf16[128,128]{1,0:T(8,128)(2,1)S(1)}, bf16[128,128]{1,0:T(8,128)(2,1)S(1)}, u32[]{:S(2)}, u32[]{:S(2)}) %collective-permute-start.1) | collective-permute-done | bytes 32800 | tf_op jit(solution)/shard_map/ppermute | solution.py:330
  80.1 5.0 %all-to-all-done.arrived = bf16[512,4,384]{2,1,0:T(4,128)(2,1)S(1)} async-done(((bf16[512,4,384]{2,1,0:T(4,128)(2,1)}), bf16[512,4,384]{2,1,0:T(4,128)(2,1)S(1)}, u32[]{:S(2)}, u32[]{:S(2)}) %all-to-all-start) | async-done | bytes 1572896 | tf_op jit(solution)/shard_map/all_to_all | solution.py:294
  85.1 2.6 %gather.1.columns = bf16[8,672,128]{2,1,0:T(8,128)(2,1)S(1)} custom-call(bf16[512,4,384]{2,1,0:T(4,128)(2,1)S(1)} %all-to-all-done.arrived), custom_call_target="tpu_custom_call" | custom-call | flops 16777216 | bytes 2097152 | tf_op jit(solution)/shard_map/gather/pallas_call | solution.py:47
  87.6 7.0 %sums.1.mine = bf16[2080,128]{1,0:T(8,128)(2,1)S(1)} custom-call(s32[2]{0:T(128)S(1)} %pad_add_fusion.where, bf16[8,672,128]{2,1,0:T(8,128)(2,1)S(1)} %gather.1.columns, bf16[128,128]{1,0:T(8,128)(2,1)S(1)} %get-tuple-element.26.refs_0_, bf16[128,128]{1,0:T(8,128)(2,1)S(1)} %collective-permute-done.1.refs_1_, ...), custom_call_target="tpu_custom_call" | custom-call | flops 4294967296 | bytes 2097152 | tf_op jit(solution)/shard_map/sums/pallas_call | solution.py:47
  94.7 6.1 %collective-permute-start.5 = (bf16[2080,128]{1,0:T(8,128)(2,1)S(1)}, bf16[2080,128]{1,0:T(8,128)(2,1)S(1)}, u32[]{:S(2)}, u32[]{:S(2)}) collective-permute-start(bf16[2080,128]{1,0:T(8,128)(2,1)S(1)} %sums.1.mine), channel_id=1, source_target_pairs={{0,64},{64,0},{1,65},{65,1},{2,66},{66,2},{3,67},{67,3},{4,68},{68... | collective-permute-start | bytes 1597448 | tf_op jit(solution)/shard_map/ppermute | solution.py:288
  100.8 1.5 collective-permute-done.5.theirs
  102.3 2.6 %refit.1 = (bf16[8,128,128]{2,1,0:T(8,128)(2,1)}, bf16[2048,256]{1,0:T(8,128)(2,1)S(1)}) custom-call(s32[2]{0:T(128)S(1)} %pad_add_fusion.where, bf16[2080,128]{1,0:T(8,128)(2,1)S(1)} %sums.1.mine, bf16[2080,128]{1,0:T(8,128)(2,1)S(1)} %collective-permute-done.5.theirs), custom_call_target="tpu_custom_call" | custom-call | flops 16777216 | bytes 2097152 | tf_op jit(solution)/shard_map/refit/pallas_call | solution.py:47
  104.9 3.5 %all-to-all-start.1 = ((bf16[8,128,128]{2,1,0:T(8,128)(2,1)}), bf16[8,128,128]{2,1,0:T(8,128)(2,1)S(1)}, u32[]{:S(2)}, u32[]{:S(2)}) async-start(bf16[8,128,128]{2,1,0:T(8,128)(2,1)} %get-tuple-element.32), calls=%async_computation.1 | async-start | bytes 524288 | tf_op jit(solution)/shard_map/all_to_all | solution.py:294
  108.3 8.7 %score.1 = f32[8,640]{1,0:T(8,128)S(1)} custom-call(bf16[8,672,128]{2,1,0:T(8,128)(2,1)S(1)} %gather.1.columns, bf16[2048,256]{1,0:T(8,128)(2,1)S(1)} %get-tuple-element.31.lists_of), custom_call_target="tpu_custom_call" | custom-call | flops 8589934592 | bytes 2097152 | tf_op jit(solution)/shard_map/score/pallas_call | solution.py:47
  117.1 2.3 %all-to-all-done.1 = bf16[8,128,128]{2,1,0:T(8,128)(2,1)S(1)} async-done(((bf16[8,128,128]{2,1,0:T(8,128)(2,1)}), bf16[8,128,128]{2,1,0:T(8,128)(2,1)S(1)}, u32[]{:S(2)}, u32[]{:S(2)}) %all-to-all-start.1) | async-done | bytes 262176 | tf_op jit(solution)/shard_map/all_to_all | solution.py:294
  119.4 10.8 %all_to_all.20 = f32[8,1,640]{2,1,0:T(1,128)S(1)} all-to-all(f32[8,1,640]{2,1,0:T(1,128)S(1)} %copy.17), channel_id=1, replica_groups=mesh['x'=8,'core'=2,'mem'=64] {'x'}, dimensions={0} | all-to-all | bytes 40960 | tf_op jit(solution)/shard_map/all_to_all | solution.py:294
  131.0 8.9 %all-to-all-start.3 = ((f32[64,1,10]{2,1,0:T(1,128)}), f32[64,1,10]{2,1,0:T(1,128)S(1)}, u32[]{:S(2)}, u32[]{:S(2)}) async-start(f32[64,1,10]{2,1,0:T(1,128)} %copy.18), calls=%async_computation.3 | async-start | bytes 65536 | tf_op jit(solution)/shard_map/all_to_all | solution.py:294
  140.2 0.9 copy.19
  141.0 9.8 %all-to-all-done.3 = f32[64,1,10]{2,1,0:T(1,128)S(1)} async-done(((f32[64,1,10]{2,1,0:T(1,128)}), f32[64,1,10]{2,1,0:T(1,128)S(1)}, u32[]{:S(2)}, u32[]{:S(2)}) %all-to-all-start.3) | async-done | bytes 2592 | tf_op jit(solution)/shard_map/all_to_all | solution.py:294
  151.4 0.8 reduce.4
  152.3 0.9 select_reduce_fusion
  (17 shorter events, 3.0 us)
Async XLA Ops:
  8.0 37.4 %copy-start = (bf16[128,1024]{1,0:T(8,128)(2,1)S(1)}, bf16[128,1024]{1,0:T(8,128)(2,1)}, u32[]{:S(2)}) copy-start(bf16[128,1024]{1,0:T(8,128)(2,1)} %old.1) | copy-start | bytes 786436
  8.0 77.0 %all-to-all-start = ((bf16[512,4,384]{2,1,0:T(4,128)(2,1)}), bf16[512,4,384]{2,1,0:T(4,128)(2,1)S(1)}, u32[]{:S(2)}, u32[]{:S(2)}) async-start(bf16[512,4,384]{2,1,0:T(4,128)(2,1)} %get-tuple-element.19), calls=%async_computation | async-start | bytes 3145728 | tf_op jit(solution)/shard_map/all_to_all | solution.py:294
  45.4 4.0 %collective-permute-start = (bf16[128,1024]{1,0:T(8,128)(2,1)S(1)}, bf16[128,1024]{1,0:T(8,128)(2,1)S(1)}, u32[]{:S(2)}, u32[]{:S(2)}) collective-permute-start(bf16[128,1024]{1,0:T(8,128)(2,1)S(1)} %copy-done), channel_id=1, source_target_pairs={{0,64},{64,0},{1,65},{65,1},{2,66},{66,2},{3,67},{67,3},{4,68},{68... | collective-permute-start | bytes 786440 | tf_op jit(solution)/shard_map/ppermute | solution.py:288
  50.0 29.4 %collective-permute-start.2 = (bf16[256,128]{1,0:T(8,128)(2,1)S(1)}, bf16[256,128]{1,0:T(8,128)(2,1)S(1)}, u32[]{:S(2)}, u32[]{:S(2)}) collective-permute-start(bf16[256,128]{1,0:T(8,128)(2,1)S(1)} %get-tuple-element.22), channel_id=1, source_target_pairs={{0,128},{128,256},{256,384},{384,512},{512,640},{640,768},{768,896... | collective-permute-start | bytes 196616 | tf_op jit(solution)/shard_map/ppermute | solution.py:334
  54.3 25.1 %collective-permute-start.3 = (bf16[256,128]{1,0:T(8,128)(2,1)S(1)}, bf16[256,128]{1,0:T(8,128)(2,1)S(1)}, u32[]{:S(2)}, u32[]{:S(2)}) collective-permute-start(bf16[256,128]{1,0:T(8,128)(2,1)S(1)} %get-tuple-element.23), channel_id=1, source_target_pairs={{0,256},{128,384},{256,512},{384,640},{512,768},{640,896},{768,0},... | collective-permute-start | bytes 196616 | tf_op jit(solution)/shard_map/ppermute | solution.py:334
  57.5 22.6 %collective-permute-start.4 = (bf16[256,128]{1,0:T(8,128)(2,1)S(1)}, bf16[256,128]{1,0:T(8,128)(2,1)S(1)}, u32[]{:S(2)}, u32[]{:S(2)}) collective-permute-start(bf16[256,128]{1,0:T(8,128)(2,1)S(1)} %get-tuple-element.24), channel_id=1, source_target_pairs={{0,384},{128,512},{256,640},{384,768},{512,896},{640,0},{768,128},... | collective-permute-start | bytes 196616 | tf_op jit(solution)/shard_map/ppermute | solution.py:334
  59.8 19.6 %collective-permute-start.1 = (bf16[128,128]{1,0:T(8,128)(2,1)S(1)}, bf16[128,128]{1,0:T(8,128)(2,1)S(1)}, u32[]{:S(2)}, u32[]{:S(2)}) collective-permute-start(bf16[128,128]{1,0:T(8,128)(2,1)S(1)} %get-tuple-element.21), channel_id=1, source_target_pairs={{0,512},{128,640},{256,768},{384,896},{512,0},{640,128},{768,256},... | collective-permute-start | bytes 98312 | tf_op jit(solution)/shard_map/ppermute | solution.py:330
  94.7 7.6 %collective-permute-start.5 = (bf16[2080,128]{1,0:T(8,128)(2,1)S(1)}, bf16[2080,128]{1,0:T(8,128)(2,1)S(1)}, u32[]{:S(2)}, u32[]{:S(2)}) collective-permute-start(bf16[2080,128]{1,0:T(8,128)(2,1)S(1)} %sums.1.mine), channel_id=1, source_target_pairs={{0,64},{64,0},{1,65},{65,1},{2,66},{66,2},{3,67},{67,3},{4,68},{68... | collective-permute-start | bytes 1597448 | tf_op jit(solution)/shard_map/ppermute | solution.py:288
  104.9 14.5 %all-to-all-start.1 = ((bf16[8,128,128]{2,1,0:T(8,128)(2,1)}), bf16[8,128,128]{2,1,0:T(8,128)(2,1)S(1)}, u32[]{:S(2)}, u32[]{:S(2)}) async-start(bf16[8,128,128]{2,1,0:T(8,128)(2,1)} %get-tuple-element.32), calls=%async_computation.1 | async-start | bytes 524288 | tf_op jit(solution)/shard_map/all_to_all | solution.py:294
  117.1 35.2 %copy-start.1 = (s32[1,512]{1,0:T(1,128)S(1)}, s32[1,512]{1,0:T(1,128)}, u32[]{:S(2)}) copy-start(s32[1,512]{1,0:T(1,128)} %get-tuple-element.34) | copy-start | bytes 6148
  131.0 19.8 %all-to-all-start.3 = ((f32[64,1,10]{2,1,0:T(1,128)}), f32[64,1,10]{2,1,0:T(1,128)S(1)}, u32[]{:S(2)}, u32[]{:S(2)}) async-start(f32[64,1,10]{2,1,0:T(1,128)} %copy.18), calls=%async_computation.3 | async-start | bytes 65536 | tf_op jit(solution)/shard_map/all_to_all | solution.py:294

commit v11 on v10

--- a/solution.py
+++ b/solution.py
@@ -12,6 +12,7 @@
 BF16 = jnp.bfloat16
 LANES = 128
 ROWS = 4
+FULL = 8
 WIDE = 3 * LANES
 NOTES = 32
 LIMIT = 28 * 2**20
@@ -93,7 +94,9 @@
     earlier = dot(hot(is_owner), before, ((1,), (0,)))
     rank = jnp.sum(jnp.where(is_owner, earlier, 0.0), axis=0, keepdims=True)
     place[...] = (first_owner * capacity + rank).astype(jnp.int32)
-    spot = rank * members + first_owner
+    turn_of = whole(rank, ROWS)
+    spot = (turn_of * members + first_owner) * ROWS + rank - ROWS * turn_of
+    spot = jnp.where(rank < FULL, spot, rank * members + first_owner)
     order = hot(rows_of((members * capacity, vectors)) == spot)
     copies[3].wait()
     packed = dot(order, embeddings[...], ((1,), (0,)))
@@ -105,9 +108,13 @@
     empty = [jnp.zeros((members, LANES), F32)] * (ROWS * WIDE // LANES - capacity - 1)
     for j in range(embeddings.shape[1] // LANES):
         at = slice(j * LANES, (j + 1) * LANES)
-        rows = [packed[p * members : (p + 1) * members, at] for p in range(capacity)]
+        rows = [packed[p * members : (p + 1) * members, at] for p in range(FULL, capacity)]
         rows += [labels] + empty
-        block = [jnp.stack(rows[t : t + ROWS], axis=1) for t in range(0, len(rows), ROWS)]
+        block = [
+            packed[p * members : (p + ROWS) * members, at].reshape(members, ROWS, LANES)
+            for p in range(0, FULL, ROWS)
+        ]
+        block.append(jnp.stack(rows, axis=1))
         payload[j * members : (j + 1) * members] = jnp.concatenate(block, axis=2).astype(BF16)
 
 
@@ -117,9 +124,16 @@
     count = members * capacity
     slots = rows - NOTES
     vector = lanes_of((members, slots))
-    from_member = vector - members * whole(vector, members)
-    from_member = hot(rows_of((members, slots)) == from_member)
-    ranked = rows_of((16, slots)) == whole(lanes_of((16, slots)), members)
+    quarter = whole(vector, ROWS)
+    quarter = jnp.where(vector < FULL * members, quarter, vector)
+    from_member = hot(
+        rows_of((members, slots)) == quarter - members * whole(quarter, members)
+    )
+    vector = lanes_of((16, slots))
+    quarter = whole(vector, ROWS)
+    rank = ROWS * whole(quarter, members) + vector - ROWS * quarter
+    rank = jnp.where(vector < FULL * members, rank, whole(vector, members))
+    ranked = rows_of((16, slots)) == rank
     for s in range(chips):
         values = arrived[s * members : (s + 1) * members].astype(F32)
 
@@ -127,7 +141,10 @@
             start = p // ROWS * LANES
             return values[:, p % ROWS, start : start + LANES].astype(BF16)
 
-        for p in range(capacity):
+        for t in range(FULL // ROWS):
+            full = values[:, :, t * LANES : (t + 1) * LANES].reshape(ROWS * members, LANES)
+            out[s, t * ROWS * members : (t + 1) * ROWS * members] = full.astype(BF16)
+        for p in range(FULL, capacity):
             out[s, p * members : (p + 1) * members] = row(p)
         if slots > count:
             out[s, count:slots] = jnp.zeros((slots - count, LANES), BF16)
@@ -229,14 +246,26 @@
 
     counts = counts_of(mine) + counts_of(theirs) + 1.0
     identity = rows_of((LANES, LANES)) == lanes_of((LANES, LANES))
-    lane = lanes_of((LANES, LANES))
     values = []
     for g in range(groups):
         at = slice(g * LANES, (g + 1) * LANES)
         divisor = jnp.sum(jnp.where(identity, counts[g : g + 1], 0.0), axis=1, keepdims=True)
         total = mine[at].astype(F32) + theirs[at].astype(F32)
-        value = (total / divisor).astype(BF16).astype(F32)
+        value = (total / divisor).astype(BF16)
         values.append(value)
+        lists_of[at] = value
+    for s in range(groups // 2):
+        one, two = values[2 * s].astype(F32), values[2 * s + 1].astype(F32)
+        parts[s] = jnp.where(where[1] == 0, one, two).astype(BF16)
+
+
+def score(groups, columns, fresh, margins, lists_of):
+    chips, rows, _ = columns.shape
+    slots = rows - NOTES
+    lane = lanes_of((LANES, LANES))
+    for g in range(groups):
+        at = slice(g * LANES, (g + 1) * LANES)
+        value = fresh[at].astype(F32)
         size = jnp.sum(value * value, axis=1, keepdims=True)
         one = size.astype(BF16).astype(F32)
         two = (size - one).astype(BF16).astype(F32)
@@ -244,13 +273,6 @@
         sizes = jnp.where(lane == 0.0, one, jnp.where(lane == 1.0, two, 0.0))
         sizes = jnp.where(lane == 2.0, three, sizes)
         lists_of[at] = jnp.concatenate([-2.0 * value, sizes], axis=1).astype(BF16)
-    for s in range(groups // 2):
-        parts[s] = jnp.where(where[1] == 0, values[2 * s], values[2 * s + 1]).astype(BF16)
-
-
-def score(groups, columns, lists_of, margins):
-    chips, rows, _ = columns.shape
-    slots = rows - NOTES
 
     def step(t, _):
         vectors, labels = pair_of(columns, slots, t)
@@ -353,7 +375,7 @@
     parts, lists_of = call(
         functools.partial(refit, groups),
         "refit",
-        (shape(chips, lists, LANES), shape(groups * LANES, 2 * LANES)),
+        (shape(chips, lists, LANES), shape(groups * LANES, LANES)),
         2**24,
         mine,
         across(mine),
@@ -367,12 +389,15 @@
         2**33,
         columns,
         lists_of,
+        scratch=[pltpu.VMEM((groups * LANES, 2 * LANES), BF16)],
     )
     scores, returned_parts = lax.optimization_barrier((scores, returned_parts))
     fresh = returned_parts.swapaxes(0, 1).reshape(lists, width)
     scores = exchange("x", scores.reshape(chips, 1, slots))
     margin = jnp.sum(scores.reshape(chips, slots), axis=0) * (1.0 / width)
-    margin = margin[:count].reshape(capacity, members).T
+    full = margin[: FULL * members].reshape(FULL // ROWS, members, ROWS)
+    rest = margin[FULL * members : count].reshape(capacity - FULL, members)
+    margin = jnp.concatenate([full.swapaxes(0, 1).reshape(members, FULL), rest.T], axis=1)
     returned = exchange("mem", margin.reshape(members, 1, capacity))
     spots = jnp.arange(count, dtype=jnp.int32)
     margins = jnp.sum(

time: 155 us -> 152 us (0.981)
  Pallas kernels: 28.9 us -> 25.4 us
    pallas_call x6, Pallas kernels: 28.9 us -> 25.4 us  [call(): pl.pallas_call(kernel, in_specs=specs, out_shape=out_shape, scratch_shape...]
  transfers between devices with their start and end apart: 9 -> 9, of which waited for: 7 -> 7; matrix products, arithmetic and copies ran while one was open for 1% -> 1% of each run, Pallas kernels for 6% -> 7%
where the time goes in v11:
time: 152 us; the launch traced here: 150 us
  starting transfers between devices  75 us (49%)
  waiting for transfers between devices  33 us (22%)
  Pallas kernels  25.4 us (17%)
  blocking collectives  11.2 us (7%)
  local copies, waits for them, and re-layouts  2.76 us (2%)
  other arithmetic  1.75 us (1%)
    all_to_all x3, starting transfers between devices, exchange(): return lax.all_to_all(a, axis, split_axis=0, concat_axis=0, tiled=True)  49.7 us
    pallas_call x6, Pallas kernels, call(): pl.pallas_call(kernel, in_specs=specs, out_shape=out_shape, scratch_shape...  25.4 us
    all_to_all x3, waiting for transfers between devices, exchange(): return lax.all_to_all(a, axis, split_axis=0, concat_axis=0, tiled=True)  16.7 us
    ppermute x1, waiting for transfers between devices, on_device(): lax.ppermute(far, 'x', [(i, (i + steps) % chips) for i in range(chips)])  13.1 us
    all_to_all x1, blocking collectives, exchange(): return lax.all_to_all(a, axis, split_axis=0, concat_axis=0, tiled=True)  11.2 us
    ppermute x3, starting transfers between devices, on_device(): olds.append(lax.ppermute(along[k - 1], ('x', 'core'), pairs))  9.79 us
    ppermute x2, starting transfers between devices, across(): return lax.ppermute(a, 'core', [(0, 1), (1, 0)])  8.94 us
    ppermute x1, starting transfers between devices, on_device(): lax.ppermute(far, 'x', [(i, (i + steps) % chips) for i in range(chips)])  6.53 us
  transfers between devices with their start and end apart: 9, of which 7 were waited for; matrix products, arithmetic and copies ran while one was open for 1% of the time, Pallas kernels for 7%

profile of v11, /device:TPU:1, one launch (start us, length us, event | category | flops | bytes accessed | tf_op | source)
XLA Modules:
  0.0 149.9 jit_solution(14953791994770800756)
XLA Ops:
  0.6 5.6 %prepare.1 = (bf16[512,4,384]{2,1,0:T(4,128)(2,1)}, s32[1,512]{1,0:T(1,128)}) custom-call(s32[1,512]{1,0:T(1,128)} %bitcast.22, s32[1,512]{1,0:T(1,128)} %bitcast.23, s32[1024,128]{1,0:T(8,128)} %bitcast.21, bf16[512,1024]{1,0:T(8,128)(2,1)} %refs_3_.1), custom_call_target="tpu_custom_call" | custom-call | flops 2147483648 | bytes 2097152 | tf_op jit(solution)/shard_map/prepare/pallas_call | solution.py:48
  6.3 37.3 %all-to-all-start = ((bf16[512,4,384]{2,1,0:T(4,128)(2,1)}), bf16[512,4,384]{2,1,0:T(4,128)(2,1)S(1)}, u32[]{:S(2)}, u32[]{:S(2)}) async-start(bf16[512,4,384]{2,1,0:T(4,128)(2,1)} %get-tuple-element.19), calls=%async_computation | async-start | bytes 3145728 | tf_op jit(solution)/shard_map/all_to_all | solution.py:316
  43.6 2.9 %collective-permute-start = (bf16[128,1024]{1,0:T(8,128)(2,1)S(1)}, bf16[128,1024]{1,0:T(8,128)(2,1)S(1)}, u32[]{:S(2)}, u32[]{:S(2)}) collective-permute-start(bf16[128,1024]{1,0:T(8,128)(2,1)S(1)} %copy-done), channel_id=1, source_target_pairs={{0,64},{64,0},{1,65},{65,1},{2,66},{66,2},{3,67},{67,3},{4,68},{68... | collective-permute-start | bytes 786440 | tf_op jit(solution)/shard_map/ppermute | solution.py:310
  46.6 1.1 collective-permute-done.other
  48.3 4.3 %collective-permute-start.2 = (bf16[256,128]{1,0:T(8,128)(2,1)S(1)}, bf16[256,128]{1,0:T(8,128)(2,1)S(1)}, u32[]{:S(2)}, u32[]{:S(2)}) collective-permute-start(bf16[256,128]{1,0:T(8,128)(2,1)S(1)} %get-tuple-element.22), channel_id=1, source_target_pairs={{0,128},{128,256},{256,384},{384,512},{512,640},{640,768},{768,896... | collective-permute-start | bytes 196616 | tf_op jit(solution)/shard_map/ppermute | solution.py:356
  52.6 3.1 %collective-permute-start.3 = (bf16[256,128]{1,0:T(8,128)(2,1)S(1)}, bf16[256,128]{1,0:T(8,128)(2,1)S(1)}, u32[]{:S(2)}, u32[]{:S(2)}) collective-permute-start(bf16[256,128]{1,0:T(8,128)(2,1)S(1)} %get-tuple-element.23), channel_id=1, source_target_pairs={{0,256},{128,384},{256,512},{384,640},{512,768},{640,896},{768,0},... | collective-permute-start | bytes 196616 | tf_op jit(solution)/shard_map/ppermute | solution.py:356
  55.7 2.4 %collective-permute-start.4 = (bf16[256,128]{1,0:T(8,128)(2,1)S(1)}, bf16[256,128]{1,0:T(8,128)(2,1)S(1)}, u32[]{:S(2)}, u32[]{:S(2)}) collective-permute-start(bf16[256,128]{1,0:T(8,128)(2,1)S(1)} %get-tuple-element.24), channel_id=1, source_target_pairs={{0,384},{128,512},{256,640},{384,768},{512,896},{640,0},{768,128},... | collective-permute-start | bytes 196616 | tf_op jit(solution)/shard_map/ppermute | solution.py:356
  58.1 6.5 %collective-permute-start.1 = (bf16[128,128]{1,0:T(8,128)(2,1)S(1)}, bf16[128,128]{1,0:T(8,128)(2,1)S(1)}, u32[]{:S(2)}, u32[]{:S(2)}) collective-permute-start(bf16[128,128]{1,0:T(8,128)(2,1)S(1)} %get-tuple-element.21), channel_id=1, source_target_pairs={{0,512},{128,640},{256,768},{384,896},{512,0},{640,128},{768,256},... | collective-permute-start | bytes 98312 | tf_op jit(solution)/shard_map/ppermute | solution.py:352
  64.6 13.1 %collective-permute-done.1.refs_1_ = bf16[128,128]{1,0:T(8,128)(2,1)S(1)} collective-permute-done((bf16[128,128]{1,0:T(8,128)(2,1)S(1)}, bf16[128,128]{1,0:T(8,128)(2,1)S(1)}, u32[]{:S(2)}, u32[]{:S(2)}) %collective-permute-start.1) | collective-permute-done | bytes 32800 | tf_op jit(solution)/shard_map/ppermute | solution.py:352
  78.3 5.0 %all-to-all-done.arrived = bf16[512,4,384]{2,1,0:T(4,128)(2,1)S(1)} async-done(((bf16[512,4,384]{2,1,0:T(4,128)(2,1)}), bf16[512,4,384]{2,1,0:T(4,128)(2,1)S(1)}, u32[]{:S(2)}, u32[]{:S(2)}) %all-to-all-start) | async-done | bytes 1572896 | tf_op jit(solution)/shard_map/all_to_all | solution.py:316
  83.3 1.3 gather.1.columns
  84.6 7.0 %sums.1.mine = bf16[2080,128]{1,0:T(8,128)(2,1)S(1)} custom-call(s32[2]{0:T(128)S(1)} %pad_add_fusion.where, bf16[8,672,128]{2,1,0:T(8,128)(2,1)S(1)} %gather.1.columns, bf16[128,128]{1,0:T(8,128)(2,1)S(1)} %get-tuple-element.26.refs_0_, bf16[128,128]{1,0:T(8,128)(2,1)S(1)} %collective-permute-done.1.refs_1_, ...), custom_call_target="tpu_custom_call" | custom-call | flops 4294967296 | bytes 2097152 | tf_op jit(solution)/shard_map/sums/pallas_call | solution.py:48
  91.7 6.1 %collective-permute-start.5 = (bf16[2080,128]{1,0:T(8,128)(2,1)S(1)}, bf16[2080,128]{1,0:T(8,128)(2,1)S(1)}, u32[]{:S(2)}, u32[]{:S(2)}) collective-permute-start(bf16[2080,128]{1,0:T(8,128)(2,1)S(1)} %sums.1.mine), channel_id=1, source_target_pairs={{0,64},{64,0},{1,65},{65,1},{2,66},{66,2},{3,67},{67,3},{4,68},{68... | collective-permute-start | bytes 1597448 | tf_op jit(solution)/shard_map/ppermute | solution.py:310
  97.7 1.5 %collective-permute-done.5.theirs = bf16[2080,128]{1,0:T(8,128)(2,1)S(1)} collective-permute-done((bf16[2080,128]{1,0:T(8,128)(2,1)S(1)}, bf16[2080,128]{1,0:T(8,128)(2,1)S(1)}, u32[]{:S(2)}, u32[]{:S(2)}) %collective-permute-start.5) | collective-permute-done | bytes 532512 | tf_op jit(solution)/shard_map/ppermute | solution.py:310
  99.3 1.6 %refit.1 = (bf16[8,128,128]{2,1,0:T(8,128)(2,1)}, bf16[2048,128]{1,0:T(8,128)(2,1)S(1)}) custom-call(s32[2]{0:T(128)S(1)} %pad_add_fusion.where, bf16[2080,128]{1,0:T(8,128)(2,1)S(1)} %sums.1.mine, bf16[2080,128]{1,0:T(8,128)(2,1)S(1)} %collective-permute-done.5.theirs), custom_call_target="tpu_custom_call" | custom-call | flops 16777216 | bytes 2097152 | tf_op jit(solution)/shard_map/refit/pallas_call | solution.py:48
  100.9 3.5 %all-to-all-start.1 = ((bf16[8,128,128]{2,1,0:T(8,128)(2,1)}), bf16[8,128,128]{2,1,0:T(8,128)(2,1)S(1)}, u32[]{:S(2)}, u32[]{:S(2)}) async-start(bf16[8,128,128]{2,1,0:T(8,128)(2,1)} %get-tuple-element.32), calls=%async_computation.1 | async-start | bytes 524288 | tf_op jit(solution)/shard_map/all_to_all | solution.py:316
  104.3 9.2 %score.1 = f32[8,640]{1,0:T(8,128)S(1)} custom-call(bf16[8,672,128]{2,1,0:T(8,128)(2,1)S(1)} %gather.1.columns, bf16[2048,128]{1,0:T(8,128)(2,1)S(1)} %get-tuple-element.31.fresh), custom_call_target="tpu_custom_call" | custom-call | flops 8589934592 | bytes 2097152 | tf_op jit(solution)/shard_map/score/pallas_call | solution.py:48
  113.5 1.9 %all-to-all-done.1 = bf16[8,128,128]{2,1,0:T(8,128)(2,1)S(1)} async-done(((bf16[8,128,128]{2,1,0:T(8,128)(2,1)}), bf16[8,128,128]{2,1,0:T(8,128)(2,1)S(1)}, u32[]{:S(2)}, u32[]{:S(2)}) %all-to-all-start.1) | async-done | bytes 262176 | tf_op jit(solution)/shard_map/all_to_all | solution.py:316
  115.4 11.2 %all_to_all.20 = f32[8,1,640]{2,1,0:T(1,128)S(1)} all-to-all(f32[8,1,640]{2,1,0:T(1,128)S(1)} %copy.18), channel_id=1, replica_groups=mesh['x'=8,'core'=2,'mem'=64] {'x'}, dimensions={0} | all-to-all | bytes 40960 | tf_op jit(solution)/shard_map/all_to_all | solution.py:316
  127.7 8.9 %all-to-all-start.3 = ((f32[64,1,10]{2,1,0:T(1,128)}), f32[64,1,10]{2,1,0:T(1,128)S(1)}, u32[]{:S(2)}, u32[]{:S(2)}) async-start(f32[64,1,10]{2,1,0:T(1,128)} %copy.20), calls=%async_computation.3 | async-start | bytes 65536 | tf_op jit(solution)/shard_map/all_to_all | solution.py:316
  136.8 0.9 copy.21
  137.7 9.8 %all-to-all-done.3 = f32[64,1,10]{2,1,0:T(1,128)S(1)} async-done(((f32[64,1,10]{2,1,0:T(1,128)}), f32[64,1,10]{2,1,0:T(1,128)S(1)}, u32[]{:S(2)}, u32[]{:S(2)}) %all-to-all-start.3) | async-done | bytes 2592 | tf_op jit(solution)/shard_map/all_to_all | solution.py:316
  148.1 0.8 reduce.4
  149.0 0.9 select_reduce_fusion
  (22 shorter events, 3.2 us)
Async XLA Ops:
  6.3 37.4 %copy-start = (bf16[128,1024]{1,0:T(8,128)(2,1)S(1)}, bf16[128,1024]{1,0:T(8,128)(2,1)}, u32[]{:S(2)}) copy-start(bf16[128,1024]{1,0:T(8,128)(2,1)} %old.1) | copy-start | bytes 786436
  6.3 77.0 %all-to-all-start = ((bf16[512,4,384]{2,1,0:T(4,128)(2,1)}), bf16[512,4,384]{2,1,0:T(4,128)(2,1)S(1)}, u32[]{:S(2)}, u32[]{:S(2)}) async-start(bf16[512,4,384]{2,1,0:T(4,128)(2,1)} %get-tuple-element.19), calls=%async_computation | async-start | bytes 3145728 | tf_op jit(solution)/shard_map/all_to_all | solution.py:316
  43.6 4.0 %collective-permute-start = (bf16[128,1024]{1,0:T(8,128)(2,1)S(1)}, bf16[128,1024]{1,0:T(8,128)(2,1)S(1)}, u32[]{:S(2)}, u32[]{:S(2)}) collective-permute-start(bf16[128,1024]{1,0:T(8,128)(2,1)S(1)} %copy-done), channel_id=1, source_target_pairs={{0,64},{64,0},{1,65},{65,1},{2,66},{66,2},{3,67},{67,3},{4,68},{68... | collective-permute-start | bytes 786440 | tf_op jit(solution)/shard_map/ppermute | solution.py:310
  48.3 29.4 %collective-permute-start.2 = (bf16[256,128]{1,0:T(8,128)(2,1)S(1)}, bf16[256,128]{1,0:T(8,128)(2,1)S(1)}, u32[]{:S(2)}, u32[]{:S(2)}) collective-permute-start(bf16[256,128]{1,0:T(8,128)(2,1)S(1)} %get-tuple-element.22), channel_id=1, source_target_pairs={{0,128},{128,256},{256,384},{384,512},{512,640},{640,768},{768,896... | collective-permute-start | bytes 196616 | tf_op jit(solution)/shard_map/ppermute | solution.py:356
  52.6 25.1 %collective-permute-start.3 = (bf16[256,128]{1,0:T(8,128)(2,1)S(1)}, bf16[256,128]{1,0:T(8,128)(2,1)S(1)}, u32[]{:S(2)}, u32[]{:S(2)}) collective-permute-start(bf16[256,128]{1,0:T(8,128)(2,1)S(1)} %get-tuple-element.23), channel_id=1, source_target_pairs={{0,256},{128,384},{256,512},{384,640},{512,768},{640,896},{768,0},... | collective-permute-start | bytes 196616 | tf_op jit(solution)/shard_map/ppermute | solution.py:356
  55.7 22.6 %collective-permute-start.4 = (bf16[256,128]{1,0:T(8,128)(2,1)S(1)}, bf16[256,128]{1,0:T(8,128)(2,1)S(1)}, u32[]{:S(2)}, u32[]{:S(2)}) collective-permute-start(bf16[256,128]{1,0:T(8,128)(2,1)S(1)} %get-tuple-element.24), channel_id=1, source_target_pairs={{0,384},{128,512},{256,640},{384,768},{512,896},{640,0},{768,128},... | collective-permute-start | bytes 196616 | tf_op jit(solution)/shard_map/ppermute | solution.py:356
  58.1 19.6 %collective-permute-start.1 = (bf16[128,128]{1,0:T(8,128)(2,1)S(1)}, bf16[128,128]{1,0:T(8,128)(2,1)S(1)}, u32[]{:S(2)}, u32[]{:S(2)}) collective-permute-start(bf16[128,128]{1,0:T(8,128)(2,1)S(1)} %get-tuple-element.21), channel_id=1, source_target_pairs={{0,512},{128,640},{256,768},{384,896},{512,0},{640,128},{768,256},... | collective-permute-start | bytes 98312 | tf_op jit(solution)/shard_map/ppermute | solution.py:352
  91.7 7.6 %collective-permute-start.5 = (bf16[2080,128]{1,0:T(8,128)(2,1)S(1)}, bf16[2080,128]{1,0:T(8,128)(2,1)S(1)}, u32[]{:S(2)}, u32[]{:S(2)}) collective-permute-start(bf16[2080,128]{1,0:T(8,128)(2,1)S(1)} %sums.1.mine), channel_id=1, source_target_pairs={{0,64},{64,0},{1,65},{65,1},{2,66},{66,2},{3,67},{67,3},{4,68},{68... | collective-permute-start | bytes 1597448 | tf_op jit(solution)/shard_map/ppermute | solution.py:310
  100.9 14.5 %all-to-all-start.1 = ((bf16[8,128,128]{2,1,0:T(8,128)(2,1)}), bf16[8,128,128]{2,1,0:T(8,128)(2,1)S(1)}, u32[]{:S(2)}, u32[]{:S(2)}) async-start(bf16[8,128,128]{2,1,0:T(8,128)(2,1)} %get-tuple-element.32), calls=%async_computation.1 | async-start | bytes 524288 | tf_op jit(solution)/shard_map/all_to_all | solution.py:316
  113.5 35.5 %copy-start.1 = (s32[1,512]{1,0:T(1,128)S(1)}, s32[1,512]{1,0:T(1,128)}, u32[]{:S(2)}) copy-start(s32[1,512]{1,0:T(1,128)} %get-tuple-element.34) | copy-start | bytes 6148
  127.7 19.8 %all-to-all-start.3 = ((f32[64,1,10]{2,1,0:T(1,128)}), f32[64,1,10]{2,1,0:T(1,128)S(1)}, u32[]{:S(2)}, u32[]{:S(2)}) async-start(f32[64,1,10]{2,1,0:T(1,128)} %copy.20), calls=%async_computation.3 | async-start | bytes 65536 | tf_op jit(solution)/shard_map/all_to_all | solution.py:316
